TPU v7x, 32 devices: a whole 2x2x4 slice. The times are simulated.
32 devices in a mesh: pulse: 4 (over y, x), gate: 8 (over z, core).
Axes of the slice: x: 2, y: 2, z: 4, core: 2. Of those that a mesh axis runs over, the one named last changes fastest.
Arguments:
- echoes: bfloat16 [2, 8, 2048, 4096], P(None, None, 'pulse', 'gate'), may hold values from -6 to 6
- replica: bfloat16 [2, 256], replicated, may hold values from -4 to 4
- beam_weights: float32 [2, 2, 8, 2048], P(None, None, None, 'pulse'), may hold values from -1.5 to 1.5
- track_doppler: int32 [8192], P(('pulse', 'gate')), may hold values from 0 to 2047, as said below
- track_gate: int32 [8192], P(('pulse', 'gate')), may hold values from 0 to 4095, as said below
- track_owner: int32 [8192], P(('pulse', 'gate')), may hold values from 0 to 31, as said below
Outputs:
- track_tiles: float32 [20480, 1024], P(('pulse', 'gate'))
Inputs may be any that keep to these rules, and one draw needn't show every extreme that they name: `track_doppler`: row k lies in Doppler block (k // 256) // 8: its bin is in that block of 512 bins. `track_gate`: row k lies in range block (k // 256) % 8: its gate is in that block of 512 gates. `track_owner`: within each aligned block of 256 rows no owner appears more than 20 times, and in every draw some owner appears exactly 20 times in every block.
All inputs are finite; a program needn't handle non-finite values.
Results may differ from a plain program's by a relative error of at most 0.015.
Values may be sent and summed in bfloat16 or wider, within the bound.
No kernel may reach another device: no remote copies, remote signals or barrier semaphores. Data moves between devices by JAX's collectives and lax.ppermute only.
A program may use at most 704 MiB of HBM per device.

v0:
```python
import math

import jax
import jax.numpy as jnp
from jax import lax
from jax.sharding import PartitionSpec as P

TILE = 16


def passed_along(value, axis, steps):
    count = lax.axis_size(axis)
    leading, last = (max(0, -steps), min(count, count - steps))
    return lax.ppermute(value, axis, [(source, source + steps) for source in range(leading, last)])


def extended_2(block, sides, width):
    for axis, dim in sides:
        count = lax.axis_size(axis)
        forward = [(i, i + 1) for i in range(count - 1)]
        backward = [(target, source) for source, target in forward]
        low = lax.ppermute(
            lax.slice_in_dim(block, block.shape[dim] - width, None, axis=dim), axis, forward
        )
        high = lax.ppermute(lax.slice_in_dim(block, 0, width, axis=dim), axis, backward)
        block = jnp.concatenate([low, block, high], axis=dim)
    return block


def compress_range(echoes, replica):
    chirp_len = replica.shape[1]
    gates = echoes.shape[3]
    echo_rim = passed_along(echoes[:, :, :, :chirp_len], "gate", -1)
    extended = jnp.concatenate([echoes, echo_rim], axis=3)
    block_width = min(128, gates)
    window_span = block_width + chirp_len
    gate_lag = lax.broadcasted_iota(
        jnp.int32, (window_span, block_width), 0
    ) - lax.broadcasted_iota(jnp.int32, (window_span, block_width), 1)
    inside = (gate_lag >= 0) & (gate_lag < chirp_len)
    safe_lag = jnp.clip(gate_lag, 0, chirp_len - 1)
    nothing = jnp.zeros((), replica.dtype)
    real_tap = jnp.where(inside, jnp.take(replica[0], safe_lag), nothing)
    imag_tap = jnp.where(inside, jnp.take(replica[1], safe_lag), nothing)
    from_real = jnp.stack([real_tap, -imag_tap], axis=1)
    from_imag = jnp.stack([imag_tap, real_tap], axis=1)
    toeplitz = jnp.stack([from_real, from_imag], axis=0)
    range_scale = 1.0 / math.sqrt(2.0 * chirp_len)
    pieces = []
    for offset in range(0, gates, block_width):
        window = extended[:, :, :, offset : offset + window_span]
        products = jnp.einsum(
            "qcpw,qwso->scpo", window, toeplitz, preferred_element_type=jnp.float32
        )
        pieces.append((products * range_scale).astype(jnp.bfloat16))
    return jnp.concatenate(pieces, axis=3)


def phase_table(rows, cols, period):
    product = (
        lax.broadcasted_iota(jnp.int32, (rows, cols), 0)
        * lax.broadcasted_iota(jnp.int32, (rows, cols), 1)
        % period
    )
    angle = product.astype(jnp.float32) * (2.0 * math.pi / period)
    return (jnp.cos(angle), jnp.sin(angle))


def complex_table(size):
    cos_part, sin_part = phase_table(size, size, size)
    top_row = jnp.stack([cos_part, sin_part])
    low_row = jnp.stack([-sin_part, cos_part])
    return jnp.stack([top_row, low_row]).astype(jnp.bfloat16)


def doppler_transform(turned):
    channels, pulse_count, gates = (turned.shape[1], turned.shape[2], turned.shape[3])
    first = 1 << pulse_count.bit_length() // 2
    second = pulse_count // first
    parts = turned.reshape(2, channels, first, second, gates)
    f32 = jnp.float32
    section = jnp.einsum(
        "oiap,icpbg->ocabg", complex_table(first), parts, preferred_element_type=f32
    )
    section_real = section[0]
    section_imag = section[1]
    cos_twist, sin_twist = phase_table(first, second, pulse_count)
    cos_twist = cos_twist[None, :, :, None]
    sin_twist = sin_twist[None, :, :, None]
    twist_real = (section_real * cos_twist + section_imag * sin_twist).astype(jnp.bfloat16)
    twist_imag = (section_imag * cos_twist - section_real * sin_twist).astype(jnp.bfloat16)
    twisted = jnp.stack([twist_real, twist_imag])
    final = jnp.einsum(
        "oieb,icabg->oceag", complex_table(second), twisted, preferred_element_type=f32
    )
    norm_scale = 1.0 / math.sqrt(pulse_count)
    return (final * norm_scale).reshape(2, channels, pulse_count, gates).astype(jnp.bfloat16)


def local(echoes, replica, beam_weights, track_doppler, track_gate, track_owner):
    compressed = compress_range(echoes, replica)
    turned = lax.all_to_all(compressed, "pulse", split_axis=1, concat_axis=2, tiled=True)
    spectra = doppler_transform(turned)
    spectrum = lax.all_to_all(spectra, "pulse", split_axis=2, concat_axis=1, tiled=True)
    spec_real = spectrum[0].astype(jnp.float32)[None]
    spec_imag = spectrum[1].astype(jnp.float32)[None]
    weight_real = beam_weights[0][:, :, :, None]
    weight_imag = beam_weights[1][:, :, :, None]
    beam_real = jnp.sum(weight_real * spec_real - weight_imag * spec_imag, axis=1)
    beam_imag = jnp.sum(weight_real * spec_imag + weight_imag * spec_real, axis=1)
    beams = jnp.stack([beam_real, beam_imag])
    beam_count = beams.shape[1]
    framed = extended_2(beams.astype(jnp.bfloat16), (("pulse", 2), ("gate", 3)), TILE // 2).astype(
        beams.dtype
    )
    local_bin = track_doppler % beams.shape[2]
    local_gate = track_gate % beams.shape[3]
    zero_index = jnp.zeros((), jnp.int32)

    def cut_tile(doppler_bin, range_gate):
        starts = (zero_index, zero_index, doppler_bin, range_gate)
        return lax.dynamic_slice(framed, starts, (2, beam_count, TILE, TILE)).reshape(-1)

    tile_rows = jax.vmap(cut_tile)(local_bin, local_gate)
    pulse_devices = lax.axis_size("pulse")
    gate_devices = lax.axis_size("gate")
    owner_total = pulse_devices * gate_devices
    track_count = track_owner.shape[0]
    capacity = max(2, 5 * track_count // (2 * owner_total))
    owner_match = (
        track_owner[:, None] == jnp.arange(owner_total, dtype=jnp.int32)[None, :]
    ).astype(jnp.int32)
    running = jnp.cumsum(owner_match, axis=0, dtype=jnp.int32)
    slot_rank = jnp.sum(running * owner_match, axis=1, dtype=jnp.int32) - 1
    slot_index = track_owner * capacity + slot_rank
    features = tile_rows.shape[1]
    outgoing = (
        jnp.zeros((owner_total * capacity, features), jnp.float32).at[slot_index].set(tile_rows)
    )
    received = lax.all_to_all(
        outgoing.astype(jnp.bfloat16), ("pulse", "gate"), split_axis=0, concat_axis=0, tiled=True
    ).astype(outgoing.dtype)
    return received


def solution(mesh):
    return jax.shard_map(
        local,
        mesh=mesh,
        in_specs=(
            P(None, None, "pulse", "gate"),
            P(),
            P(None, None, None, "pulse"),
            P(("pulse", "gate")),
            P(("pulse", "gate")),
            P(("pulse", "gate")),
        ),
        out_specs=P(("pulse", "gate"), None),
        check_vma=False,
    )
```

profile of v0, /device:TPU:0, one launch (start us, length us, event | category | flops | bytes accessed | tf_op | source)
XLA Modules:
  0.0 1372.5 jit_solution(2042380830359560391)
XLA Ops:
  0.0 7.5 fusion.70
  7.5 3.2 copy-done.1
  10.7 2.3 slice.91
  13.0 1.3 collective-permute-start
  14.5 287.1 %gather_fusion.1 = bf16[49152]{0:T(1024)(128)(2,1)S(1)} fusion(bf16[256]{0:T(256)(128)(2,1)S(1)} %get-tuple-element.9, s32[49152]{0:T(1024)S(1)} %bitcast_clamp_fusion), kind=kCustom, calls=%fused_computation.clone | custom fusion | bytes 393216 | tf_op jit(solution)/shard_map/jit(_take)/gather | solution.py:43
  301.8 287.1 %gather_fusion.2 = bf16[49152]{0:T(1024)(128)(2,1)S(1)} fusion(bf16[256]{0:T(256)(128)(2,1)S(1)} %get-tuple-element.8, s32[49152]{0:T(1024)S(1)} %bitcast_clamp_fusion), kind=kCustom, calls=%fused_computation.1.clone | custom fusion | bytes 393216 | tf_op jit(solution)/shard_map/jit(_take)/gather | solution.py:44
  589.2 4.8 fusion.19
  594.1 4.8 fusion.20
  598.9 2.5 constant_dynamic-update-slice_fusion
  601.4 1.8 fusion.21
  603.3 1.8 fusion.22
  605.1 3.6 pad_maximum_fusion
  608.7 7.4 copy.112
  616.1 6.2 all-to-all-start
  622.8 93.7 %all-to-all-done = bf16[2,8,512,512]{2,3,0,1:T(8,128)(2,1)} async-done(((bf16[2,8,512,512]{2,3,0,1:T(8,128)(2,1)}), bf16[2,8,512,512]{2,3,0,1:T(8,128)(2,1)}, u32[]{:S(2)}, u32[]{:S(2)}) %all-to-all-start) | async-done | bytes 8388640 | tf_op jit(solution)/shard_map/all_to_all | solution.py:102
  716.5 13.2 copy.114
  729.8 10.2 fusion.6
  740.0 3.5 add_convert_fusion
  743.5 6.2 maximum_bitcast_fusion
  749.7 17.7 %fusion.1 = bf16[2,2,32,64,512]{4,2,0,3,1:T(8,128)(2,1)} fusion(bf16[2,2,64,32,512,1]{4,2,0,3,1,5:T(8,128)(2,1)} %maximum_bitcast_fusion, bf16[1,2,32,32]{3,2,1,0:T(8,128)(2,1)S(1)} %get-tuple-element.29, bf16[1,2,32,32]{3,2,1,0:T(8,128)(2,1)S(1)} %get-tuple-element.28), kind=kOutput, calls=%fused_computation.8 | convolution fusion | flops 545275904 | bytes 16785408 | tf_op jit(solution)/shard_map/oieb,icabg->oceag/dot_general | solution.py:93
  767.4 11.4 copy.117
  778.8 16.4 %copy.118 = bf16[2,2,2048,512]{3,1,0,2:T(2,128)(2,1)} copy(bf16[2,2,2048,512]{3,2,1,0:T(8,128)(2,1)} %bitcast.166) | data formatting | bytes 16777216 | tf_op jit(solution)/shard_map/convert_element_type | solution.py:97
  795.3 6.0 all-to-all-start.1
  801.3 0.6 reduce-window.6
  802.3 92.0 %all-to-all-done.1 = bf16[2,2,2048,512]{3,1,0,2:T(2,128)(2,1)} async-done(((bf16[2,2,2048,512]{3,1,0,2:T(2,128)(2,1)}), bf16[2,2,2048,512]{3,1,0,2:T(2,128)(2,1)}, u32[]{:S(2)}, u32[]{:S(2)}) %all-to-all-start.1) | async-done | bytes 8388640 | tf_op jit(solution)/shard_map/all_to_all | solution.py:104
  894.3 8.3 copy.119
  902.6 11.5 slice_convert_fusion.1
  914.1 4.6 copy.120
  918.7 1.1 copy-done
  919.8 4.3 copy.121
  924.1 7.3 subtract_reduce_fusion
  931.4 3.4 collective-permute-start.1
  934.8 1.3 collective-permute-start.2
  936.3 4.2 collective-permute-done.2
  941.0 1.3 collective-permute-start.3
  942.6 1.3 collective-permute-start.4
  943.9 0.3 copy.124
  944.2 3.9 collective-permute-done.4
  948.3 4.5 maximum_convert_fusion
  952.9 231.4 %copy.126 = f32[2,2,528,528]{1,0,3,2:T(2,128)} copy(f32[2,2,528,528]{3,2,1,0:T(8,128)} %maximum_convert_fusion) | data formatting | bytes 8921088 | tf_op jit(solution)/shard_map/convert_element_type | solution.py:113
  1184.3 77.2 %gather_fusion = f32[256,2,2,16,16]{2,1,4,3,0:T(2,128)} fusion(f32[2,2,528,528]{1,0,3,2:T(2,128)} %copy.126, s32[256]{0:T(256)S(1)} %fusion.65), kind=kCustom, calls=%fused_computation.2 | custom fusion | bytes 2101248 | tf_op jit(solution)/shard_map/vmap()/gather | solution.py:122
  1261.5 55.3 %copy.127 = f32[256,2,2,16,16]{0,4,3,2,1:T(8,128)S(1)} copy(f32[256,2,2,16,16]{2,1,4,3,0:T(2,128)} %gather_fusion) | data formatting | bytes 2097152 | tf_op jit(solution)/shard_map/vmap()/gather | solution.py:122
  1316.8 1.3 copy.128
  1318.1 2.7 scatter_custom_fusion
  1320.8 1.3 convert_element_type.167
  1322.1 2.2 all_to_all.34
  1324.3 46.3 %all_to_all.39 = bf16[32,20,1024]{2,1,0:T(8,128)(2,1)S(1)} all-to-all(bf16[32,20,1024]{2,1,0:T(8,128)(2,1)S(1)} %all_to_all.34), channel_id=1, replica_groups=mesh['pulse'=4,'gate'=8] {'pulse','gate'}, dimensions={0} | all-to-all | bytes 2621440 | tf_op jit(solution)/shard_map/all_to_all | solution.py:140
  1370.6 1.6 reshape.211
  (50 shorter events, 2.8 us)
Async XLA Ops:
  7.5 3.2 copy-start.1
  7.5 7.0 copy-start.4
  13.0 585.9 %collective-permute-start = (bf16[2,8,512,256]{3,2,0,1:T(8,128)(2,1)}, bf16[2,8,512,256]{3,2,0,1:T(8,128)(2,1)}, u32[]{:S(2)}, u32[]{:S(2)}) collective-permute-start(bf16[2,8,512,256]{3,2,0,1:T(8,128)(2,1)} %slice.91), channel_id=1, source_target_pairs={{1,0},{2,1},{3,2},{4,3},{5,4},{6,5},{7,6},{9,8},{10,9},{11,10},{12... | collective-permute-start | bytes 12582920 | tf_op jit(solution)/shard_map/ppermute | solution.py:14
  589.2 9.7 slice-start
  589.2 9.7 slice-start.1
  594.0 4.9 slice-start.2
  616.1 100.5 %all-to-all-start = ((bf16[2,8,512,512]{2,3,0,1:T(8,128)(2,1)}), bf16[2,8,512,512]{2,3,0,1:T(8,128)(2,1)}, u32[]{:S(2)}, u32[]{:S(2)}) async-start(bf16[2,8,512,512]{2,3,0,1:T(8,128)(2,1)} %copy.112), calls=%async_computation | async-start | bytes 16777216 | tf_op jit(solution)/shard_map/all_to_all | solution.py:102
  795.3 6.0 copy-start.3
  795.3 7.0 copy-start.2
  795.3 99.0 %all-to-all-start.1 = ((bf16[2,2,2048,512]{3,1,0,2:T(2,128)(2,1)}), bf16[2,2,2048,512]{3,1,0,2:T(2,128)(2,1)}, u32[]{:S(2)}, u32[]{:S(2)}) async-start(bf16[2,2,2048,512]{3,1,0,2:T(2,128)(2,1)} %copy.118), calls=%async_computation.1 | async-start | bytes 16777216 | tf_op jit(solution)/shard_map/all_to_all | solution.py:104
  914.1 5.8 copy-start
  924.1 19.8 %copy-start.5 = (s32[256]{0:T(256)S(1)}, s32[256]{0:T(256)}, u32[]{:S(2)}) copy-start(s32[256]{0:T(256)} %param.11) | copy-start | bytes 3076
  924.1 19.8 %copy-start.6 = (s32[256]{0:T(256)S(1)}, s32[256]{0:T(256)}, u32[]{:S(2)}) copy-start(s32[256]{0:T(256)} %param.12) | copy-start | bytes 3076
  931.4 4.9 collective-permute-start.1
  934.8 5.8 collective-permute-start.2
  941.0 2.9 collective-permute-start.3
  942.6 5.5 collective-permute-start.4
where the time goes:
time: 1400 us; the launch traced here: 1370 us
  local copies, waits for them, and re-layouts  1030 us (74%)
  waiting for transfers between devices  194 us (14%)
  blocking collectives  46.3 us (3%)
  matrix products  41.1 us (3%)
  other arithmetic  39.7 us (3%)
  starting transfers between devices  20.7 us (1%)
    gather x2, local copies, waits for them, and re-layouts, compress_range(): real_tap = jnp.where(inside, jnp.take(replica[0], safe_lag), nothing)  287 us
    gather x2, local copies, waits for them, and re-layouts, compress_range(): imag_tap = jnp.where(inside, jnp.take(replica[1], safe_lag), nothing)  287 us
    convert_element_type x1, local copies, waits for them, and re-layouts, local(): extended_2(beams.astype(jnp.bfloat16), (('pulse', 2), ('gate', 3)), TILE...  231 us
    gather x2, local copies, waits for them, and re-layouts, cut_tile(): lax.dynamic_slice(framed, starts, (2, beam_count, TILE, TILE)).reshape(-1)  132 us
    all_to_all x1, waiting for transfers between devices, local(): lax.all_to_all(compressed, 'pulse', split_axis=1, concat_axis=2, tiled=True)  93.7 us
    all_to_all x1, waiting for transfers between devices, local(): lax.all_to_all(spectra, 'pulse', split_axis=2, concat_axis=1, tiled=True)  92 us
    all_to_all x1, blocking collectives, local(): lax.all_to_all(outgoing.astype(jnp.bfloat16), ('pulse', 'gate'), split_ax...  46.3 us
  transfers between devices with their start and end apart: 7, of which 5 were waited for; matrix products, arithmetic and copies ran while one was open for 43% of the time, Pallas kernels for 0%

commit v1 on v0

v1 whole, which is shorter than its diff:
```python
import functools
import math

import jax
import jax.numpy as jnp
import ml_dtypes
import numpy as np
from jax import lax
from jax.experimental import pallas as pl
from jax.experimental.pallas import tpu as pltpu
from jax.sharding import PartitionSpec as P

TILE = 16
HALF = TILE // 2
LANES = 128
F32 = jnp.float32
BF16 = jnp.bfloat16
VMEM_LIMIT = 63 * 2**20
SMALL_COST = pl.CostEstimate(flops=2**20, bytes_accessed=2**16, transcendentals=0)


def passed_along(value, axis, steps):
    count = lax.axis_size(axis)
    leading, last = (max(0, -steps), min(count, count - steps))
    return lax.ppermute(value, axis, [(source, source + steps) for source in range(leading, last)])


def pulse_table(bins, depth):
    angle = 2.0 * np.pi * (np.outer(np.arange(bins), np.arange(depth)) % bins) / bins
    cos_part, sin_part = np.cos(angle), np.sin(angle)
    table = np.stack(
        [np.concatenate([cos_part, sin_part], 1), np.concatenate([-sin_part, cos_part], 1)]
    )
    table = table.reshape(2, bins // 8, 8, 2 * depth).transpose(1, 0, 2, 3)
    return table.reshape(2 * bins, 2 * depth).astype(ml_dtypes.bfloat16)


def weights_body(ranks, me_ref, *rest):
    parts, rest = rest[:ranks], rest[ranks:]
    cos_ref, sin_ref, select_ref, spread_ref, out_ref, line_ref = rest[:4] + rest[-2:]
    bins = parts[0].shape[1]
    span = out_ref.shape[0] * 8
    lanes = cos_ref.shape[1]
    me = me_ref[0]
    step = pl.program_id(0)

    @pl.when(step == 0)
    def _():
        line_ref[:HALF, :] = jnp.zeros((HALF, line_ref.shape[1]), F32)
        line_ref[HALF + ranks * bins :, :] = jnp.zeros((HALF, line_ref.shape[1]), F32)
        for slot in range(ranks):
            first = pl.multiple_of((slot ^ me) * bins + HALF, 8)
            line_ref[pl.ds(first, bins), :] = parts[slot][...].T

    base_cos, base_sin = cos_ref[...], sin_ref[...]
    lane_id = lax.broadcasted_iota(jnp.int32, (span, lanes), 1)
    phase = lane_id // 2 % ranks
    first_part = lane_id % 2 == 0
    offset = lax.broadcasted_iota(jnp.int32, (span, lanes), 0) + step * span + (ranks * 8 - HALF)
    lines = []
    for slot in range(ranks):
        block = slot ^ me
        rows = line_ref[pl.ds(pl.multiple_of(block * bins + step * span, 8), span), :]
        high = rows.astype(BF16)
        low = (rows - high.astype(F32)).astype(BF16)
        wide = jnp.dot(high, select_ref[...], preferred_element_type=F32) + jnp.dot(
            low, select_ref[...], preferred_element_type=F32
        )
        turn = (me * offset + block * phase) & (ranks - 1)
        turn_cos = jnp.ones(turn.shape, F32)
        turn_sin = jnp.zeros(turn.shape, F32)
        for value in range(1, ranks):
            angle = 2 * math.pi * value / ranks
            turn_cos = jnp.where(turn == value, round(math.cos(angle), 12), turn_cos)
            turn_sin = jnp.where(turn == value, round(math.sin(angle), 12), turn_sin)
        cos_part = turn_cos * base_cos - turn_sin * base_sin
        sin_part = turn_sin * base_cos + turn_cos * base_sin
        own = jnp.where(first_part, cos_part, sin_part)
        other = jnp.where(first_part, sin_part, -cos_part)
        real, imag = wide[:, :lanes], wide[:, lanes:]
        out_real = (real * own + imag * other).reshape(span // 8, 8, lanes)
        out_imag = (imag * own - real * other).reshape(span // 8, 8, lanes)
        both = jnp.concatenate([out_real, out_imag], axis=1).reshape(span * 2, lanes)
        lines.append(both.astype(BF16))
    product = jnp.dot(
        jnp.concatenate(lines, axis=0), spread_ref[...], preferred_element_type=F32
    )
    row_id = lax.broadcasted_iota(jnp.int32, product.shape, 0) % 8
    diagonal = row_id == lax.broadcasted_iota(jnp.int32, product.shape, 1) % 8
    product = jnp.where(diagonal, product, 0.0).astype(BF16)
    product = product.reshape(ranks, span // 8, 16, product.shape[1])
    depth = out_ref.shape[3]
    for beam in range(product.shape[3] // depth):
        for slot in range(ranks):
            out_ref[:, beam * ranks + slot] = product[
                slot, :, :, beam * depth : (beam + 1) * depth
            ]


def divisor_up_to(value, limit):
    return max(step for step in range(1, limit + 1) if value % step == 0)


def combining_weights(beam_weights, pulse_len, extra, before):
    _, beams, channels, bins = beam_weights.shape
    ranks = lax.axis_size("pulse")
    me = lax.axis_index("pulse")
    total = bins * ranks
    rows = bins + TILE
    count = 2 * beams * channels
    flat = jnp.concatenate([beam_weights.reshape(count, bins), extra])
    parts = [flat] + [
        lax.ppermute(flat, "pulse", [(rank, rank ^ slot) for rank in range(ranks)])
        for slot in range(1, ranks)
    ]
    small = channels * ranks * 2
    column = np.arange(small)
    phase = column // 2 % ranks
    angle = 2.0 * np.pi * (np.outer(np.arange(rows) - HALF, phase) % total) / total
    scale = 1.0 / math.sqrt(total * 2.0 * pulse_len)
    base_cos = np.tile(np.cos(angle) * scale, (1, beams)).astype(np.float32)
    base_sin = np.tile(np.sin(angle) * scale, (1, beams)).astype(np.float32)
    lanes = beams * small
    source = np.arange(count)[:, None]
    target = np.arange(2 * lanes)[None, :]
    wanted = target // small * channels + target % small // (2 * ranks)
    select = (source == wanted).astype(ml_dtypes.bfloat16)
    spread = (np.arange(lanes * 8)[None, :] // 8 == np.arange(lanes)[:, None]).astype(
        ml_dtypes.bfloat16
    )
    groups = rows // 8
    per = divisor_up_to(groups, 11)
    scalar = pl.BlockSpec(memory_space=pltpu.SMEM)
    table = pl.pallas_call(
        functools.partial(weights_body, ranks),
        grid=(groups // per,),
        out_shape=jax.ShapeDtypeStruct((groups, beams * ranks, 16, small * 8), BF16),
        in_specs=[scalar]
        + [pl.BlockSpec((count, bins), lambda i: (0, 0))] * ranks
        + [
            pl.BlockSpec((per * 8, lanes), lambda i: (i, 0)),
            pl.BlockSpec((per * 8, lanes), lambda i: (i, 0)),
            pl.BlockSpec(select.shape, lambda i: (0, 0)),
            pl.BlockSpec(spread.shape, lambda i: (0, 0)),
        ]
        + [pl.BlockSpec(memory_space=pl.ANY)] * len(before),
        out_specs=pl.BlockSpec((per, beams * ranks, 16, small * 8), lambda i: (i, 0, 0, 0)),
        scratch_shapes=[pltpu.VMEM((total + TILE, count), F32)],
        compiler_params=pltpu.CompilerParams(vmem_limit_bytes=VMEM_LIMIT),
        cost_estimate=SMALL_COST,
        name="combining_weights",
    )(me.reshape(1), *parts, base_cos, base_sin, select, spread, *before)
    return table, [part[count:] for part in parts]


def slot_kinds(ranks):
    whole_slots = [slot for slot in range(ranks) if slot & (slot - 1) == 0]
    return whole_slots, [slot for slot in range(ranks) if slot not in whole_slots]


def partial_beams_body(ranks, beams, edges, echo_ref, table_ref, weight_hbm, *rest):
    outs, (wide_ref, taken_ref, stage_ref, weight_ref, weight_sem) = rest[:-5], rest[-5:]
    whole_slots, cut_slots = slot_kinds(ranks)
    count = len(whole_slots)
    outs = outs[-(count + 2 + len(edges)) :]
    far_ref, edge_refs, flag_ref = outs[count], outs[count + 1 : -1], outs[-1]
    flag_ref[...] = jnp.ones(flag_ref.shape, F32)
    _, channels, pulses, width = echo_ref.shape
    depth = pulses // ranks
    groups = table_ref.shape[0] // 16
    columns = width // LANES
    fetch = pltpu.make_async_copy(weight_hbm, weight_ref, weight_sem)
    fetch.start()

    def deinterleave(channel, side):
        for part in range(2):
            wide = echo_ref[part, channel].astype(F32)
            for column in range(columns):
                wide_ref[side, part, column] = wide[:, column * LANES : (column + 1) * LANES]
        for phase in range(ranks):
            here = pl.ds(phase, depth, stride=ranks)
            for part in range(2):
                for column in range(columns):
                    taken_ref[
                        side,
                        phase,
                        part * depth : (part + 1) * depth,
                        column * LANES : (column + 1) * LANES,
                    ] = wide_ref[side, part, column, here, :].astype(BF16)

    def transform(channel, side):
        for phase in range(ranks):
            product = jnp.dot(
                table_ref[...], taken_ref[side, phase], preferred_element_type=F32
            )
            stage_ref[:, channel * ranks + phase] = product.astype(BF16).reshape(groups, 16, width)

    deinterleave(0, 0)

    def two_channels(step, carry):
        first = step * 2
        deinterleave(first + 1, 1)
        transform(first, 0)
        deinterleave(lax.min(first + 2, channels - 1), 0)
        transform(first + 1, 1)
        return carry

    lax.fori_loop(0, channels // 2, two_channels, 0)
    fetch.wait()

    _, pairs, _, inner = weight_ref.shape
    lines = pairs * 2
    steps = weight_ref.shape[0] // 2
    per = divisor_up_to(steps, 4)

    def combine(turn, carry):
        for within in range(per):
            step = turn * per + within
            halves = []
            for half in range(2):
                group = step * 2 + half
                source = lax.rem(group + groups - 1, groups)
                data = stage_ref[source].reshape(inner, width)
                weight = weight_ref[group].reshape(lines * 8, inner)
                product = jnp.dot(weight, data, preferred_element_type=F32)
                halves.append(product.reshape(lines, 8, width))
            both = jnp.concatenate(halves, axis=1).astype(BF16)
            here = pl.ds(pl.multiple_of(step * 16, 16), 16)
            for line in range(lines):
                beam, slot, part = line // (2 * ranks), line // 2 % ranks, line % 2
                value = both[line]
                for tile in range(columns):
                    piece = value[:, tile * LANES : (tile + 1) * LANES]
                    lanes = slice(part * LANES, (part + 1) * LANES)
                    if slot in whole_slots:
                        outs[whole_slots.index(slot)][beam, tile, here, lanes] = piece
                        continue
                    entry = cut_slots.index(slot) * beams + beam
                    far_ref[entry, tile, here, lanes] = piece
                    for edge, edge_ref in zip(edges, edge_refs):
                        if edge == tile:
                            edge_ref[entry, 0, here, lanes] = piece
        return carry

    lax.fori_loop(0, steps // per, combine, 0)


def partial_beams(echoes, table, weights, chunk, width, edges, before=()):
    _, channels, pulses, _ = echoes.shape
    ranks = lax.axis_size("pulse")
    beams = weights.shape[1] // ranks
    rows = weights.shape[0] * 8
    groups = table.shape[0] // 16
    whole_slots, cut_slots = slot_kinds(ranks)
    far = len(cut_slots) * beams
    tiles = width // LANES
    outs = [jax.ShapeDtypeStruct((beams, tiles, rows, 2 * LANES), BF16)] * len(whole_slots)
    outs += [jax.ShapeDtypeStruct((far, tiles, rows, 2 * LANES), BF16)]
    outs += [jax.ShapeDtypeStruct((far, 1, rows, 2 * LANES), BF16)] * len(edges)
    outs += [jax.ShapeDtypeStruct((8, LANES), F32)]
    whole = pl.BlockSpec(memory_space=pltpu.VMEM)
    anywhere = pl.BlockSpec(memory_space=pl.ANY)
    result = pl.pallas_call(
        functools.partial(partial_beams_body, ranks, beams, edges),
        grid=(1,),
        out_shape=outs,
        in_specs=[
            pl.BlockSpec((2, channels, pulses, width), lambda i: (0, 0, 0, chunk)),
            whole,
            anywhere,
        ]
        + [anywhere] * len(before),
        out_specs=[whole] * len(outs),
        scratch_shapes=[
            pltpu.VMEM((2, 2, width // LANES, pulses, LANES), F32),
            pltpu.VMEM((2, ranks, 2 * pulses // ranks, width), BF16),
            pltpu.VMEM((groups, channels * ranks, 16, width), BF16),
            pltpu.VMEM(weights.shape, BF16),
            pltpu.SemaphoreType.DMA,
        ],
        compiler_params=pltpu.CompilerParams(vmem_limit_bytes=VMEM_LIMIT),
        cost_estimate=SMALL_COST,
        name="partial_beams",
    )(echoes, table, weights, *before)
    count = len(whole_slots)
    return result[:count], result[count], result[count + 1 : -1], result[-1]


def summed_body(terms, edges, *refs):
    ins, outs = refs[:terms], refs[-1 - len(edges) :]
    total = ins[0][...].astype(F32)
    for term in ins[1:]:
        total += term[...].astype(F32)
    total = total.astype(BF16)
    outs[0][...] = total
    for edge, edge_ref in zip(edges, outs[1:]):
        edge_ref[0, 0] = total[0, edge]


def summed_block(terms, edges, before=()):
    beams, tiles, rows, lanes = terms[0].shape
    block = pl.BlockSpec((1, tiles, rows, lanes), lambda i: (i, 0, 0, 0))
    single = pl.BlockSpec((1, 1, rows, lanes), lambda i: (i, 0, 0, 0))
    return pl.pallas_call(
        functools.partial(summed_body, len(terms), edges),
        grid=(beams,),
        out_shape=[jax.ShapeDtypeStruct(terms[0].shape, BF16)]
        + [jax.ShapeDtypeStruct((beams, 1, rows, lanes), BF16)] * len(edges),
        in_specs=[block] * len(terms) + [pl.BlockSpec(memory_space=pl.ANY)] * len(before),
        out_specs=[block] + [single] * len(edges),
        compiler_params=pltpu.CompilerParams(vmem_limit_bytes=VMEM_LIMIT),
        cost_estimate=SMALL_COST,
        name="summed_block",
    )(*terms, *before)


def toeplitz_body(replica_ref, before_ref, out_ref):
    chirp = replica_ref.shape[1]
    span = chirp + LANES
    padded = jnp.concatenate(
        [replica_ref[...].astype(F32), jnp.zeros((2, LANES), F32)], axis=1
    )
    taps = []
    for part in range(2):
        rows = jnp.broadcast_to(padded[part : part + 1], (LANES, span))
        taps.append(pltpu.roll(rows, 0, 1, stride=1, stride_axis=0).T)
    real, imag = (tap.astype(BF16) for tap in taps)
    split = LANES // 2
    low, high = slice(0, split), slice(split, LANES)
    for part, (own, other) in enumerate(((real, -imag), (imag, real))):
        columns = jnp.concatenate(
            [own[:, low], other[:, low], other[:, high], own[:, high]], axis=1
        )
        for tile in range(span // LANES):
            first = (2 * tile + part) * LANES
            out_ref[first : first + LANES, :] = columns[tile * LANES : (tile + 1) * LANES]


def toeplitz_taps(replica, before):
    return pl.pallas_call(
        toeplitz_body,
        out_shape=jax.ShapeDtypeStruct((2 * (replica.shape[1] + LANES), 2 * LANES), BF16),
        in_specs=[pl.BlockSpec(memory_space=pltpu.VMEM), pl.BlockSpec(memory_space=pl.ANY)],
        cost_estimate=SMALL_COST,
        name="toeplitz_taps",
    )(replica, before)


def tiles_body(tracks, place_ref, flag_ref, taps_ref, repeat_ref, gather_ref, *rest):
    pieces, (out_ref, line_ref, cut_ref) = rest[:-3], rest[-3:]
    entry = pl.program_id(0)
    rows = pieces[0].shape[2]
    span = taps_ref.shape[0] // (2 * LANES)
    columns = [(piece, tile) for piece in pieces for tile in range(piece.shape[1])]
    for block in range(len(columns) - span + 1):
        window = [piece[0, tile] for piece, tile in columns[block : block + span]]
        product = jnp.dot(
            jnp.concatenate(window, axis=1), taps_ref[...], preferred_element_type=F32
        )
        if block == 0:
            product = jnp.where(flag_ref[:1, :1] == 0.0, 0.0, product)
        line_ref[2 * block * rows : (2 * block + 1) * rows, :] = product[:, :LANES]
        line_ref[(2 * block + 1) * rows : (2 * block + 2) * rows, :] = product[:, LANES:]

    lane_id = lax.broadcasted_iota(jnp.int32, (TILE, LANES), 1) % (LANES // 2)
    batch = 16

    def cut(step, carry):
        values = []
        for within in range(batch):
            track = step * batch + within
            row = place_ref[0, entry, track]
            low = line_ref[pl.ds(row, TILE), :]
            high = line_ref[pl.ds(row + rows, TILE), :]
            values.append(jnp.where(lane_id >= place_ref[1, entry, track], low, high))
        values = [
            pltpu.roll(value, place_ref[2, entry, step * batch + within], 1)
            for within, value in enumerate(values)
        ]
        here = pl.ds(pl.multiple_of(step * batch * TILE, batch * TILE), batch * TILE)
        cut_ref[here, :] = jnp.concatenate(values, axis=0).astype(BF16)
        return carry

    lax.fori_loop(0, tracks // batch, cut, 0)

    group = 2 * LANES
    many = divisor_up_to(tracks * TILE // group, 4) * group
    row_id = lax.broadcasted_iota(jnp.int32, (many, group), 0) % 8
    wanted = row_id == lax.broadcasted_iota(jnp.int32, (many, group), 1) % LANES // TILE
    for start in range(0, tracks * TILE, many):
        repeated = jnp.dot(
            cut_ref[start : start + many, :], repeat_ref[...], preferred_element_type=F32
        )
        masked = jnp.where(wanted, repeated, 0.0).astype(BF16)
        for first in range(0, many, group):
            value = jnp.dot(
                gather_ref[...], masked[first : first + group], preferred_element_type=F32
            )
            here = (start + first) // 8
            out_ref[0, here : here + group // 8, :] = value.astype(BF16)


def slots_body(terms, slot_ref, *rest):
    parts, (out_ref, total_ref, sorted_ref) = rest[:terms], rest[-3:]
    total = parts[0][0].astype(F32)
    for part in parts[1:]:
        total += part[0].astype(F32)
    for part in range(2):
        total_ref[part] = total[:, part * LANES : (part + 1) * LANES]
    sorted_ref[...] = jnp.zeros(sorted_ref.shape, F32)

    def move(track, carry):
        target = pl.ds(slot_ref[track] * 2, 2)
        sorted_ref[:, target, :] = total_ref[:, pl.ds(track * 2, 2), :]
        return carry

    lax.fori_loop(0, slot_ref.shape[0], move, 0, unroll=8)
    for part in range(2):
        out_ref[:, part * LANES : (part + 1) * LANES] = sorted_ref[part].astype(BF16)


def slotted(terms, slots, slot_total):
    count, lanes = terms[0][0].shape[1:]
    return pl.pallas_call(
        functools.partial(slots_body, len(terms)),
        grid=(1,),
        out_shape=jax.ShapeDtypeStruct((slot_total * 2, lanes), BF16),
        in_specs=[pl.BlockSpec(memory_space=pltpu.SMEM)]
        + [
            pl.BlockSpec((1, count, lanes), lambda i, entry=entry: (entry, 0, 0))
            for _, entry in terms
        ],
        out_specs=pl.BlockSpec((slot_total * 2, lanes), lambda i: (0, 0)),
        scratch_shapes=[
            pltpu.VMEM((2, count, LANES), F32),
            pltpu.VMEM((2, slot_total * 2, LANES), F32),
        ],
        compiler_params=pltpu.CompilerParams(vmem_limit_bytes=VMEM_LIMIT),
        cost_estimate=SMALL_COST,
        name="slotted_tiles",
    )(slots, *[term for term, _ in terms])


def cut_places(bins, gates, rows):
    first = gates + (LANES - HALF)
    half = LANES // 2
    return jnp.stack([first // half * rows + bins, first % half, (LANES - first % LANES) % LANES])


def beam_tiles(taps, pieces, places, flag, gate_len):
    _, entries, tracks = places.shape
    rows = pieces[0][0].shape[2]
    scalar = pl.BlockSpec(memory_space=pltpu.SMEM)
    blocks = gate_len // LANES + 2
    group = 2 * LANES
    column = np.arange(group)[None, :]
    repeat = np.arange(LANES)[:, None] == column // LANES * (LANES // 2) + column % TILE
    repeat = repeat.astype(ml_dtypes.bfloat16)
    gather = np.arange(group // 8)[:, None] == np.arange(group)[None, :] // 8
    gather = gather.astype(ml_dtypes.bfloat16)
    return pl.pallas_call(
        functools.partial(tiles_body, tracks),
        grid=(entries,),
        out_shape=jax.ShapeDtypeStruct((entries, tracks * 2, group), BF16),
        in_specs=[
            scalar,
            pl.BlockSpec(flag.shape, lambda i: (0, 0)),
            pl.BlockSpec(taps.shape, lambda i: (0, 0)),
            pl.BlockSpec(repeat.shape, lambda i: (0, 0)),
            pl.BlockSpec(gather.shape, lambda i: (0, 0)),
        ]
        + [
            pl.BlockSpec((1,) + piece.shape[1:], lambda i, offset=offset: (i + offset, 0, 0, 0))
            for piece, offset in pieces
        ],
        out_specs=pl.BlockSpec((1, tracks * 2, group), lambda i: (i, 0, 0)),
        scratch_shapes=[
            pltpu.VMEM((2 * blocks * rows, LANES), F32),
            pltpu.VMEM((tracks * TILE, LANES), BF16),
        ],
        compiler_params=pltpu.CompilerParams(vmem_limit_bytes=VMEM_LIMIT),
        cost_estimate=SMALL_COST,
        name="beam_tiles",
    )(places, flag, taps, repeat, gather, *[piece for piece, _ in pieces])


def finish_body(*refs):
    parts, out_ref, wide_ref = refs[:-2], refs[-2], refs[-1]
    rows = out_ref.shape[0]
    for beam, part in enumerate(parts):
        for side in range(2):
            wide_ref[...] = part[:, side * LANES : (side + 1) * LANES].astype(F32)
            for half in range(2):
                column = ((side * len(parts) + beam) * 2 + half) * LANES
                out_ref[:, column : column + LANES] = wide_ref[pl.ds(half, rows, stride=2), :]


def finished(parts, rows):
    whole = pl.BlockSpec(memory_space=pltpu.VMEM)
    return pl.pallas_call(
        finish_body,
        out_shape=jax.ShapeDtypeStruct((rows, len(parts) * 4 * LANES), F32),
        in_specs=[whole] * len(parts),
        out_specs=whole,
        scratch_shapes=[pltpu.VMEM((rows * 2, LANES), F32)],
        compiler_params=pltpu.CompilerParams(vmem_limit_bytes=32 * 2**20),
        cost_estimate=SMALL_COST,
        name="finished_tiles",
    )(*parts)


def local(echoes, replica, beam_weights, track_doppler, track_gate, track_owner):
    gate_len = echoes.shape[3]
    chirp = replica.shape[1]
    _, beams, _, bins = beam_weights.shape
    ranks = lax.axis_size("pulse")
    owners = ranks * lax.axis_size("gate")
    table = pulse_table(bins, echoes.shape[2] // ranks)

    track_count = track_owner.shape[0]
    capacity = max(2, 5 * track_count // (2 * owners))
    owner_match = (
        track_owner[:, None] == jnp.arange(owners, dtype=jnp.int32)[None, :]
    ).astype(jnp.int32)
    running = jnp.cumsum(owner_match, axis=0, dtype=jnp.int32)
    slot_rank = jnp.sum(running * owner_match, axis=1, dtype=jnp.int32) - 1
    slots = track_owner * capacity + slot_rank
    place = jnp.stack([track_doppler % bins, track_gate % gate_len])

    def exchanged(value, slot):
        return lax.ppermute(value, "pulse", [(rank, rank ^ slot) for rank in range(ranks)])

    whole_slots, cut_slots = slot_kinds(ranks)

    width = gate_len // 2
    last_tile = width // LANES - 1
    spare_chunk, spare_steps = chirp % gate_len // width, chirp // gate_len + 1
    halo_chunks = [(position // gate_len + 1, position % gate_len // width) for position in range(0, chirp, width)]
    edges = [[], [last_tile]]
    edges[spare_chunk] = [0] + edges[spare_chunk]

    extra = jnp.pad(place.astype(F32), ((0, 6), (0, bins - place.shape[1])))
    rows = bins + TILE
    track_count = place.shape[1]
    place = cut_places(place[0], place[1], rows)[:, None]
    weights, extras = combining_weights(beam_weights, chirp, extra, [place])
    far_places = [extras[slot][:2, :track_count].astype(jnp.int32) for slot in cut_slots]
    far_places = jnp.stack(
        [cut_places(item[0], item[1], rows) for item in far_places for _ in range(beams)], axis=1
    )
    first_blocks, far, far_edges, flag = partial_beams(echoes, table, weights, 0, width, edges[0])
    fars, ends = [far], [far_edges]
    flag = passed_along(flag, "gate", 1)
    second_blocks, far, far_edges, ones = partial_beams(
        echoes, table, weights, 1, width, edges[1], before=[flag, far_places]
    )
    taps = toeplitz_taps(replica, ones)
    fars, ends = fars + [far], ends + [far_edges]

    def with_halo(full, spare, left):
        before = passed_along(left, "gate", 1)
        after = [passed_along(full[chunk], "gate", -steps) for steps, chunk in halo_chunks]
        return [before] + full + after + [passed_along(spare, "gate", -spare_steps)]

    def neighbours(blocks):
        return [blocks[0]] + [
            exchanged(blocks[kind], whole_slots[kind]) for kind in range(1, len(whole_slots))
        ]

    first = summed_block(neighbours(first_blocks), edges[0])
    far_pieces = with_halo(fars, ends[spare_chunk][0], ends[1][-1])
    far_tiles = beam_tiles(
        taps, [(piece, 0) for piece in far_pieces], far_places, flag, gate_len
    )
    arrived = [
        exchanged(far_tiles[kind * beams : (kind + 1) * beams], slot)
        for kind, slot in enumerate(cut_slots)
    ]
    second = summed_block(neighbours(second_blocks), edges[1], before=[far_tiles])
    own_pieces = with_halo([first[0], second[0]], [first, second][spare_chunk][1], second[-1])
    results = []
    for beam in range(beams):
        tiles = beam_tiles(
            taps, [(piece, beam) for piece in own_pieces], place, flag, gate_len
        )
        tiles = slotted(
            [(tiles, 0)] + [(item, beam) for item in arrived], slots, owners * capacity
        )
        sent = lax.all_to_all(
            tiles.reshape(owners, capacity * 2, 2 * LANES),
            ("pulse", "gate"),
            split_axis=0,
            concat_axis=0,
            tiled=True,
        )
        results.append(sent.reshape(owners * capacity * 2, 2 * LANES))
    return finished(results, owners * capacity)


def solution(mesh):
    return jax.shard_map(
        local,
        mesh=mesh,
        in_specs=(
            P(None, None, "pulse", "gate"),
            P(),
            P(None, None, None, "pulse"),
            P(("pulse", "gate")),
            P(("pulse", "gate")),
            P(("pulse", "gate")),
        ),
        out_specs=P(("pulse", "gate"), None),
        check_vma=False,
    )
```

time: 1400 us -> 164 us (0.12); the launches traced: 1370 us -> 163 us
  local copies, waits for them, and re-layouts: 1030 us -> 2.8 us
  waiting for transfers between devices: 194 us -> 14.4 us
  Pallas kernels: 0 us -> 80.1 us
  matrix products: 41.1 us -> 0 us
  other arithmetic: 39.7 us -> 4.26 us
  blocking collectives: 46.3 us -> 21.8 us
  starting transfers between devices: 20.7 us -> 39.7 us
    gather x6 -> x0, local copies, waits for them, and re-layouts: 707 us -> none  [the longest x2 287 us: compress_range(): real_tap = jnp.where(inside, jnp.take(replica[0], safe_lag), nothing)]
    convert_element_type x6 -> x0, local copies, waits for them, and re-layouts: 270 us -> none  [the longest x1 231 us: local(): extended_2(beams.astype(jnp.bfloat16), (('pulse', 2), ('gate', 3)), TILE...]
    all_to_all x2 -> x1, waiting for transfers between devices: 186 us -> 8.88 us  [local(): lax.all_to_all(tiles.reshape(owners, capacity * 2, 2 * LANES), ('pulse',...]
    pallas_call x0 -> x12, Pallas kernels: none -> 80.1 us  [the longest x2 29.1 us: partial_beams(): pl.pallas_call(functools.partial(partial_beams_body, ranks, beams, edges)...]
    dot_general x6 -> x0, matrix products: 41.1 us -> none  [the longest x1 17.7 us: doppler_transform(): jnp.einsum('oieb,icabg->oceag', complex_table(second), twisted, preferred...]
    all_to_all x1, blocking collectives: 46.3 us -> 21.8 us  [local(): lax.all_to_all(tiles.reshape(owners, capacity * 2, 2 * LANES), ('pulse',...]
    all_to_all x3 -> x0, local copies, waits for them, and re-layouts: 23.8 us -> none  [the longest x1 13.2 us: local(): lax.all_to_all(compressed, 'pulse', split_axis=1, concat_axis=2, tiled=True)]
    convert_element_type x5 -> x3, other arithmetic: 20.8 us -> 0.72 us  [the longest x1 0.7 us: local(): extras[slot][:2, :track_count].astype(jnp.int32)]
  transfers between devices with their start and end apart: 7 -> 16, of which waited for: 5 -> 5; matrix products, arithmetic and copies ran while one was open for 43% -> 2% of each run, Pallas kernels for 0% -> 33%
where the time goes in v1:
time: 164 us; the launch traced here: 163 us
  Pallas kernels  80.1 us (49%)
  starting transfers between devices  39.7 us (24%)
  blocking collectives  21.8 us (13%)
  waiting for transfers between devices  14.4 us (9%)
  other arithmetic  4.26 us (3%)
  local copies, waits for them, and re-layouts  2.8 us (2%)
    pallas_call x2, Pallas kernels, partial_beams(): pl.pallas_call(functools.partial(partial_beams_body, ranks, beams, edges)...  29.1 us
    pallas_call x3, Pallas kernels, beam_tiles(): pl.pallas_call(functools.partial(tiles_body, tracks), grid=(entries,), ou...  28.2 us
    all_to_all x1, blocking collectives, local(): lax.all_to_all(tiles.reshape(owners, capacity * 2, 2 * LANES), ('pulse',...  21.8 us
    ppermute x7, starting transfers between devices, passed_along(): lax.ppermute(value, axis, [(source, source + steps) for source in range(l...  18.3 us
    all_to_all x1, starting transfers between devices, local(): lax.all_to_all(tiles.reshape(owners, capacity * 2, 2 * LANES), ('pulse',...  10.9 us
    all_to_all x1, waiting for transfers between devices, local(): lax.all_to_all(tiles.reshape(owners, capacity * 2, 2 * LANES), ('pulse',...  8.88 us
    pallas_call x1, Pallas kernels, combining_weights(): pl.pallas_call(functools.partial(weights_body, ranks), grid=(groups // pe...  7.96 us
    ppermute x5, starting transfers between devices, exchanged(): lax.ppermute(value, 'pulse', [(rank, rank ^ slot) for rank in range(ranks)])  6.05 us
  transfers between devices with their start and end apart: 16, of which 5 were waited for; matrix products, arithmetic and copies ran while one was open for 2% of the time, Pallas kernels for 33%

profile of v1, /device:TPU:0, one launch (start us, length us, event | category | flops | bytes accessed | tf_op | source)
XLA Modules:
  0.0 163.3 jit_solution(3746433159345134227)
XLA Ops:
  0.0 0.7 multiply_add_fusion
  0.7 0.8 select_maximum_fusion.rest_0_
  1.6 3.9 %collective-permute-start.2 = (f32[40,512]{1,0:T(8,128)S(1)}, f32[40,512]{1,0:T(8,128)S(1)}, u32[]{:S(2)}, u32[]{:S(2)}) collective-permute-start(f32[40,512]{1,0:T(8,128)S(1)} %select_maximum_fusion.rest_0_), channel_id=1, source_target_pairs={{0,24},{8,16},{16,8},{24,0},{1,25},{9,17},{17,9},{25,1},{2,26},{10... | collective-permute-start | bytes 245768 | tf_op jit(solution)/shard_map/ppermute | solution.py:113
  5.5 0.5 collective-permute-start
  6.0 0.1 collective-permute-start.1
  6.1 0.6 broadcast_in_dim.2.rest_8_.place_ref
  6.7 1.6 collective-permute-done.2.rest_3_
  8.3 1.8 %collective-permute-done.rest_1_ = f32[40,512]{1,0:T(8,128)S(1)} collective-permute-done((f32[40,512]{1,0:T(8,128)S(1)}, f32[40,512]{1,0:T(8,128)S(1)}, u32[]{:S(2)}, u32[]{:S(2)}) %collective-permute-start) | collective-permute-done | bytes 81952 | tf_op jit(solution)/shard_map/ppermute | solution.py:113
  10.2 0.3 collective-permute-done.1.rest_2_
  10.5 0.4 copy-done.4
  10.8 0.3 copy-done.5
  11.1 8.0 %combining_weights.1.weight_hbm = bf16[66,8,16,512]{3,2,1,0:T(8,128)(2,1)} custom-call(s32[1]{0:T(128)} %bitcast.5.me_ref, f32[40,512]{1,0:T(8,128)} %copy-done.2, f32[40,512]{1,0:T(8,128)} %copy-done.4, f32[40,512]{1,0:T(8,128)} %copy-done.5, f32[40,512]{1,0:T(8,128)} %copy-done.3, f32[528,128]{1,0:T(8,128)} %constant.126.clone.rest_4_, ...), custom_call_target="tpu_custom_call" | custom-call | flops 1048576 | bytes 65536 | tf_op jit(solution)/shard_map/combining_weights/pallas_call | solution.py:134
  19.0 14.4 %partial_beams.2 = (bf16[2,2,528,256]{3,2,1,0:T(8,128)(2,1)}, bf16[2,2,528,256]{3,2,1,0:T(8,128)(2,1)}, bf16[2,2,528,256]{3,2,1,0:T(8,128)(2,1)}, bf16[2,2,528,256]{3,2,1,0:T(8,128)(2,1)}, f32[8,128]{1,0:T(8,128)}) custom-call(bf16[2,8,512,512]{3,2,1,0:T(8,128)(2,1)} %echo_ref.3, bf16[1024,256]{1,0:T(8,128)(2,1)} %constant.130.clone.table_ref, ...), custom_call_target="tpu_custom_call" | custom-call | flops 1048576 | bytes 65536 | tf_op jit(solution)/shard_map/partial_beams/pallas_call | solution.py:263
  33.5 1.6 collective-permute-start.10
  35.1 0.9 collective-permute-start.11
  36.0 1.3 collective-permute-start.3
  37.3 0.7 slice_convert_fusion
  38.0 0.6 pad_add_fusion.rest_1_.place_ref
  38.6 1.3 collective-permute-start.7
  39.9 0.0 collective-permute-done.3.rest_0_.flag_ref
  40.0 0.6 copy-done.6
  40.5 14.7 %partial_beams.3 = (bf16[2,2,528,256]{3,2,1,0:T(8,128)(2,1)}, bf16[2,2,528,256]{3,2,1,0:T(8,128)(2,1)}, bf16[2,2,528,256]{3,2,1,0:T(8,128)(2,1)}, bf16[2,2,528,2...) custom-call(bf16[2,8,512,512]{3,2,1,0:T(8,128)(2,1)} %echo_ref.3, ...), custom_call_target="tpu_custom_call" | custom-call | flops 1048576 | bytes 65536 | tf_op jit(solution)/shard_map/partial_beams/pallas_call | solution.py:263
  55.2 0.6 collective-permute-start.4
  55.8 1.1 collective-permute-start.5
  56.9 1.8 %collective-permute-done.10.refs_1_ = bf16[2,2,528,256]{3,2,1,0:T(8,128)(2,1)} collective-permute-done((bf16[2,2,528,256]{3,2,1,0:T(8,128)(2,1)}, bf16[2,2,528,256]{3,2,1,0:T(8,128)(2,1)}, u32[]{:S(2)}, u32[]{:S(2)}) %collective-permute-start.10) | collective-permute-done | bytes 1081376 | tf_op jit(solution)/shard_map/ppermute | solution.py:531
  58.7 2.5 %collective-permute-start.6 = (bf16[2,1,528,256]{3,2,1,0:T(8,128)(2,1)}, bf16[2,1,528,256]{3,2,1,0:T(8,128)(2,1)S(1)}, u32[]{:S(2)}, u32[]{:S(2)}) collective-permute-start(bf16[2,1,528,256]{3,2,1,0:T(8,128)(2,1)} %get-tuple-element.25), channel_id=1, source_target_pairs={{0,1},{1,2},{2,3},{3,4},{4,5},{5,6},{6,7},{8,9},{9,10},{10,11},{11... | collective-permute-start | bytes 1622024 | tf_op jit(solution)/shard_map/ppermute | solution.py:25
  61.3 1.3 collective-permute-start.8
  62.6 2.9 %summed_block.3.rest_1_ = bf16[2,2,528,256]{3,2,1,0:T(8,128)(2,1)} custom-call(bf16[2,2,528,256]{3,2,1,0:T(8,128)(2,1)} %get-tuple-element.30.refs_0_, bf16[2,2,528,256]{3,2,1,0:T(8,128)(2,1)} %collective-permute-done.10.refs_1_, bf16[2,2,528,256]{3,2,1,0:T(8,128)(2,1)} %collective-permute-done.11.refs_2_), custom_call_target="tpu_custom_call" | custom-call | flops 1048576 | bytes 65536 | tf_op jit(solution)/shard_map/summed_block/pallas_call | solution.py:304
  65.4 1.3 collective-permute-start.12
  66.7 1.8 %toeplitz_taps.1.taps_ref = bf16[768,256]{1,0:T(8,128)(2,1)} custom-call(bf16[2,256]{1,0:T(2,128)(2,1)} %replica_ref.1, f32[8,128]{1,0:T(8,128)} %get-tuple-element.21.before_ref), custom_call_target="tpu_custom_call" | custom-call | flops 1048576 | bytes 65536 | tf_op jit(solution)/shard_map/toeplitz_taps/pallas_call | solution.py:340
  68.5 13.2 %beam_tiles.3.refs_3_ = bf16[2,512,256]{2,1,0:T(8,128)(2,1)} custom-call(s32[3,2,256]{2,1,0:T(2,128)} %pad_add_fusion.rest_1_.place_ref, f32[8,128]{1,0:T(8,128)} %copy-done.6, bf16[768,256]{1,0:T(8,128)(2,1)} %toeplitz_taps.1.taps_ref, bf16[128,256]{1,0:T(8,128)(2,1)} %constant.131.clone.repeat_ref, bf16[32,256]{1,0:T(8,128)(2,1)} %constant.128.clone.rest_6_.gather_ref, ...), custom_call_target="tpu_custom_call" | custom-call | flops 1048576 | bytes 65536 | tf_op jit(solution)/shard_map/beam_tiles/pallas_call | solution.py:461
  81.7 1.9 %collective-permute-start.14 = (bf16[2,512,256]{2,1,0:T(8,128)(2,1)}, bf16[2,512,256]{2,1,0:T(8,128)(2,1)}, u32[]{:S(2)}, u32[]{:S(2)}) collective-permute-start(bf16[2,512,256]{2,1,0:T(8,128)(2,1)} %beam_tiles.3.refs_3_), channel_id=1, source_target_pairs={{0,24},{8,16},{16,8},{24,0},{1,25},{9,17},{17,9},{25,1},{2,26},{10... | collective-permute-start | bytes 1572872 | tf_op jit(solution)/shard_map/ppermute | solution.py:531
  83.6 3.0 %summed_block.2 = (bf16[2,2,528,256]{3,2,1,0:T(8,128)(2,1)}, bf16[2,1,528,256]{3,2,1,0:T(8,128)(2,1)}, bf16[2,1,528,256]{3,2,1,0:T(8,128)(2,1)}) custom-call(bf16[2,2,528,256]{3,2,1,0:T(8,128)(2,1)} %get-tuple-element.22.refs_0_, bf16[2,2,528,256]{3,2,1,0:T(8,128)(2,1)} %collective-permute-done.4.refs_1_, ...), custom_call_target="tpu_custom_call" | custom-call | flops 1048576 | bytes 65536 | tf_op jit(solution)/shard_map/summed_block/pallas_call | solution.py:304
  86.5 1.3 collective-permute-start.13
  87.8 9.3 %collective-permute-start.9 = (bf16[2,1,528,256]{3,2,1,0:T(8,128)(2,1)}, bf16[2,1,528,256]{3,2,1,0:T(8,128)(2,1)}, u32[]{:S(2)}, u32[]{:S(2)}) collective-permute-start(bf16[2,1,528,256]{3,2,1,0:T(8,128)(2,1)} %get-tuple-element.29), channel_id=1, source_target_pairs={{0,1},{1,2},{2,3},{3,4},{4,5},{5,6},{6,7},{8,9},{9,10},{10,11},{11... | collective-permute-start | bytes 1622024 | tf_op jit(solution)/shard_map/ppermute | solution.py:25
  97.2 0.6 reduce-window.6
  97.8 0.2 slice_reduce_fusion
  98.0 0.1 fusion.1
  98.1 0.6 add_add_fusion.slot_ref
  98.7 0.8 copy-done
  99.5 7.5 %beam_tiles.5.rest_0_ = bf16[1,512,256]{2,1,0:T(8,128)(2,1)} custom-call(s32[3,1,256]{2,1,0:T(1,128)} %broadcast_in_dim.2.rest_8_.place_ref, f32[8,128]{1,0:T(8,128)} %copy-done.6, bf16[768,256]{1,0:T(8,128)(2,1)} %toeplitz_taps.1.taps_ref, bf16[128,256]{1,0:T(8,128)(2,1)} %constant.131.clone.repeat_ref, bf16[32,256]{1,0:T(8,128)(2,1)} %constant.128.clone.rest_6_.gather_ref, ...), custom_call_target="tpu_custom_call" | custom-call | flops 1048576 | bytes 65536 | tf_op jit(solution)/shard_map/beam_tiles/pallas_call | solution.py:461
  107.0 2.6 %slotted_tiles.3 = bf16[1280,256]{1,0:T(8,128)(2,1)} custom-call(s32[256]{0:T(256)} %add_add_fusion.slot_ref, bf16[1,512,256]{2,1,0:T(8,128)(2,1)} %beam_tiles.5.rest_0_, bf16[2,512,256]{2,1,0:T(8,128)(2,1)} %collective-permute-done.14.rest_1_), custom_call_target="tpu_custom_call" | custom-call | flops 1048576 | bytes 65536 | tf_op jit(solution)/shard_map/slotted_tiles/pallas_call | solution.py:424
  109.6 10.9 %all-to-all-start.1 = ((bf16[32,40,256]{2,1,0:T(8,128)(2,1)}), bf16[32,40,256]{2,1,0:T(8,128)(2,1)S(1)}, u32[]{:S(2)}, u32[]{:S(2)}) async-start(bf16[32,40,256]{2,1,0:T(8,128)(2,1)} %bitcast.29), calls=%async_computation.1 | async-start | bytes 1310720 | tf_op jit(solution)/shard_map/all_to_all | solution.py:589
  120.5 7.5 %beam_tiles.4.rest_0_ = bf16[1,512,256]{2,1,0:T(8,128)(2,1)} custom-call(s32[3,1,256]{2,1,0:T(1,128)} %broadcast_in_dim.2.rest_8_.place_ref, f32[8,128]{1,0:T(8,128)} %copy-done.6, bf16[768,256]{1,0:T(8,128)(2,1)} %toeplitz_taps.1.taps_ref, bf16[128,256]{1,0:T(8,128)(2,1)} %constant.131.clone.repeat_ref, bf16[32,256]{1,0:T(8,128)(2,1)} %constant.128.clone.rest_6_.gather_ref, ...), custom_call_target="tpu_custom_call" | custom-call | flops 1048576 | bytes 65536 | tf_op jit(solution)/shard_map/beam_tiles/pallas_call | solution.py:461
  128.0 2.6 %slotted_tiles.2 = bf16[1280,256]{1,0:T(8,128)(2,1)} custom-call(s32[256]{0:T(256)} %add_add_fusion.slot_ref, bf16[1,512,256]{2,1,0:T(8,128)(2,1)} %beam_tiles.4.rest_0_, bf16[2,512,256]{2,1,0:T(8,128)(2,1)} %collective-permute-done.14.rest_1_), custom_call_target="tpu_custom_call" | custom-call | flops 1048576 | bytes 65536 | tf_op jit(solution)/shard_map/slotted_tiles/pallas_call | solution.py:424
  130.6 8.9 %all-to-all-done.1 = bf16[32,40,256]{2,1,0:T(8,128)(2,1)S(1)} async-done(((bf16[32,40,256]{2,1,0:T(8,128)(2,1)}), bf16[32,40,256]{2,1,0:T(8,128)(2,1)S(1)}, u32[]{:S(2)}, u32[]{:S(2)}) %all-to-all-start.1) | async-done | bytes 655392 | tf_op jit(solution)/shard_map/all_to_all | solution.py:589
  139.5 21.8 %all_to_all.10 = bf16[32,40,256]{2,1,0:T(8,128)(2,1)S(1)} all-to-all(bf16[32,40,256]{2,1,0:T(8,128)(2,1)} %bitcast.30), channel_id=1, replica_groups=mesh['pulse'=4,'gate'=8] {'pulse','gate'}, dimensions={0} | all-to-all | bytes 1310720 | tf_op jit(solution)/shard_map/all_to_all | solution.py:589
  161.3 2.0 %finished_tiles.1 = f32[640,1024]{1,0:T(8,128)} custom-call(bf16[1280,256]{1,0:T(8,128)(2,1)S(1)} %bitcast.28, bf16[1280,256]{1,0:T(8,128)(2,1)S(1)} %bitcast.27), custom_call_target="tpu_custom_call" | custom-call | flops 1048576 | bytes 65536 | tf_op jit(solution)/shard_map/finished_tiles/pallas_call | solution.py:500
  (32 shorter events, 0.2 us)
Async XLA Ops:
  1.6 8.9 %copy-start.2 = (f32[40,512]{1,0:T(8,128)}, f32[40,512]{1,0:T(8,128)S(1)}, u32[]{:S(2)}) copy-start(f32[40,512]{1,0:T(8,128)S(1)} %select_maximum_fusion.rest_0_) | copy-start | bytes 245764
  1.6 6.7 %collective-permute-start.2 = (f32[40,512]{1,0:T(8,128)S(1)}, f32[40,512]{1,0:T(8,128)S(1)}, u32[]{:S(2)}, u32[]{:S(2)}) collective-permute-start(f32[40,512]{1,0:T(8,128)S(1)} %select_maximum_fusion.rest_0_), channel_id=1, source_target_pairs={{0,24},{8,16},{16,8},{24,0},{1,25},{9,17},{17,9},{25,1},{2,26},{10... | collective-permute-start | bytes 245768 | tf_op jit(solution)/shard_map/ppermute | solution.py:113
  5.5 4.7 %collective-permute-start = (f32[40,512]{1,0:T(8,128)S(1)}, f32[40,512]{1,0:T(8,128)S(1)}, u32[]{:S(2)}, u32[]{:S(2)}) collective-permute-start(f32[40,512]{1,0:T(8,128)S(1)} %select_maximum_fusion.rest_0_), channel_id=1, source_target_pairs={{0,8},{8,0},{16,24},{24,16},{1,9},{9,1},{17,25},{25,17},{2,10},{10... | collective-permute-start | bytes 245768 | tf_op jit(solution)/shard_map/ppermute | solution.py:113
  6.0 4.4 %collective-permute-start.1 = (f32[40,512]{1,0:T(8,128)S(1)}, f32[40,512]{1,0:T(8,128)S(1)}, u32[]{:S(2)}, u32[]{:S(2)}) collective-permute-start(f32[40,512]{1,0:T(8,128)S(1)} %select_maximum_fusion.rest_0_), channel_id=1, source_target_pairs={{0,16},{8,24},{16,0},{24,8},{1,17},{9,25},{17,1},{25,9},{2,18},{10... | collective-permute-start | bytes 245768 | tf_op jit(solution)/shard_map/ppermute | solution.py:113
  8.3 2.1 %copy-start.3 = (f32[40,512]{1,0:T(8,128)}, f32[40,512]{1,0:T(8,128)S(1)}, u32[]{:S(2)}) copy-start(f32[40,512]{1,0:T(8,128)S(1)} %collective-permute-done.2.rest_3_) | copy-start | bytes 245764
  10.2 0.6 copy-start.4
  10.5 0.6 copy-start.5
  33.5 25.2 %collective-permute-start.10 = (bf16[2,2,528,256]{3,2,1,0:T(8,128)(2,1)}, bf16[2,2,528,256]{3,2,1,0:T(8,128)(2,1)}, u32[]{:S(2)}, u32[]{:S(2)}) collective-permute-start(bf16[2,2,528,256]{3,2,1,0:T(8,128)(2,1)} %get-tuple-element.31), channel_id=1, source_target_pairs={{0,8},{8,0},{16,24},{24,16},{1,9},{9,1},{17,25},{25,17},{2,10},{10... | collective-permute-start | bytes 3244040 | tf_op jit(solution)/shard_map/ppermute | solution.py:531
  35.1 26.2 %collective-permute-start.11 = (bf16[2,2,528,256]{3,2,1,0:T(8,128)(2,1)}, bf16[2,2,528,256]{3,2,1,0:T(8,128)(2,1)}, u32[]{:S(2)}, u32[]{:S(2)}) collective-permute-start(bf16[2,2,528,256]{3,2,1,0:T(8,128)(2,1)} %get-tuple-element.32), channel_id=1, source_target_pairs={{0,16},{8,24},{16,0},{24,8},{1,17},{9,25},{17,1},{25,9},{2,18},{10... | collective-permute-start | bytes 3244040 | tf_op jit(solution)/shard_map/ppermute | solution.py:531
  36.0 3.9 %collective-permute-start.3 = (f32[8,128]{1,0:T(8,128)}, f32[8,128]{1,0:T(8,128)S(1)}, u32[]{:S(2)}, u32[]{:S(2)}) collective-permute-start(f32[8,128]{1,0:T(8,128)} %get-tuple-element.20), channel_id=1, source_target_pairs={{0,1},{1,2},{2,3},{3,4},{4,5},{5,6},{6,7},{8,9},{9,10},{10,11},{11... | collective-permute-start | bytes 12296 | tf_op jit(solution)/shard_map/ppermute | solution.py:25
  38.6 29.9 %collective-permute-start.7 = (bf16[2,2,528,256]{3,2,1,0:T(8,128)(2,1)}, bf16[2,2,528,256]{3,2,1,0:T(8,128)(2,1)}, u32[]{:S(2)}, u32[]{:S(2)}) collective-permute-start(bf16[2,2,528,256]{3,2,1,0:T(8,128)(2,1)} %get-tuple-element.26.rest_1_), channel_id=1, source_target_pairs={{1,0},{2,1},{3,2},{4,3},{5,4},{6,5},{7,6},{9,8},{10,9},{11,10},{12... | collective-permute-start | bytes 3244040 | tf_op jit(solution)/shard_map/ppermute | solution.py:25
  39.9 0.6 copy-start.6
  55.2 28.3 %collective-permute-start.4 = (bf16[2,2,528,256]{3,2,1,0:T(8,128)(2,1)}, bf16[2,2,528,256]{3,2,1,0:T(8,128)(2,1)}, u32[]{:S(2)}, u32[]{:S(2)}) collective-permute-start(bf16[2,2,528,256]{3,2,1,0:T(8,128)(2,1)} %get-tuple-element.23), channel_id=1, source_target_pairs={{0,8},{8,0},{16,24},{24,16},{1,9},{9,1},{17,25},{25,17},{2,10},{10... | collective-permute-start | bytes 3244040 | tf_op jit(solution)/shard_map/ppermute | solution.py:531
  55.8 27.7 %collective-permute-start.5 = (bf16[2,2,528,256]{3,2,1,0:T(8,128)(2,1)}, bf16[2,2,528,256]{3,2,1,0:T(8,128)(2,1)}, u32[]{:S(2)}, u32[]{:S(2)}) collective-permute-start(bf16[2,2,528,256]{3,2,1,0:T(8,128)(2,1)} %get-tuple-element.24), channel_id=1, source_target_pairs={{0,16},{8,24},{16,0},{24,8},{1,17},{9,25},{17,1},{25,9},{2,18},{10... | collective-permute-start | bytes 3244040 | tf_op jit(solution)/shard_map/ppermute | solution.py:531
  58.7 6.7 %collective-permute-start.6 = (bf16[2,1,528,256]{3,2,1,0:T(8,128)(2,1)}, bf16[2,1,528,256]{3,2,1,0:T(8,128)(2,1)S(1)}, u32[]{:S(2)}, u32[]{:S(2)}) collective-permute-start(bf16[2,1,528,256]{3,2,1,0:T(8,128)(2,1)} %get-tuple-element.25), channel_id=1, source_target_pairs={{0,1},{1,2},{2,3},{3,4},{4,5},{5,6},{6,7},{8,9},{9,10},{10,11},{11... | collective-permute-start | bytes 1622024 | tf_op jit(solution)/shard_map/ppermute | solution.py:25
  61.3 7.3 %collective-permute-start.8 = (bf16[2,1,528,256]{3,2,1,0:T(8,128)(2,1)}, bf16[2,1,528,256]{3,2,1,0:T(8,128)(2,1)}, u32[]{:S(2)}, u32[]{:S(2)}) collective-permute-start(bf16[2,1,528,256]{3,2,1,0:T(8,128)(2,1)} %get-tuple-element.28), channel_id=1, source_target_pairs={{1,0},{2,1},{3,2},{4,3},{5,4},{6,5},{7,6},{9,8},{10,9},{11,10},{12... | collective-permute-start | bytes 1622024 | tf_op jit(solution)/shard_map/ppermute | solution.py:25
  65.4 3.1 %copy-start.1 = (bf16[2,1,528,256]{3,2,1,0:T(8,128)(2,1)}, bf16[2,1,528,256]{3,2,1,0:T(8,128)(2,1)S(1)}, u32[]{:S(2)}) copy-start(bf16[2,1,528,256]{3,2,1,0:T(8,128)(2,1)S(1)} %collective-permute-done.6.rest_0_) | copy-start | bytes 1622020
  65.4 33.3 %collective-permute-start.12 = (bf16[2,2,528,256]{3,2,1,0:T(8,128)(2,1)}, bf16[2,2,528,256]{3,2,1,0:T(8,128)(2,1)}, u32[]{:S(2)}, u32[]{:S(2)}) collective-permute-start(bf16[2,2,528,256]{3,2,1,0:T(8,128)(2,1)} %summed_block.3.rest_1_), channel_id=1, source_target_pairs={{1,0},{2,1},{3,2},{4,3},{5,4},{6,5},{7,6},{9,8},{10,9},{11,10},{12... | collective-permute-start | bytes 3244040 | tf_op jit(solution)/shard_map/ppermute | solution.py:25
  81.7 25.3 %collective-permute-start.14 = (bf16[2,512,256]{2,1,0:T(8,128)(2,1)}, bf16[2,512,256]{2,1,0:T(8,128)(2,1)}, u32[]{:S(2)}, u32[]{:S(2)}) collective-permute-start(bf16[2,512,256]{2,1,0:T(8,128)(2,1)} %beam_tiles.3.refs_3_), channel_id=1, source_target_pairs={{0,24},{8,16},{16,8},{24,0},{1,25},{9,17},{17,9},{25,1},{2,26},{10... | collective-permute-start | bytes 1572872 | tf_op jit(solution)/shard_map/ppermute | solution.py:531
  83.5 13.6 %copy-start.7 = (s32[256]{0:T(256)S(1)}, s32[256]{0:T(256)}, u32[]{:S(2)}) copy-start(s32[256]{0:T(256)} %param.22) | copy-start | bytes 3076
  86.5 12.1 %collective-permute-start.13 = (bf16[2,1,528,256]{3,2,1,0:T(8,128)(2,1)}, bf16[2,1,528,256]{3,2,1,0:T(8,128)(2,1)S(1)}, u32[]{:S(2)}, u32[]{:S(2)}) collective-permute-start(bf16[2,1,528,256]{3,2,1,0:T(8,128)(2,1)} %get-tuple-element.34), channel_id=1, source_target_pairs={{1,0},{2,1},{3,2},{4,3},{5,4},{6,5},{7,6},{9,8},{10,9},{11,10},{12... | collective-permute-start | bytes 1622024 | tf_op jit(solution)/shard_map/ppermute | solution.py:25
  87.8 10.9 %collective-permute-start.9 = (bf16[2,1,528,256]{3,2,1,0:T(8,128)(2,1)}, bf16[2,1,528,256]{3,2,1,0:T(8,128)(2,1)}, u32[]{:S(2)}, u32[]{:S(2)}) collective-permute-start(bf16[2,1,528,256]{3,2,1,0:T(8,128)(2,1)} %get-tuple-element.29), channel_id=1, source_target_pairs={{0,1},{1,2},{2,3},{3,4},{4,5},{5,6},{6,7},{8,9},{9,10},{10,11},{11... | collective-permute-start | bytes 1622024 | tf_op jit(solution)/shard_map/ppermute | solution.py:25
  98.7 0.8 copy-start
  109.6 29.9 %all-to-all-start.1 = ((bf16[32,40,256]{2,1,0:T(8,128)(2,1)}), bf16[32,40,256]{2,1,0:T(8,128)(2,1)S(1)}, u32[]{:S(2)}, u32[]{:S(2)}) async-start(bf16[32,40,256]{2,1,0:T(8,128)(2,1)} %bitcast.29), calls=%async_computation.1 | async-start | bytes 1310720 | tf_op jit(solution)/shard_map/all_to_all | solution.py:589

commit v2 on v1

--- a/solution.py
+++ b/solution.py
@@ -35,122 +35,109 @@
     return table.reshape(2 * bins, 2 * depth).astype(ml_dtypes.bfloat16)
 
 
-def weights_body(ranks, me_ref, *rest):
-    parts, rest = rest[:ranks], rest[ranks:]
-    cos_ref, sin_ref, select_ref, spread_ref, out_ref, line_ref = rest[:4] + rest[-2:]
-    bins = parts[0].shape[1]
-    span = out_ref.shape[0] * 8
-    lanes = cos_ref.shape[1]
-    me = me_ref[0]
-    step = pl.program_id(0)
-
-    @pl.when(step == 0)
-    def _():
-        line_ref[:HALF, :] = jnp.zeros((HALF, line_ref.shape[1]), F32)
-        line_ref[HALF + ranks * bins :, :] = jnp.zeros((HALF, line_ref.shape[1]), F32)
-        for slot in range(ranks):
-            first = pl.multiple_of((slot ^ me) * bins + HALF, 8)
-            line_ref[pl.ds(first, bins), :] = parts[slot][...].T
-
+def gather_lines(me, parts, line_ref):
+    count, bins = line_ref.shape[1], parts[0].shape[1]
+    ends = jnp.zeros((HALF, count), F32)
+    line_ref[:HALF, :] = ends
+    line_ref[HALF + len(parts) * bins :, :] = ends
+    for slot, part in enumerate(parts):
+        first = pl.multiple_of((slot ^ me) * bins + HALF, 8)
+        line_ref[pl.ds(first, bins), :] = part[:count, :].T
+
+
+def quarter_turns(turn, ranks):
+    cos_part = jnp.ones(turn.shape, F32)
+    sin_part = jnp.zeros(turn.shape, F32)
+    for value in range(1, ranks):
+        angle = 2 * math.pi * value / ranks
+        cos_part = jnp.where(turn == value, round(math.cos(angle), 12), cos_part)
+        sin_part = jnp.where(turn == value, round(math.sin(angle), 12), sin_part)
+    return cos_part, sin_part
+
+
+def turn_tables(ranks, me, cos_ref, sin_ref, turned_ref):
+    rows, lanes = cos_ref.shape
+    offset = lax.broadcasted_iota(jnp.int32, (rows, lanes), 0) + (ranks * 8 - HALF)
+    turn_cos, turn_sin = quarter_turns((me * offset) & (ranks - 1), ranks)
     base_cos, base_sin = cos_ref[...], sin_ref[...]
-    lane_id = lax.broadcasted_iota(jnp.int32, (span, lanes), 1)
-    phase = lane_id // 2 % ranks
-    first_part = lane_id % 2 == 0
-    offset = lax.broadcasted_iota(jnp.int32, (span, lanes), 0) + step * span + (ranks * 8 - HALF)
-    lines = []
-    for slot in range(ranks):
-        block = slot ^ me
+    turned_ref[0] = turn_cos * base_cos - turn_sin * base_sin
+    turned_ref[1] = turn_sin * base_cos + turn_cos * base_sin
+
+
+def fill_weights(ranks, bins, slot, me, line_ref, turned_ref, select_ref, weight_ref):
+    groups, pairs, _, depth = weight_ref.shape
+    per = divisor_up_to(groups, 11)
+    span = per * 8
+    lanes = turned_ref.shape[2]
+    lane_id = lax.broadcasted_iota(jnp.int32, (8, lanes), 1)
+    block = slot ^ me
+    slot_cos, slot_sin = quarter_turns((block * (lane_id // 2 % ranks)) & (ranks - 1), ranks)
+    first_part = lane_id[:1] % 2 == 0
+    slot_cos, slot_sin = slot_cos[:1], slot_sin[:1]
+    own_cos = jnp.where(first_part, slot_cos, slot_sin)
+    own_sin = jnp.where(first_part, -slot_sin, slot_cos)
+    cells = (span * 2, LANES)
+    column = lax.broadcasted_iota(jnp.int32, cells, 1)
+    diagonal = lax.broadcasted_iota(jnp.int32, cells, 0) % 8 == column % 8
+    source_lane = column // 8
+    for step in range(groups // per):
+        here = slice(step * span, (step + 1) * span)
         rows = line_ref[pl.ds(pl.multiple_of(block * bins + step * span, 8), span), :]
         high = rows.astype(BF16)
         low = (rows - high.astype(F32)).astype(BF16)
         wide = jnp.dot(high, select_ref[...], preferred_element_type=F32) + jnp.dot(
             low, select_ref[...], preferred_element_type=F32
         )
-        turn = (me * offset + block * phase) & (ranks - 1)
-        turn_cos = jnp.ones(turn.shape, F32)
-        turn_sin = jnp.zeros(turn.shape, F32)
-        for value in range(1, ranks):
-            angle = 2 * math.pi * value / ranks
-            turn_cos = jnp.where(turn == value, round(math.cos(angle), 12), turn_cos)
-            turn_sin = jnp.where(turn == value, round(math.sin(angle), 12), turn_sin)
-        cos_part = turn_cos * base_cos - turn_sin * base_sin
-        sin_part = turn_sin * base_cos + turn_cos * base_sin
-        own = jnp.where(first_part, cos_part, sin_part)
-        other = jnp.where(first_part, sin_part, -cos_part)
+        base_cos, base_sin = turned_ref[0, here, :], turned_ref[1, here, :]
+        own = base_cos * own_cos + base_sin * own_sin
+        other = base_sin * own_cos - base_cos * own_sin
         real, imag = wide[:, :lanes], wide[:, lanes:]
-        out_real = (real * own + imag * other).reshape(span // 8, 8, lanes)
-        out_imag = (imag * own - real * other).reshape(span // 8, 8, lanes)
+        out_real = (real * own + imag * other).reshape(per, 8, lanes)
+        out_imag = (imag * own - real * other).reshape(per, 8, lanes)
         both = jnp.concatenate([out_real, out_imag], axis=1).reshape(span * 2, lanes)
-        lines.append(both.astype(BF16))
-    product = jnp.dot(
-        jnp.concatenate(lines, axis=0), spread_ref[...], preferred_element_type=F32
-    )
-    row_id = lax.broadcasted_iota(jnp.int32, product.shape, 0) % 8
-    diagonal = row_id == lax.broadcasted_iota(jnp.int32, product.shape, 1) % 8
-    product = jnp.where(diagonal, product, 0.0).astype(BF16)
-    product = product.reshape(ranks, span // 8, 16, product.shape[1])
-    depth = out_ref.shape[3]
-    for beam in range(product.shape[3] // depth):
-        for slot in range(ranks):
-            out_ref[:, beam * ranks + slot] = product[
-                slot, :, :, beam * depth : (beam + 1) * depth
-            ]
+        for first in range(0, lanes * 8, LANES):
+            source = first // 8 // LANES * LANES
+            wide = jnp.take_along_axis(
+                both[:, source : source + LANES],
+                source_lane + (first // 8 - source),
+                axis=1,
+                mode="promise_in_bounds",
+            )
+            wide = jnp.where(diagonal, wide, 0.0).astype(BF16).reshape(per, 16, LANES)
+            lane = first % depth
+            weight_ref[
+                step * per : (step + 1) * per,
+                first // depth * ranks + slot,
+                :,
+                lane : lane + LANES,
+            ] = wide
 
 
 def divisor_up_to(value, limit):
     return max(step for step in range(1, limit + 1) if value % step == 0)
 
 
-def combining_weights(beam_weights, pulse_len, extra, before):
+def weight_tables(beam_weights, pulse_len):
     _, beams, channels, bins = beam_weights.shape
     ranks = lax.axis_size("pulse")
-    me = lax.axis_index("pulse")
     total = bins * ranks
-    rows = bins + TILE
     count = 2 * beams * channels
-    flat = jnp.concatenate([beam_weights.reshape(count, bins), extra])
+    flat = beam_weights.reshape(count, bins)
     parts = [flat] + [
         lax.ppermute(flat, "pulse", [(rank, rank ^ slot) for rank in range(ranks)])
         for slot in range(1, ranks)
     ]
     small = channels * ranks * 2
-    column = np.arange(small)
-    phase = column // 2 % ranks
-    angle = 2.0 * np.pi * (np.outer(np.arange(rows) - HALF, phase) % total) / total
+    phase = np.arange(small) // 2 % ranks
+    angle = 2.0 * np.pi * (np.outer(np.arange(bins + TILE) - HALF, phase) % total) / total
     scale = 1.0 / math.sqrt(total * 2.0 * pulse_len)
     base_cos = np.tile(np.cos(angle) * scale, (1, beams)).astype(np.float32)
     base_sin = np.tile(np.sin(angle) * scale, (1, beams)).astype(np.float32)
-    lanes = beams * small
-    source = np.arange(count)[:, None]
-    target = np.arange(2 * lanes)[None, :]
+    target = np.arange(2 * beams * small)[None, :]
     wanted = target // small * channels + target % small // (2 * ranks)
-    select = (source == wanted).astype(ml_dtypes.bfloat16)
-    spread = (np.arange(lanes * 8)[None, :] // 8 == np.arange(lanes)[:, None]).astype(
-        ml_dtypes.bfloat16
-    )
-    groups = rows // 8
-    per = divisor_up_to(groups, 11)
-    scalar = pl.BlockSpec(memory_space=pltpu.SMEM)
-    table = pl.pallas_call(
-        functools.partial(weights_body, ranks),
-        grid=(groups // per,),
-        out_shape=jax.ShapeDtypeStruct((groups, beams * ranks, 16, small * 8), BF16),
-        in_specs=[scalar]
-        + [pl.BlockSpec((count, bins), lambda i: (0, 0))] * ranks
-        + [
-            pl.BlockSpec((per * 8, lanes), lambda i: (i, 0)),
-            pl.BlockSpec((per * 8, lanes), lambda i: (i, 0)),
-            pl.BlockSpec(select.shape, lambda i: (0, 0)),
-            pl.BlockSpec(spread.shape, lambda i: (0, 0)),
-        ]
-        + [pl.BlockSpec(memory_space=pl.ANY)] * len(before),
-        out_specs=pl.BlockSpec((per, beams * ranks, 16, small * 8), lambda i: (i, 0, 0, 0)),
-        scratch_shapes=[pltpu.VMEM((total + TILE, count), F32)],
-        compiler_params=pltpu.CompilerParams(vmem_limit_bytes=VMEM_LIMIT),
-        cost_estimate=SMALL_COST,
-        name="combining_weights",
-    )(me.reshape(1), *parts, base_cos, base_sin, select, spread, *before)
-    return table, [part[count:] for part in parts]
+    select = (np.arange(count)[:, None] == wanted).astype(ml_dtypes.bfloat16)
+    me = lax.axis_index("pulse").reshape(1)
+    return [me] + parts + [base_cos, base_sin, select]
 
 
 def slot_kinds(ranks):
@@ -158,19 +145,33 @@
     return whole_slots, [slot for slot in range(ranks) if slot not in whole_slots]
 
 
-def partial_beams_body(ranks, beams, edges, echo_ref, table_ref, weight_hbm, *rest):
-    outs, (wide_ref, taken_ref, stage_ref, weight_ref, weight_sem) = rest[:-5], rest[-5:]
+def partial_beams_body(ranks, beams, edges, tables, before, echo_ref, table_ref, *rest):
+    sources, rest = rest[: max(tables, 1)], rest[max(tables, 1) + before :]
+    outs, (wide_ref, taken_ref, stage_ref, weight_ref, weight_sem) = rest[:-7], rest[-7:-2]
+    line_ref, turned_ref = rest[-2:]
     whole_slots, cut_slots = slot_kinds(ranks)
     count = len(whole_slots)
-    outs = outs[-(count + 2 + len(edges)) :]
-    far_ref, edge_refs, flag_ref = outs[count], outs[count + 1 : -1], outs[-1]
+    far_ref, edge_refs, flag_ref = outs[count], outs[count + 1 : count + 1 + len(edges)], outs[count + 1 + len(edges)]
     flag_ref[...] = jnp.ones(flag_ref.shape, F32)
     _, channels, pulses, width = echo_ref.shape
     depth = pulses // ranks
     groups = table_ref.shape[0] // 16
     columns = width // LANES
-    fetch = pltpu.make_async_copy(weight_hbm, weight_ref, weight_sem)
-    fetch.start()
+    turns = channels // 2
+    if tables:
+        me = sources[0][0]
+        bins = sources[1].shape[1]
+        gather_lines(me, sources[1 : 1 + ranks], line_ref)
+        turn_tables(ranks, me, *sources[1 + ranks : 3 + ranks], turned_ref)
+
+        def weights_of(slot):
+            fill_weights(ranks, bins, slot, me, line_ref, turned_ref, sources[-1], weight_ref)
+
+        if ranks % turns:
+            lax.fori_loop(0, ranks, lambda slot, carry: (weights_of(slot), carry)[1], 0)
+    else:
+        fetch = pltpu.make_async_copy(sources[0], weight_ref, weight_sem)
+        fetch.start()
 
     def deinterleave(channel, side):
         for part in range(2):
@@ -203,10 +204,17 @@
         transform(first, 0)
         deinterleave(lax.min(first + 2, channels - 1), 0)
         transform(first + 1, 1)
+        if tables and ranks % turns == 0:
+            for within in range(ranks // turns):
+                weights_of(step * (ranks // turns) + within)
         return carry
 
-    lax.fori_loop(0, channels // 2, two_channels, 0)
-    fetch.wait()
+    lax.fori_loop(0, turns, two_channels, 0)
+    if tables:
+        keep = pltpu.make_async_copy(weight_ref, outs[-1], weight_sem)
+        keep.start()
+    else:
+        fetch.wait()
 
     _, pairs, _, inner = weight_ref.shape
     lines = pairs * 2
@@ -243,47 +251,59 @@
         return carry
 
     lax.fori_loop(0, steps // per, combine, 0)
-
-
-def partial_beams(echoes, table, weights, chunk, width, edges, before=()):
+    if tables:
+        keep.wait()
+
+
+def partial_beams(echoes, table, sources, beams, chunk, width, edges, before=()):
     _, channels, pulses, _ = echoes.shape
     ranks = lax.axis_size("pulse")
-    beams = weights.shape[1] // ranks
-    rows = weights.shape[0] * 8
     groups = table.shape[0] // 16
+    rows = groups * 8 + TILE
     whole_slots, cut_slots = slot_kinds(ranks)
     far = len(cut_slots) * beams
     tiles = width // LANES
+    tables = len(sources) if len(sources) > 1 else 0
+    weights = jax.ShapeDtypeStruct((rows // 8, beams * ranks, 16, channels * ranks * 16), BF16)
     outs = [jax.ShapeDtypeStruct((beams, tiles, rows, 2 * LANES), BF16)] * len(whole_slots)
     outs += [jax.ShapeDtypeStruct((far, tiles, rows, 2 * LANES), BF16)]
     outs += [jax.ShapeDtypeStruct((far, 1, rows, 2 * LANES), BF16)] * len(edges)
     outs += [jax.ShapeDtypeStruct((8, LANES), F32)]
     whole = pl.BlockSpec(memory_space=pltpu.VMEM)
     anywhere = pl.BlockSpec(memory_space=pl.ANY)
+    if tables:
+        source_specs = [pl.BlockSpec(memory_space=pltpu.SMEM)] + [
+            pl.BlockSpec(item.shape, lambda i: (0, 0)) for item in sources[1:]
+        ]
+    else:
+        source_specs = [anywhere]
     result = pl.pallas_call(
-        functools.partial(partial_beams_body, ranks, beams, edges),
+        functools.partial(partial_beams_body, ranks, beams, edges, tables, len(before)),
         grid=(1,),
-        out_shape=outs,
+        out_shape=outs + ([weights] if tables else []),
         in_specs=[
             pl.BlockSpec((2, channels, pulses, width), lambda i: (0, 0, 0, chunk)),
-            whole,
-            anywhere,
+            pl.BlockSpec(table.shape, lambda i: (0, 0)),
         ]
+        + source_specs
         + [anywhere] * len(before),
-        out_specs=[whole] * len(outs),
+        out_specs=[whole] * len(outs) + ([anywhere] if tables else []),
         scratch_shapes=[
             pltpu.VMEM((2, 2, width // LANES, pulses, LANES), F32),
             pltpu.VMEM((2, ranks, 2 * pulses // ranks, width), BF16),
             pltpu.VMEM((groups, channels * ranks, 16, width), BF16),
             pltpu.VMEM(weights.shape, BF16),
             pltpu.SemaphoreType.DMA,
+            pltpu.VMEM((ranks * groups * 8 + TILE, 2 * beams * channels), F32),
+            pltpu.VMEM((2, rows, beams * channels * ranks * 2), F32),
         ],
         compiler_params=pltpu.CompilerParams(vmem_limit_bytes=VMEM_LIMIT),
         cost_estimate=SMALL_COST,
         name="partial_beams",
-    )(echoes, table, weights, *before)
+    )(echoes, table, *sources, *before)
     count = len(whole_slots)
-    return result[:count], result[count], result[count + 1 : -1], result[-1]
+    flag = count + 1 + len(edges)
+    return result[:count], result[count], result[count + 1 : flag], result[flag], result[flag + 1 :]
 
 
 def summed_body(terms, edges, *refs):
@@ -314,7 +334,7 @@
     )(*terms, *before)
 
 
-def toeplitz_body(replica_ref, before_ref, out_ref):
+def toeplitz_body(replica_ref, out_ref):
     chirp = replica_ref.shape[1]
     span = chirp + LANES
     padded = jnp.concatenate(
@@ -336,18 +356,17 @@
             out_ref[first : first + LANES, :] = columns[tile * LANES : (tile + 1) * LANES]
 
 
-def toeplitz_taps(replica, before):
+def toeplitz_taps(replica):
     return pl.pallas_call(
         toeplitz_body,
         out_shape=jax.ShapeDtypeStruct((2 * (replica.shape[1] + LANES), 2 * LANES), BF16),
-        in_specs=[pl.BlockSpec(memory_space=pltpu.VMEM), pl.BlockSpec(memory_space=pl.ANY)],
         cost_estimate=SMALL_COST,
         name="toeplitz_taps",
-    )(replica, before)
-
-
-def tiles_body(tracks, place_ref, flag_ref, taps_ref, repeat_ref, gather_ref, *rest):
-    pieces, (out_ref, line_ref, cut_ref) = rest[:-3], rest[-3:]
+    )(replica)
+
+
+def tiles_body(tracks, count, place_ref, flag_ref, taps_ref, repeat_ref, gather_ref, *rest):
+    pieces, (out_ref, line_ref, cut_ref) = rest[:count], rest[-3:]
     entry = pl.program_id(0)
     rows = pieces[0].shape[2]
     span = taps_ref.shape[0] // (2 * LANES)
@@ -459,7 +478,7 @@
     gather = np.arange(group // 8)[:, None] == np.arange(group)[None, :] // 8
     gather = gather.astype(ml_dtypes.bfloat16)
     return pl.pallas_call(
-        functools.partial(tiles_body, tracks),
+        functools.partial(tiles_body, tracks, len(pieces)),
         grid=(entries,),
         out_shape=jax.ShapeDtypeStruct((entries, tracks * 2, group), BF16),
         in_specs=[
@@ -539,22 +558,23 @@
     edges = [[], [last_tile]]
     edges[spare_chunk] = [0] + edges[spare_chunk]
 
-    extra = jnp.pad(place.astype(F32), ((0, 6), (0, bins - place.shape[1])))
     rows = bins + TILE
-    track_count = place.shape[1]
-    place = cut_places(place[0], place[1], rows)[:, None]
-    weights, extras = combining_weights(beam_weights, chirp, extra, [place])
-    far_places = [extras[slot][:2, :track_count].astype(jnp.int32) for slot in cut_slots]
+    place = cut_places(place[0], place[1], rows)
+    far_places = [exchanged(place, slot) for slot in cut_slots]
+    place = place[:, None]
+    sources = weight_tables(beam_weights, chirp)
     far_places = jnp.stack(
-        [cut_places(item[0], item[1], rows) for item in far_places for _ in range(beams)], axis=1
+        [item for item in far_places for _ in range(beams)], axis=1
     )
-    first_blocks, far, far_edges, flag = partial_beams(echoes, table, weights, 0, width, edges[0])
+    taps = toeplitz_taps(replica)
+    first_blocks, far, far_edges, flag, weights = partial_beams(
+        echoes, table, sources, beams, 0, width, edges[0], before=[taps, far_places]
+    )
     fars, ends = [far], [far_edges]
     flag = passed_along(flag, "gate", 1)
-    second_blocks, far, far_edges, ones = partial_beams(
-        echoes, table, weights, 1, width, edges[1], before=[flag, far_places]
+    second_blocks, far, far_edges, _, _ = partial_beams(
+        echoes, table, weights, beams, 1, width, edges[1], before=[flag]
     )
-    taps = toeplitz_taps(replica, ones)
     fars, ends = fars + [far], ends + [far_edges]
 
     def with_halo(full, spare, left):
@@ -569,14 +589,12 @@
 
     first = summed_block(neighbours(first_blocks), edges[0])
     far_pieces = with_halo(fars, ends[spare_chunk][0], ends[1][-1])
-    far_tiles = beam_tiles(
-        taps, [(piece, 0) for piece in far_pieces], far_places, flag, gate_len
-    )
+    far_tiles = beam_tiles(taps, [(piece, 0) for piece in far_pieces], far_places, flag, gate_len)
+    second = summed_block(neighbours(second_blocks), edges[1], before=[far_tiles])
     arrived = [
         exchanged(far_tiles[kind * beams : (kind + 1) * beams], slot)
         for kind, slot in enumerate(cut_slots)
     ]
-    second = summed_block(neighbours(second_blocks), edges[1], before=[far_tiles])
     own_pieces = with_halo([first[0], second[0]], [first, second][spare_chunk][1], second[-1])
     results = []
     for beam in range(beams):

time: 164 us -> 160 us (0.976)
  other arithmetic: 4.26 us -> 2.05 us
  Pallas kernels: 80.1 us -> 78.4 us
    ppermute x5 -> x6, starting transfers between devices: 6.05 us -> 9.58 us  [exchanged(): lax.ppermute(value, 'pulse', [(rank, rank ^ slot) for rank in range(ranks)])]
    ppermute x3, waiting for transfers between devices: 3.7 us -> 0.6 us  [weight_tables(): lax.ppermute(flat, 'pulse', [(rank, rank ^ slot) for rank in range(ranks)])]
    ppermute x5 -> x6, waiting for transfers between devices: 1.81 us -> 3.87 us  [exchanged(): lax.ppermute(value, 'pulse', [(rank, rank ^ slot) for rank in range(ranks)])]
    ppermute x7, starting transfers between devices: 18.3 us -> 16.3 us  [passed_along(): lax.ppermute(value, axis, [(source, source + steps) for source in range(l...]
    pallas_call x6 -> x5, Pallas kernels: 65.3 us -> 63.6 us  [the longest x2 35.4 us: partial_beams(): pl.pallas_call(functools.partial(partial_beams_body, ranks, beams, edges,...]
  transfers between devices with their start and end apart: 16 -> 17, of which waited for: 5 -> 7; matrix products, arithmetic and copies ran while one was open for 2% -> 2% of each run, Pallas kernels for 33% -> 33%
where the time goes in v2:
time: 160 us; the launch traced here: 159 us
  Pallas kernels  78.4 us (49%)
  starting transfers between devices  39.5 us (25%)
  blocking collectives  21.8 us (14%)
  waiting for transfers between devices  14.6 us (9%)
  local copies, waits for them, and re-layouts  2.82 us (2%)
  other arithmetic  2.05 us (1%)
    pallas_call x2, Pallas kernels, partial_beams(): pl.pallas_call(functools.partial(partial_beams_body, ranks, beams, edges,...  35.4 us
    pallas_call x3, Pallas kernels, beam_tiles(): pl.pallas_call(functools.partial(tiles_body, tracks, len(pieces)), grid=(...  28.2 us
    all_to_all x1, blocking collectives, local(): lax.all_to_all(tiles.reshape(owners, capacity * 2, 2 * LANES), ('pulse',...  21.8 us
    ppermute x7, starting transfers between devices, passed_along(): lax.ppermute(value, axis, [(source, source + steps) for source in range(l...  16.3 us
    all_to_all x1, starting transfers between devices, local(): lax.all_to_all(tiles.reshape(owners, capacity * 2, 2 * LANES), ('pulse',...  10.1 us
    ppermute x6, starting transfers between devices, exchanged(): lax.ppermute(value, 'pulse', [(rank, rank ^ slot) for rank in range(ranks)])  9.58 us
    all_to_all x1, waiting for transfers between devices, local(): lax.all_to_all(tiles.reshape(owners, capacity * 2, 2 * LANES), ('pulse',...  9.06 us
    pallas_call x2, Pallas kernels, summed_block(): pl.pallas_call(functools.partial(summed_body, len(terms), edges), grid=(b...  5.84 us
  transfers between devices with their start and end apart: 17, of which 7 were waited for; matrix products, arithmetic and copies ran while one was open for 2% of the time, Pallas kernels for 33%

profile of v2, /device:TPU:0, one launch (start us, length us, event | category | flops | bytes accessed | tf_op | source)
XLA Modules:
  0.0 159.3 jit_solution(12815778505745210704)
XLA Ops:
  0.0 0.7 fusion.3
  0.8 4.0 %collective-permute-start.3 = (s32[3,256]{1,0:T(4,128)S(1)}, s32[3,256]{1,0:T(4,128)S(1)}, u32[]{:S(2)}, u32[]{:S(2)}) collective-permute-start(s32[3,256]{1,0:T(4,128)S(1)} %pad_add_fusion.1), channel_id=1, source_target_pairs={{0,24},{8,16},{16,8},{24,0},{1,25},{9,17},{17,9},{25,1},{2,26},{10... | collective-permute-start | bytes 9224 | tf_op jit(solution)/shard_map/ppermute | solution.py:550
  4.7 0.1 collective-permute-start.2
  4.8 1.9 %collective-permute-start.1 = (f32[32,512]{1,0:T(8,128)}, f32[32,512]{1,0:T(8,128)S(1)}, u32[]{:S(2)}, u32[]{:S(2)}) collective-permute-start(f32[32,512]{1,0:T(8,128)} %bitcast.31), channel_id=1, source_target_pairs={{0,16},{8,24},{16,0},{24,8},{1,17},{9,25},{17,1},{25,9},{2,18},{10... | collective-permute-start | bytes 196616 | tf_op jit(solution)/shard_map/ppermute | solution.py:127
  6.7 1.5 collective-permute-start
  8.2 1.8 %toeplitz_taps.1.rest_8_.taps_ref = bf16[768,256]{1,0:T(8,128)(2,1)} custom-call(bf16[2,256]{1,0:T(2,128)(2,1)} %replica_ref.1), custom_call_target="tpu_custom_call" | custom-call | flops 1048576 | bytes 65536 | tf_op jit(solution)/shard_map/toeplitz_taps/pallas_call | solution.py:360
  10.0 0.6 copy.20.rest_9_.place_ref
  10.6 0.6 collective-permute-done.rest_2_
  11.2 0.0 copy-done.2
  11.2 0.0 copy-done.3
  11.2 0.6 copy-done.4
  11.8 20.7 %partial_beams.2 = (bf16[2,2,528,256]{3,2,1,0:T(8,128)(2,1)}, bf16[2,2,528,256]{3,2,1,0:T(8,128)(2,1)}, bf16[2,2,528,256]{3,2,1,0:T(8,128)(2,1)}, bf16[2,2,528,2...) custom-call(bf16[2,8,512,512]{3,2,1,0:T(8,128)(2,1)} %echo_ref.3, ...), custom_call_target="tpu_custom_call" | custom-call | flops 1048576 | bytes 65536 | tf_op jit(solution)/shard_map/partial_beams/pallas_call | solution.py:280
  32.5 1.6 collective-permute-start.11
  34.1 0.5 collective-permute-start.12
  34.6 1.3 collective-permute-start.4
  35.8 1.3 collective-permute-start.8
  37.2 0.6 copy-done.5
  37.7 14.7 %partial_beams.3 = (bf16[2,2,528,256]{3,2,1,0:T(8,128)(2,1)}, bf16[2,2,528,256]{3,2,1,0:T(8,128)(2,1)}, bf16[2,2,528,256]{3,2,1,0:T(8,128)(2,1)}, bf16[2,2,528,2...) custom-call(bf16[2,8,512,512]{3,2,1,0:T(8,128)(2,1)} %echo_ref.3, ...), custom_call_target="tpu_custom_call" | custom-call | flops 1048576 | bytes 65536 | tf_op jit(solution)/shard_map/partial_beams/pallas_call | solution.py:280
  52.4 0.5 collective-permute-start.5
  52.9 1.6 %collective-permute-start.6 = (bf16[2,2,528,256]{3,2,1,0:T(8,128)(2,1)}, bf16[2,2,528,256]{3,2,1,0:T(8,128)(2,1)}, u32[]{:S(2)}, u32[]{:S(2)}) collective-permute-start(bf16[2,2,528,256]{3,2,1,0:T(8,128)(2,1)} %get-tuple-element.24), channel_id=1, source_target_pairs={{0,16},{8,24},{16,0},{24,8},{1,17},{9,25},{17,1},{25,9},{2,18},{10... | collective-permute-start | bytes 3244040 | tf_op jit(solution)/shard_map/ppermute | solution.py:550
  54.6 2.8 %collective-permute-done.11.refs_1_ = bf16[2,2,528,256]{3,2,1,0:T(8,128)(2,1)} collective-permute-done((bf16[2,2,528,256]{3,2,1,0:T(8,128)(2,1)}, bf16[2,2,528,256]{3,2,1,0:T(8,128)(2,1)}, u32[]{:S(2)}, u32[]{:S(2)}) %collective-permute-start.11) | collective-permute-done | bytes 1081376 | tf_op jit(solution)/shard_map/ppermute | solution.py:550
  57.4 1.5 collective-permute-start.7
  58.9 1.3 collective-permute-start.9
  60.2 2.9 %summed_block.3.rest_1_ = bf16[2,2,528,256]{3,2,1,0:T(8,128)(2,1)} custom-call(bf16[2,2,528,256]{3,2,1,0:T(8,128)(2,1)} %get-tuple-element.30.refs_0_, bf16[2,2,528,256]{3,2,1,0:T(8,128)(2,1)} %collective-permute-done.11.refs_1_, bf16[2,2,528,256]{3,2,1,0:T(8,128)(2,1)} %collective-permute-done.12.refs_2_), custom_call_target="tpu_custom_call" | custom-call | flops 1048576 | bytes 65536 | tf_op jit(solution)/shard_map/summed_block/pallas_call | solution.py:324
  63.1 1.3 collective-permute-start.13
  64.4 0.5 collective-permute-done.9.rest_4_
  64.8 13.2 %beam_tiles.3.refs_3_ = bf16[2,512,256]{2,1,0:T(8,128)(2,1)} custom-call(s32[3,2,256]{2,1,0:T(2,128)} %copy.20.rest_9_.place_ref, f32[8,128]{1,0:T(8,128)} %copy-done.5, bf16[768,256]{1,0:T(8,128)(2,1)} %toeplitz_taps.1.rest_8_.taps_ref, bf16[128,256]{1,0:T(8,128)(2,1)} %constant.93.clone.repeat_ref, bf16[32,256]{1,0:T(8,128)(2,1)} %constant.92.clone.rest_7_.gather_ref, ...), custom_call_target="tpu_custom_call" | custom-call | flops 1048576 | bytes 65536 | tf_op jit(solution)/shard_map/beam_tiles/pallas_call | solution.py:480
  78.0 1.4 collective-permute-start.15
  79.4 0.1 collective-permute-done.5.refs_1_
  79.6 0.9 collective-permute-done.6.refs_2_
  80.5 3.0 %summed_block.2 = (bf16[2,2,528,256]{3,2,1,0:T(8,128)(2,1)}, bf16[2,1,528,256]{3,2,1,0:T(8,128)(2,1)}, bf16[2,1,528,256]{3,2,1,0:T(8,128)(2,1)}) custom-call(bf16[2,2,528,256]{3,2,1,0:T(8,128)(2,1)} %get-tuple-element.22.refs_0_, bf16[2,2,528,256]{3,2,1,0:T(8,128)(2,1)} %collective-permute-done.5.refs_1_, ...), custom_call_target="tpu_custom_call" | custom-call | flops 1048576 | bytes 65536 | tf_op jit(solution)/shard_map/summed_block/pallas_call | solution.py:324
  83.4 8.2 %collective-permute-start.10 = (bf16[2,1,528,256]{3,2,1,0:T(8,128)(2,1)}, bf16[2,1,528,256]{3,2,1,0:T(8,128)(2,1)S(1)}, u32[]{:S(2)}, u32[]{:S(2)}) collective-permute-start(bf16[2,1,528,256]{3,2,1,0:T(8,128)(2,1)} %get-tuple-element.29), channel_id=1, source_target_pairs={{0,1},{1,2},{2,3},{3,4},{4,5},{5,6},{6,7},{8,9},{9,10},{10,11},{11... | collective-permute-start | bytes 1622024 | tf_op jit(solution)/shard_map/ppermute | solution.py:25
  91.7 1.5 collective-permute-start.14
  93.2 0.6 broadcast_in_dim.2.place_ref
  93.8 0.6 reduce-window.6
  94.4 0.2 slice_reduce_fusion
  94.6 0.1 fusion.1
  94.7 0.6 add_add_fusion.slot_ref
  95.3 0.6 collective-permute-done.14.rest_4_
  95.9 0.2 copy-done
  96.1 7.5 %beam_tiles.4.rest_0_ = bf16[1,512,256]{2,1,0:T(8,128)(2,1)} custom-call(s32[3,1,256]{2,1,0:T(1,128)} %broadcast_in_dim.2.place_ref, f32[8,128]{1,0:T(8,128)} %copy-done.5, bf16[768,256]{1,0:T(8,128)(2,1)} %toeplitz_taps.1.rest_8_.taps_ref, bf16[128,256]{1,0:T(8,128)(2,1)} %constant.93.clone.repeat_ref, bf16[32,256]{1,0:T(8,128)(2,1)} %constant.92.clone.rest_7_.gather_ref, ...), custom_call_target="tpu_custom_call" | custom-call | flops 1048576 | bytes 65536 | tf_op jit(solution)/shard_map/beam_tiles/pallas_call | solution.py:480
  103.7 2.6 %slotted_tiles.2 = bf16[1280,256]{1,0:T(8,128)(2,1)} custom-call(s32[256]{0:T(256)} %add_add_fusion.slot_ref, bf16[1,512,256]{2,1,0:T(8,128)(2,1)} %beam_tiles.4.rest_0_, bf16[2,512,256]{2,1,0:T(8,128)(2,1)} %collective-permute-done.15.rest_1_), custom_call_target="tpu_custom_call" | custom-call | flops 1048576 | bytes 65536 | tf_op jit(solution)/shard_map/slotted_tiles/pallas_call | solution.py:443
  106.3 10.1 %all-to-all-start = ((bf16[32,40,256]{2,1,0:T(8,128)(2,1)}), bf16[32,40,256]{2,1,0:T(8,128)(2,1)S(1)}, u32[]{:S(2)}, u32[]{:S(2)}) async-start(bf16[32,40,256]{2,1,0:T(8,128)(2,1)} %bitcast.28), calls=%async_computation | async-start | bytes 1310720 | tf_op jit(solution)/shard_map/all_to_all | solution.py:607
  116.4 7.5 %beam_tiles.5.rest_0_ = bf16[1,512,256]{2,1,0:T(8,128)(2,1)} custom-call(s32[3,1,256]{2,1,0:T(1,128)} %broadcast_in_dim.2.place_ref, f32[8,128]{1,0:T(8,128)} %copy-done.5, bf16[768,256]{1,0:T(8,128)(2,1)} %toeplitz_taps.1.rest_8_.taps_ref, bf16[128,256]{1,0:T(8,128)(2,1)} %constant.93.clone.repeat_ref, bf16[32,256]{1,0:T(8,128)(2,1)} %constant.92.clone.rest_7_.gather_ref, ...), custom_call_target="tpu_custom_call" | custom-call | flops 1048576 | bytes 65536 | tf_op jit(solution)/shard_map/beam_tiles/pallas_call | solution.py:480
  123.9 2.6 %slotted_tiles.3 = bf16[1280,256]{1,0:T(8,128)(2,1)} custom-call(s32[256]{0:T(256)} %add_add_fusion.slot_ref, bf16[1,512,256]{2,1,0:T(8,128)(2,1)} %beam_tiles.5.rest_0_, bf16[2,512,256]{2,1,0:T(8,128)(2,1)} %collective-permute-done.15.rest_1_), custom_call_target="tpu_custom_call" | custom-call | flops 1048576 | bytes 65536 | tf_op jit(solution)/shard_map/slotted_tiles/pallas_call | solution.py:443
  126.5 9.1 %all-to-all-done = bf16[32,40,256]{2,1,0:T(8,128)(2,1)S(1)} async-done(((bf16[32,40,256]{2,1,0:T(8,128)(2,1)}), bf16[32,40,256]{2,1,0:T(8,128)(2,1)S(1)}, u32[]{:S(2)}, u32[]{:S(2)}) %all-to-all-start) | async-done | bytes 655392 | tf_op jit(solution)/shard_map/all_to_all | solution.py:607
  135.5 21.8 %all_to_all.10 = bf16[32,40,256]{2,1,0:T(8,128)(2,1)S(1)} all-to-all(bf16[32,40,256]{2,1,0:T(8,128)(2,1)} %bitcast.29), channel_id=1, replica_groups=mesh['pulse'=4,'gate'=8] {'pulse','gate'}, dimensions={0} | all-to-all | bytes 1310720 | tf_op jit(solution)/shard_map/all_to_all | solution.py:607
  157.3 2.0 %finished_tiles.1 = f32[640,1024]{1,0:T(8,128)} custom-call(bf16[1280,256]{1,0:T(8,128)(2,1)S(1)} %bitcast.26, bf16[1280,256]{1,0:T(8,128)(2,1)S(1)} %bitcast.27), custom_call_target="tpu_custom_call" | custom-call | flops 1048576 | bytes 65536 | tf_op jit(solution)/shard_map/finished_tiles/pallas_call | solution.py:519
  (25 shorter events, 0.1 us)
Async XLA Ops:
  0.8 9.2 %collective-permute-start.3 = (s32[3,256]{1,0:T(4,128)S(1)}, s32[3,256]{1,0:T(4,128)S(1)}, u32[]{:S(2)}, u32[]{:S(2)}) collective-permute-start(s32[3,256]{1,0:T(4,128)S(1)} %pad_add_fusion.1), channel_id=1, source_target_pairs={{0,24},{8,16},{16,8},{24,0},{1,25},{9,17},{17,9},{25,1},{2,26},{10... | collective-permute-start | bytes 9224 | tf_op jit(solution)/shard_map/ppermute | solution.py:550
  4.7 5.9 %collective-permute-start.2 = (f32[32,512]{1,0:T(8,128)}, f32[32,512]{1,0:T(8,128)S(1)}, u32[]{:S(2)}, u32[]{:S(2)}) collective-permute-start(f32[32,512]{1,0:T(8,128)} %bitcast.30), channel_id=1, source_target_pairs={{0,24},{8,16},{16,8},{24,0},{1,25},{9,17},{17,9},{25,1},{2,26},{10... | collective-permute-start | bytes 196616 | tf_op jit(solution)/shard_map/ppermute | solution.py:127
  4.8 5.8 %collective-permute-start.1 = (f32[32,512]{1,0:T(8,128)}, f32[32,512]{1,0:T(8,128)S(1)}, u32[]{:S(2)}, u32[]{:S(2)}) collective-permute-start(f32[32,512]{1,0:T(8,128)} %bitcast.31), channel_id=1, source_target_pairs={{0,16},{8,24},{16,0},{24,8},{1,17},{9,25},{17,1},{25,9},{2,18},{10... | collective-permute-start | bytes 196616 | tf_op jit(solution)/shard_map/ppermute | solution.py:127
  6.7 4.5 %collective-permute-start = (f32[32,512]{1,0:T(8,128)}, f32[32,512]{1,0:T(8,128)S(1)}, u32[]{:S(2)}, u32[]{:S(2)}) collective-permute-start(f32[32,512]{1,0:T(8,128)} %bitcast.32), channel_id=1, source_target_pairs={{0,8},{8,0},{16,24},{24,16},{1,9},{9,1},{17,25},{25,17},{2,10},{10... | collective-permute-start | bytes 196616 | tf_op jit(solution)/shard_map/ppermute | solution.py:127
  10.6 0.6 copy-start.2
  10.6 0.6 copy-start.3
  11.2 0.6 copy-start.4
  32.5 24.9 %collective-permute-start.11 = (bf16[2,2,528,256]{3,2,1,0:T(8,128)(2,1)}, bf16[2,2,528,256]{3,2,1,0:T(8,128)(2,1)}, u32[]{:S(2)}, u32[]{:S(2)}) collective-permute-start(bf16[2,2,528,256]{3,2,1,0:T(8,128)(2,1)} %get-tuple-element.31), channel_id=1, source_target_pairs={{0,8},{8,0},{16,24},{24,16},{1,9},{9,1},{17,25},{25,17},{2,10},{10... | collective-permute-start | bytes 3244040 | tf_op jit(solution)/shard_map/ppermute | solution.py:550
  34.1 24.8 %collective-permute-start.12 = (bf16[2,2,528,256]{3,2,1,0:T(8,128)(2,1)}, bf16[2,2,528,256]{3,2,1,0:T(8,128)(2,1)}, u32[]{:S(2)}, u32[]{:S(2)}) collective-permute-start(bf16[2,2,528,256]{3,2,1,0:T(8,128)(2,1)} %get-tuple-element.32), channel_id=1, source_target_pairs={{0,16},{8,24},{16,0},{24,8},{1,17},{9,25},{17,1},{25,9},{2,18},{10... | collective-permute-start | bytes 3244040 | tf_op jit(solution)/shard_map/ppermute | solution.py:550
  34.6 2.6 %collective-permute-start.4 = (f32[8,128]{1,0:T(8,128)}, f32[8,128]{1,0:T(8,128)S(1)}, u32[]{:S(2)}, u32[]{:S(2)}) collective-permute-start(f32[8,128]{1,0:T(8,128)} %get-tuple-element.20), channel_id=1, source_target_pairs={{0,1},{1,2},{2,3},{3,4},{4,5},{5,6},{6,7},{8,9},{9,10},{10,11},{11... | collective-permute-start | bytes 12296 | tf_op jit(solution)/shard_map/ppermute | solution.py:25
  35.8 29.0 %collective-permute-start.8 = (bf16[2,2,528,256]{3,2,1,0:T(8,128)(2,1)}, bf16[2,2,528,256]{3,2,1,0:T(8,128)(2,1)}, u32[]{:S(2)}, u32[]{:S(2)}) collective-permute-start(bf16[2,2,528,256]{3,2,1,0:T(8,128)(2,1)} %get-tuple-element.26.rest_1_), channel_id=1, source_target_pairs={{1,0},{2,1},{3,2},{4,3},{5,4},{6,5},{7,6},{9,8},{10,9},{11,10},{12... | collective-permute-start | bytes 3244040 | tf_op jit(solution)/shard_map/ppermute | solution.py:25
  37.2 0.6 copy-start.5
  52.4 27.1 %collective-permute-start.5 = (bf16[2,2,528,256]{3,2,1,0:T(8,128)(2,1)}, bf16[2,2,528,256]{3,2,1,0:T(8,128)(2,1)}, u32[]{:S(2)}, u32[]{:S(2)}) collective-permute-start(bf16[2,2,528,256]{3,2,1,0:T(8,128)(2,1)} %get-tuple-element.23), channel_id=1, source_target_pairs={{0,8},{8,0},{16,24},{24,16},{1,9},{9,1},{17,25},{25,17},{2,10},{10... | collective-permute-start | bytes 3244040 | tf_op jit(solution)/shard_map/ppermute | solution.py:550
  52.9 27.5 %collective-permute-start.6 = (bf16[2,2,528,256]{3,2,1,0:T(8,128)(2,1)}, bf16[2,2,528,256]{3,2,1,0:T(8,128)(2,1)}, u32[]{:S(2)}, u32[]{:S(2)}) collective-permute-start(bf16[2,2,528,256]{3,2,1,0:T(8,128)(2,1)} %get-tuple-element.24), channel_id=1, source_target_pairs={{0,16},{8,24},{16,0},{24,8},{1,17},{9,25},{17,1},{25,9},{2,18},{10... | collective-permute-start | bytes 3244040 | tf_op jit(solution)/shard_map/ppermute | solution.py:550
  57.4 5.7 %collective-permute-start.7 = (bf16[2,1,528,256]{3,2,1,0:T(8,128)(2,1)}, bf16[2,1,528,256]{3,2,1,0:T(8,128)(2,1)S(1)}, u32[]{:S(2)}, u32[]{:S(2)}) collective-permute-start(bf16[2,1,528,256]{3,2,1,0:T(8,128)(2,1)} %get-tuple-element.25), channel_id=1, source_target_pairs={{0,1},{1,2},{2,3},{3,4},{4,5},{5,6},{6,7},{8,9},{9,10},{10,11},{11... | collective-permute-start | bytes 1622024 | tf_op jit(solution)/shard_map/ppermute | solution.py:25
  58.9 5.9 %collective-permute-start.9 = (bf16[2,1,528,256]{3,2,1,0:T(8,128)(2,1)}, bf16[2,1,528,256]{3,2,1,0:T(8,128)(2,1)}, u32[]{:S(2)}, u32[]{:S(2)}) collective-permute-start(bf16[2,1,528,256]{3,2,1,0:T(8,128)(2,1)} %get-tuple-element.28), channel_id=1, source_target_pairs={{1,0},{2,1},{3,2},{4,3},{5,4},{6,5},{7,6},{9,8},{10,9},{11,10},{12... | collective-permute-start | bytes 1622024 | tf_op jit(solution)/shard_map/ppermute | solution.py:25
  63.1 1.8 %copy-start.1 = (bf16[2,1,528,256]{3,2,1,0:T(8,128)(2,1)}, bf16[2,1,528,256]{3,2,1,0:T(8,128)(2,1)S(1)}, u32[]{:S(2)}) copy-start(bf16[2,1,528,256]{3,2,1,0:T(8,128)(2,1)S(1)} %collective-permute-done.7.rest_0_) | copy-start | bytes 1622020
  63.1 32.8 %collective-permute-start.13 = (bf16[2,2,528,256]{3,2,1,0:T(8,128)(2,1)}, bf16[2,2,528,256]{3,2,1,0:T(8,128)(2,1)}, u32[]{:S(2)}, u32[]{:S(2)}) collective-permute-start(bf16[2,2,528,256]{3,2,1,0:T(8,128)(2,1)} %summed_block.3.rest_1_), channel_id=1, source_target_pairs={{1,0},{2,1},{3,2},{4,3},{5,4},{6,5},{7,6},{9,8},{10,9},{11,10},{12... | collective-permute-start | bytes 3244040 | tf_op jit(solution)/shard_map/ppermute | solution.py:25
  78.0 25.6 %collective-permute-start.15 = (bf16[2,512,256]{2,1,0:T(8,128)(2,1)}, bf16[2,512,256]{2,1,0:T(8,128)(2,1)}, u32[]{:S(2)}, u32[]{:S(2)}) collective-permute-start(bf16[2,512,256]{2,1,0:T(8,128)(2,1)} %beam_tiles.3.refs_3_), channel_id=1, source_target_pairs={{0,24},{8,16},{16,8},{24,0},{1,25},{9,17},{17,9},{25,1},{2,26},{10... | collective-permute-start | bytes 1572872 | tf_op jit(solution)/shard_map/ppermute | solution.py:550
  80.5 12.7 %copy-start.6 = (s32[256]{0:T(256)S(1)}, s32[256]{0:T(256)}, u32[]{:S(2)}) copy-start(s32[256]{0:T(256)} %param.21) | copy-start | bytes 3076
  83.4 11.9 %collective-permute-start.10 = (bf16[2,1,528,256]{3,2,1,0:T(8,128)(2,1)}, bf16[2,1,528,256]{3,2,1,0:T(8,128)(2,1)S(1)}, u32[]{:S(2)}, u32[]{:S(2)}) collective-permute-start(bf16[2,1,528,256]{3,2,1,0:T(8,128)(2,1)} %get-tuple-element.29), channel_id=1, source_target_pairs={{0,1},{1,2},{2,3},{3,4},{4,5},{5,6},{6,7},{8,9},{9,10},{10,11},{11... | collective-permute-start | bytes 1622024 | tf_op jit(solution)/shard_map/ppermute | solution.py:25
  91.7 4.2 %collective-permute-start.14 = (bf16[2,1,528,256]{3,2,1,0:T(8,128)(2,1)}, bf16[2,1,528,256]{3,2,1,0:T(8,128)(2,1)}, u32[]{:S(2)}, u32[]{:S(2)}) collective-permute-start(bf16[2,1,528,256]{3,2,1,0:T(8,128)(2,1)} %get-tuple-element.34), channel_id=1, source_target_pairs={{1,0},{2,1},{3,2},{4,3},{5,4},{6,5},{7,6},{9,8},{10,9},{11,10},{12... | collective-permute-start | bytes 1622024 | tf_op jit(solution)/shard_map/ppermute | solution.py:25
  95.3 0.8 copy-start
  106.3 29.3 %all-to-all-start = ((bf16[32,40,256]{2,1,0:T(8,128)(2,1)}), bf16[32,40,256]{2,1,0:T(8,128)(2,1)S(1)}, u32[]{:S(2)}, u32[]{:S(2)}) async-start(bf16[32,40,256]{2,1,0:T(8,128)(2,1)} %bitcast.28), calls=%async_computation | async-start | bytes 1310720 | tf_op jit(solution)/shard_map/all_to_all | solution.py:607

commit v3 on v2

--- a/solution.py
+++ b/solution.py
@@ -334,7 +334,7 @@
     )(*terms, *before)
 
 
-def toeplitz_body(replica_ref, out_ref):
+def toeplitz_body(replica_ref, through_ref, out_ref, through_out):
     chirp = replica_ref.shape[1]
     span = chirp + LANES
     padded = jnp.concatenate(
@@ -356,13 +356,20 @@
             out_ref[first : first + LANES, :] = columns[tile * LANES : (tile + 1) * LANES]
 
 
-def toeplitz_taps(replica):
+def toeplitz_taps(replica, through):
+    anywhere = pl.BlockSpec(memory_space=pl.ANY)
     return pl.pallas_call(
         toeplitz_body,
-        out_shape=jax.ShapeDtypeStruct((2 * (replica.shape[1] + LANES), 2 * LANES), BF16),
+        out_shape=[
+            jax.ShapeDtypeStruct((2 * (replica.shape[1] + LANES), 2 * LANES), BF16),
+            jax.ShapeDtypeStruct(through.shape, through.dtype),
+        ],
+        in_specs=[pl.BlockSpec(memory_space=pltpu.VMEM), anywhere],
+        out_specs=[pl.BlockSpec(memory_space=pltpu.VMEM), anywhere],
+        input_output_aliases={1: 1},
         cost_estimate=SMALL_COST,
         name="toeplitz_taps",
-    )(replica)
+    )(replica, through)
 
 
 def tiles_body(tracks, count, place_ref, flag_ref, taps_ref, repeat_ref, gather_ref, *rest):
@@ -559,16 +566,15 @@
     edges[spare_chunk] = [0] + edges[spare_chunk]
 
     rows = bins + TILE
-    place = cut_places(place[0], place[1], rows)
+    taps, place = toeplitz_taps(replica, cut_places(place[0], place[1], rows))
     far_places = [exchanged(place, slot) for slot in cut_slots]
     place = place[:, None]
     sources = weight_tables(beam_weights, chirp)
     far_places = jnp.stack(
         [item for item in far_places for _ in range(beams)], axis=1
     )
-    taps = toeplitz_taps(replica)
     first_blocks, far, far_edges, flag, weights = partial_beams(
-        echoes, table, sources, beams, 0, width, edges[0], before=[taps, far_places]
+        echoes, table, sources, beams, 0, width, edges[0], before=[taps]
     )
     fars, ends = [far], [far_edges]
     flag = passed_along(flag, "gate", 1)

time: 160 us -> 160 us (level)
  starting transfers between devices: 39.5 us -> 36.9 us
  waiting for transfers between devices: 14.6 us -> 16.4 us
    ppermute x6, starting transfers between devices: 9.58 us -> 7.56 us  [exchanged(): lax.ppermute(value, 'pulse', [(rank, rank ^ slot) for rank in range(ranks)])]
    ppermute x3, waiting for transfers between devices: 0.6 us -> 2.26 us  [weight_tables(): lax.ppermute(flat, 'pulse', [(rank, rank ^ slot) for rank in range(ranks)])]
  transfers between devices with their start and end apart: 17 -> 17, of which waited for: 7 -> 5; matrix products, arithmetic and copies ran while one was open for 2% -> 3% of each run, Pallas kernels for 33% -> 33%
where the time goes in v3:
time: 160 us; the launch traced here: 159 us
  Pallas kernels  78.4 us (49%)
  starting transfers between devices  36.9 us (23%)
  blocking collectives  21.8 us (14%)
  waiting for transfers between devices  16.4 us (10%)
  other arithmetic  3.23 us (2%)
  local copies, waits for them, and re-layouts  2.23 us (1%)
    pallas_call x2, Pallas kernels, partial_beams(): pl.pallas_call(functools.partial(partial_beams_body, ranks, beams, edges,...  35.4 us
    pallas_call x3, Pallas kernels, beam_tiles(): pl.pallas_call(functools.partial(tiles_body, tracks, len(pieces)), grid=(...  28.2 us
    all_to_all x1, blocking collectives, local(): lax.all_to_all(tiles.reshape(owners, capacity * 2, 2 * LANES), ('pulse',...  21.8 us
    ppermute x7, starting transfers between devices, passed_along(): lax.ppermute(value, axis, [(source, source + steps) for source in range(l...  14.8 us
    all_to_all x1, starting transfers between devices, local(): lax.all_to_all(tiles.reshape(owners, capacity * 2, 2 * LANES), ('pulse',...  10.1 us
    all_to_all x1, waiting for transfers between devices, local(): lax.all_to_all(tiles.reshape(owners, capacity * 2, 2 * LANES), ('pulse',...  9.06 us
    ppermute x6, starting transfers between devices, exchanged(): lax.ppermute(value, 'pulse', [(rank, rank ^ slot) for rank in range(ranks)])  7.56 us
    pallas_call x2, Pallas kernels, summed_block(): pl.pallas_call(functools.partial(summed_body, len(terms), edges), grid=(b...  5.86 us
  transfers between devices with their start and end apart: 17, of which 5 were waited for; matrix products, arithmetic and copies ran while one was open for 3% of the time, Pallas kernels for 33%

profile of v3, /device:TPU:0, one launch (start us, length us, event | category | flops | bytes accessed | tf_op | source)
XLA Modules:
  0.0 159.2 jit_solution(2145701344280128109)
XLA Ops:
  0.0 2.9 %collective-permute-start = (f32[32,512]{1,0:T(8,128)}, f32[32,512]{1,0:T(8,128)S(1)}, u32[]{:S(2)}, u32[]{:S(2)}) collective-permute-start(f32[32,512]{1,0:T(8,128)} %bitcast.29), channel_id=1, source_target_pairs={{0,8},{8,0},{16,24},{24,16},{1,9},{9,1},{17,25},{25,17},{2,10},{10... | collective-permute-start | bytes 196616 | tf_op jit(solution)/shard_map/ppermute | solution.py:127
  2.9 1.5 collective-permute-start.1
  4.5 0.7 fusion.3
  5.2 0.6 pad_add_fusion.1.through_ref
  5.8 1.8 %toeplitz_taps.1 = (bf16[768,256]{1,0:T(8,128)(2,1)}, s32[3,256]{1,0:T(4,128)}) custom-call(bf16[2,256]{1,0:T(2,128)(2,1)} %replica_ref.1, s32[3,256]{1,0:T(4,128)} %pad_add_fusion.1.through_ref), custom_call_target="tpu_custom_call", output_to_operand_aliasing={{1}: (1, {})} | custom-call | flops 1048576 | bytes 65536 | tf_op jit(solution)/shard_map/toeplitz_taps/pallas_call | solution.py:361
  7.6 0.0 collective-permute-done.rest_2_
  7.6 0.0 collective-permute-done.1.rest_3_
  7.6 2.3 %collective-permute-done.2.rest_4_ = f32[32,512]{1,0:T(8,128)S(1)} collective-permute-done((f32[32,512]{1,0:T(8,128)}, f32[32,512]{1,0:T(8,128)S(1)}, u32[]{:S(2)}, u32[]{:S(2)}) %collective-permute-start.2) | collective-permute-done | bytes 65568 | tf_op jit(solution)/shard_map/ppermute | solution.py:127
  9.8 0.6 copy-done.4
  10.5 20.7 %partial_beams.2 = (bf16[2,2,528,256]{3,2,1,0:T(8,128)(2,1)}, bf16[2,2,528,256]{3,2,1,0:T(8,128)(2,1)}, bf16[2,2,528,256]{3,2,1,0:T(8,128)(2,1)}, bf16[2,2,528,2...) custom-call(bf16[2,8,512,512]{3,2,1,0:T(8,128)(2,1)} %echo_ref.3, ...), custom_call_target="tpu_custom_call" | custom-call | flops 1048576 | bytes 65536 | tf_op jit(solution)/shard_map/partial_beams/pallas_call | solution.py:280
  31.1 0.6 collective-permute-start.11
  31.7 0.7 collective-permute-start.12
  32.5 1.3 collective-permute-start.3
  33.8 2.3 %collective-permute-start.6 = (s32[3,256]{1,0:T(4,128)S(1)}, s32[3,256]{1,0:T(4,128)S(1)}, u32[]{:S(2)}, u32[]{:S(2)}) collective-permute-start(s32[3,256]{1,0:T(4,128)S(1)} %copy-done.6), channel_id=1, source_target_pairs={{0,24},{8,16},{16,8},{24,0},{1,25},{9,17},{17,9},{25,1},{2,26},{10... | collective-permute-start | bytes 9224 | tf_op jit(solution)/shard_map/ppermute | solution.py:557
  36.1 1.3 collective-permute-start.8
  37.4 0.0 collective-permute-done.3.rest_1_.flag_ref
  37.4 0.6 copy-done.5
  38.0 14.7 %partial_beams.3 = (bf16[2,2,528,256]{3,2,1,0:T(8,128)(2,1)}, bf16[2,2,528,256]{3,2,1,0:T(8,128)(2,1)}, bf16[2,2,528,256]{3,2,1,0:T(8,128)(2,1)}, bf16[2,2,528,2...) custom-call(bf16[2,8,512,512]{3,2,1,0:T(8,128)(2,1)} %echo_ref.3, ...), custom_call_target="tpu_custom_call" | custom-call | flops 1048576 | bytes 65536 | tf_op jit(solution)/shard_map/partial_beams/pallas_call | solution.py:280
  52.7 0.6 collective-permute-start.4
  53.3 2.3 %collective-permute-done.6 = s32[3,256]{1,0:T(4,128)S(1)} collective-permute-done((s32[3,256]{1,0:T(4,128)S(1)}, s32[3,256]{1,0:T(4,128)S(1)}, u32[]{:S(2)}, u32[]{:S(2)}) %collective-permute-start.6) | collective-permute-done | bytes 3104 | tf_op jit(solution)/shard_map/ppermute | solution.py:557
  55.6 1.4 collective-permute-start.5
  57.0 0.0 collective-permute-done.11.refs_1_
  57.0 1.3 collective-permute-start.7
  58.3 1.3 collective-permute-start.9
  59.6 2.9 %summed_block.3.rest_1_ = bf16[2,2,528,256]{3,2,1,0:T(8,128)(2,1)} custom-call(bf16[2,2,528,256]{3,2,1,0:T(8,128)(2,1)} %get-tuple-element.34.refs_0_, bf16[2,2,528,256]{3,2,1,0:T(8,128)(2,1)} %collective-permute-done.11.refs_1_, bf16[2,2,528,256]{3,2,1,0:T(8,128)(2,1)} %collective-permute-done.12.refs_2_), custom_call_target="tpu_custom_call" | custom-call | flops 1048576 | bytes 65536 | tf_op jit(solution)/shard_map/summed_block/pallas_call | solution.py:324
  62.5 1.3 collective-permute-start.13
  63.8 0.6 pad_add_fusion.place_ref
  64.4 13.2 %beam_tiles.3.refs_3_ = bf16[2,512,256]{2,1,0:T(8,128)(2,1)} custom-call(s32[3,2,256]{2,1,0:T(2,128)} %pad_add_fusion.place_ref, f32[8,128]{1,0:T(8,128)} %copy-done.5, bf16[768,256]{1,0:T(8,128)(2,1)} %get-tuple-element.23.rest_8_.taps_ref, bf16[128,256]{1,0:T(8,128)(2,1)} %constant.93.clone.repeat_ref, bf16[32,256]{1,0:T(8,128)(2,1)} %constant.92.clone.rest_7_.gather_ref, ...), custom_call_target="tpu_custom_call" | custom-call | flops 1048576 | bytes 65536 | tf_op jit(solution)/shard_map/beam_tiles/pallas_call | solution.py:487
  77.6 2.0 %collective-permute-start.15 = (bf16[2,512,256]{2,1,0:T(8,128)(2,1)}, bf16[2,512,256]{2,1,0:T(8,128)(2,1)}, u32[]{:S(2)}, u32[]{:S(2)}) collective-permute-start(bf16[2,512,256]{2,1,0:T(8,128)(2,1)} %beam_tiles.3.refs_3_), channel_id=1, source_target_pairs={{0,24},{8,16},{16,8},{24,0},{1,25},{9,17},{17,9},{25,1},{2,26},{10... | collective-permute-start | bytes 1572872 | tf_op jit(solution)/shard_map/ppermute | solution.py:557
  79.6 2.2 %collective-permute-done.5.refs_2_ = bf16[2,2,528,256]{3,2,1,0:T(8,128)(2,1)} collective-permute-done((bf16[2,2,528,256]{3,2,1,0:T(8,128)(2,1)}, bf16[2,2,528,256]{3,2,1,0:T(8,128)(2,1)}, u32[]{:S(2)}, u32[]{:S(2)}) %collective-permute-start.5) | collective-permute-done | bytes 1081376 | tf_op jit(solution)/shard_map/ppermute | solution.py:557
  81.7 3.0 %summed_block.2 = (bf16[2,2,528,256]{3,2,1,0:T(8,128)(2,1)}, bf16[2,1,528,256]{3,2,1,0:T(8,128)(2,1)}, bf16[2,1,528,256]{3,2,1,0:T(8,128)(2,1)}) custom-call(bf16[2,2,528,256]{3,2,1,0:T(8,128)(2,1)} %get-tuple-element.26.refs_0_, bf16[2,2,528,256]{3,2,1,0:T(8,128)(2,1)} %collective-permute-done.4.refs_1_, ...), custom_call_target="tpu_custom_call" | custom-call | flops 1048576 | bytes 65536 | tf_op jit(solution)/shard_map/summed_block/pallas_call | solution.py:324
  84.7 6.9 %collective-permute-start.10 = (bf16[2,1,528,256]{3,2,1,0:T(8,128)(2,1)}, bf16[2,1,528,256]{3,2,1,0:T(8,128)(2,1)S(1)}, u32[]{:S(2)}, u32[]{:S(2)}) collective-permute-start(bf16[2,1,528,256]{3,2,1,0:T(8,128)(2,1)} %get-tuple-element.33), channel_id=1, source_target_pairs={{0,1},{1,2},{2,3},{3,4},{4,5},{5,6},{6,7},{8,9},{9,10},{10,11},{11... | collective-permute-start | bytes 1622024 | tf_op jit(solution)/shard_map/ppermute | solution.py:25
  91.6 1.5 collective-permute-start.14
  93.1 0.6 broadcast_in_dim.2.place_ref
  93.7 0.6 reduce-window.6
  94.3 0.2 slice_reduce_fusion
  94.5 0.1 fusion.1
  94.6 0.6 add_add_fusion.slot_ref
  95.2 0.6 collective-permute-done.14.rest_4_
  95.8 0.2 copy-done
  96.0 7.5 %beam_tiles.5.rest_0_ = bf16[1,512,256]{2,1,0:T(8,128)(2,1)} custom-call(s32[3,1,256]{2,1,0:T(1,128)} %broadcast_in_dim.2.place_ref, f32[8,128]{1,0:T(8,128)} %copy-done.5, bf16[768,256]{1,0:T(8,128)(2,1)} %get-tuple-element.23.rest_8_.taps_ref, bf16[128,256]{1,0:T(8,128)(2,1)} %constant.93.clone.repeat_ref, ...), custom_call_target="tpu_custom_call" | custom-call | flops 1048576 | bytes 65536 | tf_op jit(solution)/shard_map/beam_tiles/pallas_call | solution.py:487
  103.6 2.6 %slotted_tiles.3 = bf16[1280,256]{1,0:T(8,128)(2,1)} custom-call(s32[256]{0:T(256)} %add_add_fusion.slot_ref, bf16[1,512,256]{2,1,0:T(8,128)(2,1)} %beam_tiles.5.rest_0_, bf16[2,512,256]{2,1,0:T(8,128)(2,1)} %collective-permute-done.15.rest_1_), custom_call_target="tpu_custom_call" | custom-call | flops 1048576 | bytes 65536 | tf_op jit(solution)/shard_map/slotted_tiles/pallas_call | solution.py:450
  106.2 10.1 %all-to-all-start.1 = ((bf16[32,40,256]{2,1,0:T(8,128)(2,1)}), bf16[32,40,256]{2,1,0:T(8,128)(2,1)S(1)}, u32[]{:S(2)}, u32[]{:S(2)}) async-start(bf16[32,40,256]{2,1,0:T(8,128)(2,1)} %bitcast.27), calls=%async_computation.1 | async-start | bytes 1310720 | tf_op jit(solution)/shard_map/all_to_all | solution.py:613
  116.2 7.5 %beam_tiles.4.rest_0_ = bf16[1,512,256]{2,1,0:T(8,128)(2,1)} custom-call(s32[3,1,256]{2,1,0:T(1,128)} %broadcast_in_dim.2.place_ref, f32[8,128]{1,0:T(8,128)} %copy-done.5, bf16[768,256]{1,0:T(8,128)(2,1)} %get-tuple-element.23.rest_8_.taps_ref, bf16[128,256]{1,0:T(8,128)(2,1)} %constant.93.clone.repeat_ref, ...), custom_call_target="tpu_custom_call" | custom-call | flops 1048576 | bytes 65536 | tf_op jit(solution)/shard_map/beam_tiles/pallas_call | solution.py:487
  123.7 2.6 %slotted_tiles.2 = bf16[1280,256]{1,0:T(8,128)(2,1)} custom-call(s32[256]{0:T(256)} %add_add_fusion.slot_ref, bf16[1,512,256]{2,1,0:T(8,128)(2,1)} %beam_tiles.4.rest_0_, bf16[2,512,256]{2,1,0:T(8,128)(2,1)} %collective-permute-done.15.rest_1_), custom_call_target="tpu_custom_call" | custom-call | flops 1048576 | bytes 65536 | tf_op jit(solution)/shard_map/slotted_tiles/pallas_call | solution.py:450
  126.3 9.1 %all-to-all-done.1 = bf16[32,40,256]{2,1,0:T(8,128)(2,1)S(1)} async-done(((bf16[32,40,256]{2,1,0:T(8,128)(2,1)}), bf16[32,40,256]{2,1,0:T(8,128)(2,1)S(1)}, u32[]{:S(2)}, u32[]{:S(2)}) %all-to-all-start.1) | async-done | bytes 655392 | tf_op jit(solution)/shard_map/all_to_all | solution.py:613
  135.4 21.8 %all_to_all.10 = bf16[32,40,256]{2,1,0:T(8,128)(2,1)S(1)} all-to-all(bf16[32,40,256]{2,1,0:T(8,128)(2,1)} %bitcast.28), channel_id=1, replica_groups=mesh['pulse'=4,'gate'=8] {'pulse','gate'}, dimensions={0} | all-to-all | bytes 1310720 | tf_op jit(solution)/shard_map/all_to_all | solution.py:613
  157.2 2.0 %finished_tiles.1 = f32[640,1024]{1,0:T(8,128)} custom-call(bf16[1280,256]{1,0:T(8,128)(2,1)S(1)} %bitcast.26, bf16[1280,256]{1,0:T(8,128)(2,1)S(1)} %bitcast.25), custom_call_target="tpu_custom_call" | custom-call | flops 1048576 | bytes 65536 | tf_op jit(solution)/shard_map/finished_tiles/pallas_call | solution.py:526
  (27 shorter events, 0.1 us)
Async XLA Ops:
  0.0 7.6 %collective-permute-start = (f32[32,512]{1,0:T(8,128)}, f32[32,512]{1,0:T(8,128)S(1)}, u32[]{:S(2)}, u32[]{:S(2)}) collective-permute-start(f32[32,512]{1,0:T(8,128)} %bitcast.29), channel_id=1, source_target_pairs={{0,8},{8,0},{16,24},{24,16},{1,9},{9,1},{17,25},{25,17},{2,10},{10... | collective-permute-start | bytes 196616 | tf_op jit(solution)/shard_map/ppermute | solution.py:127
  2.9 4.6 %collective-permute-start.1 = (f32[32,512]{1,0:T(8,128)}, f32[32,512]{1,0:T(8,128)S(1)}, u32[]{:S(2)}, u32[]{:S(2)}) collective-permute-start(f32[32,512]{1,0:T(8,128)} %bitcast.30), channel_id=1, source_target_pairs={{0,16},{8,24},{16,0},{24,8},{1,17},{9,25},{17,1},{25,9},{2,18},{10... | collective-permute-start | bytes 196616 | tf_op jit(solution)/shard_map/ppermute | solution.py:127
  4.5 5.4 %collective-permute-start.2 = (f32[32,512]{1,0:T(8,128)}, f32[32,512]{1,0:T(8,128)S(1)}, u32[]{:S(2)}, u32[]{:S(2)}) collective-permute-start(f32[32,512]{1,0:T(8,128)} %bitcast.31), channel_id=1, source_target_pairs={{0,24},{8,16},{16,8},{24,0},{1,25},{9,17},{17,9},{25,1},{2,26},{10... | collective-permute-start | bytes 196616 | tf_op jit(solution)/shard_map/ppermute | solution.py:127
  7.6 2.3 %copy-start.2 = (f32[32,512]{1,0:T(8,128)}, f32[32,512]{1,0:T(8,128)S(1)}, u32[]{:S(2)}) copy-start(f32[32,512]{1,0:T(8,128)S(1)} %collective-permute-done.rest_2_) | copy-start | bytes 196612
  7.6 2.3 %copy-start.3 = (f32[32,512]{1,0:T(8,128)}, f32[32,512]{1,0:T(8,128)S(1)}, u32[]{:S(2)}) copy-start(f32[32,512]{1,0:T(8,128)S(1)} %collective-permute-done.1.rest_3_) | copy-start | bytes 196612
  9.8 0.6 copy-start.4
  10.5 23.3 %copy-start.6 = (s32[3,256]{1,0:T(4,128)S(1)}, s32[3,256]{1,0:T(4,128)}, u32[]{:S(2)}) copy-start(s32[3,256]{1,0:T(4,128)} %get-tuple-element.22) | copy-start | bytes 9220
  31.1 25.8 %collective-permute-start.11 = (bf16[2,2,528,256]{3,2,1,0:T(8,128)(2,1)}, bf16[2,2,528,256]{3,2,1,0:T(8,128)(2,1)}, u32[]{:S(2)}, u32[]{:S(2)}) collective-permute-start(bf16[2,2,528,256]{3,2,1,0:T(8,128)(2,1)} %get-tuple-element.35), channel_id=1, source_target_pairs={{0,8},{8,0},{16,24},{24,16},{1,9},{9,1},{17,25},{25,17},{2,10},{10... | collective-permute-start | bytes 3244040 | tf_op jit(solution)/shard_map/ppermute | solution.py:557
  31.7 26.5 %collective-permute-start.12 = (bf16[2,2,528,256]{3,2,1,0:T(8,128)(2,1)}, bf16[2,2,528,256]{3,2,1,0:T(8,128)(2,1)}, u32[]{:S(2)}, u32[]{:S(2)}) collective-permute-start(bf16[2,2,528,256]{3,2,1,0:T(8,128)(2,1)} %get-tuple-element.36), channel_id=1, source_target_pairs={{0,16},{8,24},{16,0},{24,8},{1,17},{9,25},{17,1},{25,9},{2,18},{10... | collective-permute-start | bytes 3244040 | tf_op jit(solution)/shard_map/ppermute | solution.py:557
  32.5 4.9 %collective-permute-start.3 = (f32[8,128]{1,0:T(8,128)}, f32[8,128]{1,0:T(8,128)S(1)}, u32[]{:S(2)}, u32[]{:S(2)}) collective-permute-start(f32[8,128]{1,0:T(8,128)} %get-tuple-element.24), channel_id=1, source_target_pairs={{0,1},{1,2},{2,3},{3,4},{4,5},{5,6},{6,7},{8,9},{9,10},{10,11},{11... | collective-permute-start | bytes 12296 | tf_op jit(solution)/shard_map/ppermute | solution.py:25
  33.8 21.8 %collective-permute-start.6 = (s32[3,256]{1,0:T(4,128)S(1)}, s32[3,256]{1,0:T(4,128)S(1)}, u32[]{:S(2)}, u32[]{:S(2)}) collective-permute-start(s32[3,256]{1,0:T(4,128)S(1)} %copy-done.6), channel_id=1, source_target_pairs={{0,24},{8,16},{16,8},{24,0},{1,25},{9,17},{17,9},{25,1},{2,26},{10... | collective-permute-start | bytes 9224 | tf_op jit(solution)/shard_map/ppermute | solution.py:557
  36.1 28.3 %collective-permute-start.8 = (bf16[2,2,528,256]{3,2,1,0:T(8,128)(2,1)}, bf16[2,2,528,256]{3,2,1,0:T(8,128)(2,1)}, u32[]{:S(2)}, u32[]{:S(2)}) collective-permute-start(bf16[2,2,528,256]{3,2,1,0:T(8,128)(2,1)} %get-tuple-element.30.rest_1_), channel_id=1, source_target_pairs={{1,0},{2,1},{3,2},{4,3},{5,4},{6,5},{7,6},{9,8},{10,9},{11,10},{12... | collective-permute-start | bytes 3244040 | tf_op jit(solution)/shard_map/ppermute | solution.py:25
  37.4 0.6 copy-start.5
  52.7 26.9 %collective-permute-start.4 = (bf16[2,2,528,256]{3,2,1,0:T(8,128)(2,1)}, bf16[2,2,528,256]{3,2,1,0:T(8,128)(2,1)}, u32[]{:S(2)}, u32[]{:S(2)}) collective-permute-start(bf16[2,2,528,256]{3,2,1,0:T(8,128)(2,1)} %get-tuple-element.27), channel_id=1, source_target_pairs={{0,8},{8,0},{16,24},{24,16},{1,9},{9,1},{17,25},{25,17},{2,10},{10... | collective-permute-start | bytes 3244040 | tf_op jit(solution)/shard_map/ppermute | solution.py:557
  55.6 26.1 %collective-permute-start.5 = (bf16[2,2,528,256]{3,2,1,0:T(8,128)(2,1)}, bf16[2,2,528,256]{3,2,1,0:T(8,128)(2,1)}, u32[]{:S(2)}, u32[]{:S(2)}) collective-permute-start(bf16[2,2,528,256]{3,2,1,0:T(8,128)(2,1)} %get-tuple-element.28), channel_id=1, source_target_pairs={{0,16},{8,24},{16,0},{24,8},{1,17},{9,25},{17,1},{25,9},{2,18},{10... | collective-permute-start | bytes 3244040 | tf_op jit(solution)/shard_map/ppermute | solution.py:557
  57.0 5.5 %collective-permute-start.7 = (bf16[2,1,528,256]{3,2,1,0:T(8,128)(2,1)}, bf16[2,1,528,256]{3,2,1,0:T(8,128)(2,1)S(1)}, u32[]{:S(2)}, u32[]{:S(2)}) collective-permute-start(bf16[2,1,528,256]{3,2,1,0:T(8,128)(2,1)} %get-tuple-element.29), channel_id=1, source_target_pairs={{0,1},{1,2},{2,3},{3,4},{4,5},{5,6},{6,7},{8,9},{9,10},{10,11},{11... | collective-permute-start | bytes 1622024 | tf_op jit(solution)/shard_map/ppermute | solution.py:25
  58.3 6.1 %collective-permute-start.9 = (bf16[2,1,528,256]{3,2,1,0:T(8,128)(2,1)}, bf16[2,1,528,256]{3,2,1,0:T(8,128)(2,1)}, u32[]{:S(2)}, u32[]{:S(2)}) collective-permute-start(bf16[2,1,528,256]{3,2,1,0:T(8,128)(2,1)} %get-tuple-element.32), channel_id=1, source_target_pairs={{1,0},{2,1},{3,2},{4,3},{5,4},{6,5},{7,6},{9,8},{10,9},{11,10},{12... | collective-permute-start | bytes 1622024 | tf_op jit(solution)/shard_map/ppermute | solution.py:25
  62.5 1.9 %copy-start.1 = (bf16[2,1,528,256]{3,2,1,0:T(8,128)(2,1)}, bf16[2,1,528,256]{3,2,1,0:T(8,128)(2,1)S(1)}, u32[]{:S(2)}) copy-start(bf16[2,1,528,256]{3,2,1,0:T(8,128)(2,1)S(1)} %collective-permute-done.7.rest_0_) | copy-start | bytes 1622020
  62.5 33.3 %collective-permute-start.13 = (bf16[2,2,528,256]{3,2,1,0:T(8,128)(2,1)}, bf16[2,2,528,256]{3,2,1,0:T(8,128)(2,1)}, u32[]{:S(2)}, u32[]{:S(2)}) collective-permute-start(bf16[2,2,528,256]{3,2,1,0:T(8,128)(2,1)} %summed_block.3.rest_1_), channel_id=1, source_target_pairs={{1,0},{2,1},{3,2},{4,3},{5,4},{6,5},{7,6},{9,8},{10,9},{11,10},{12... | collective-permute-start | bytes 3244040 | tf_op jit(solution)/shard_map/ppermute | solution.py:25
  77.6 26.0 %collective-permute-start.15 = (bf16[2,512,256]{2,1,0:T(8,128)(2,1)}, bf16[2,512,256]{2,1,0:T(8,128)(2,1)}, u32[]{:S(2)}, u32[]{:S(2)}) collective-permute-start(bf16[2,512,256]{2,1,0:T(8,128)(2,1)} %beam_tiles.3.refs_3_), channel_id=1, source_target_pairs={{0,24},{8,16},{16,8},{24,0},{1,25},{9,17},{17,9},{25,1},{2,26},{10... | collective-permute-start | bytes 1572872 | tf_op jit(solution)/shard_map/ppermute | solution.py:557
  81.7 11.4 %copy-start.7 = (s32[256]{0:T(256)S(1)}, s32[256]{0:T(256)}, u32[]{:S(2)}) copy-start(s32[256]{0:T(256)} %param.21) | copy-start | bytes 3076
  84.7 10.5 %collective-permute-start.10 = (bf16[2,1,528,256]{3,2,1,0:T(8,128)(2,1)}, bf16[2,1,528,256]{3,2,1,0:T(8,128)(2,1)S(1)}, u32[]{:S(2)}, u32[]{:S(2)}) collective-permute-start(bf16[2,1,528,256]{3,2,1,0:T(8,128)(2,1)} %get-tuple-element.33), channel_id=1, source_target_pairs={{0,1},{1,2},{2,3},{3,4},{4,5},{5,6},{6,7},{8,9},{9,10},{10,11},{11... | collective-permute-start | bytes 1622024 | tf_op jit(solution)/shard_map/ppermute | solution.py:25
  91.6 4.2 %collective-permute-start.14 = (bf16[2,1,528,256]{3,2,1,0:T(8,128)(2,1)}, bf16[2,1,528,256]{3,2,1,0:T(8,128)(2,1)}, u32[]{:S(2)}, u32[]{:S(2)}) collective-permute-start(bf16[2,1,528,256]{3,2,1,0:T(8,128)(2,1)} %get-tuple-element.38), channel_id=1, source_target_pairs={{1,0},{2,1},{3,2},{4,3},{5,4},{6,5},{7,6},{9,8},{10,9},{11,10},{12... | collective-permute-start | bytes 1622024 | tf_op jit(solution)/shard_map/ppermute | solution.py:25
  95.2 0.8 copy-start
  106.2 29.2 %all-to-all-start.1 = ((bf16[32,40,256]{2,1,0:T(8,128)(2,1)}), bf16[32,40,256]{2,1,0:T(8,128)(2,1)S(1)}, u32[]{:S(2)}, u32[]{:S(2)}) async-start(bf16[32,40,256]{2,1,0:T(8,128)(2,1)} %bitcast.27), calls=%async_computation.1 | async-start | bytes 1310720 | tf_op jit(solution)/shard_map/all_to_all | solution.py:613

commit v4 on v2

--- a/solution.py
+++ b/solution.py
@@ -425,17 +425,16 @@
     for part in parts[1:]:
         total += part[0].astype(F32)
     for part in range(2):
-        total_ref[part] = total[:, part * LANES : (part + 1) * LANES]
+        here = pl.ds(part, total.shape[0], stride=2)
+        total_ref[here, :] = total[:, part * LANES : (part + 1) * LANES]
     sorted_ref[...] = jnp.zeros(sorted_ref.shape, F32)
 
     def move(track, carry):
-        target = pl.ds(slot_ref[track] * 2, 2)
-        sorted_ref[:, target, :] = total_ref[:, pl.ds(track * 2, 2), :]
+        sorted_ref[pl.ds(slot_ref[track] * 4, 4), :] = total_ref[pl.ds(track * 4, 4), :]
         return carry
 
     lax.fori_loop(0, slot_ref.shape[0], move, 0, unroll=8)
-    for part in range(2):
-        out_ref[:, part * LANES : (part + 1) * LANES] = sorted_ref[part].astype(BF16)
+    out_ref[...] = sorted_ref[...].astype(BF16)
 
 
 def slotted(terms, slots, slot_total):
@@ -443,16 +442,16 @@
     return pl.pallas_call(
         functools.partial(slots_body, len(terms)),
         grid=(1,),
-        out_shape=jax.ShapeDtypeStruct((slot_total * 2, lanes), BF16),
+        out_shape=jax.ShapeDtypeStruct((slot_total * 4, LANES), BF16),
         in_specs=[pl.BlockSpec(memory_space=pltpu.SMEM)]
         + [
             pl.BlockSpec((1, count, lanes), lambda i, entry=entry: (entry, 0, 0))
             for _, entry in terms
         ],
-        out_specs=pl.BlockSpec((slot_total * 2, lanes), lambda i: (0, 0)),
+        out_specs=pl.BlockSpec((slot_total * 4, LANES), lambda i: (0, 0)),
         scratch_shapes=[
-            pltpu.VMEM((2, count, LANES), F32),
-            pltpu.VMEM((2, slot_total * 2, LANES), F32),
+            pltpu.VMEM((count * 2, LANES), F32),
+            pltpu.VMEM((slot_total * 4, LANES), F32),
         ],
         compiler_params=pltpu.CompilerParams(vmem_limit_bytes=VMEM_LIMIT),
         cost_estimate=SMALL_COST,
@@ -507,11 +506,12 @@
     parts, out_ref, wide_ref = refs[:-2], refs[-2], refs[-1]
     rows = out_ref.shape[0]
     for beam, part in enumerate(parts):
-        for side in range(2):
-            wide_ref[...] = part[:, side * LANES : (side + 1) * LANES].astype(F32)
-            for half in range(2):
+        wide_ref[...] = part[...].astype(F32)
+        for half in range(2):
+            for side in range(2):
                 column = ((side * len(parts) + beam) * 2 + half) * LANES
-                out_ref[:, column : column + LANES] = wide_ref[pl.ds(half, rows, stride=2), :]
+                here = pl.ds(half * 2 + side, rows, stride=4)
+                out_ref[:, column : column + LANES] = wide_ref[here, :]
 
 
 def finished(parts, rows):
@@ -521,7 +521,7 @@
         out_shape=jax.ShapeDtypeStruct((rows, len(parts) * 4 * LANES), F32),
         in_specs=[whole] * len(parts),
         out_specs=whole,
-        scratch_shapes=[pltpu.VMEM((rows * 2, LANES), F32)],
+        scratch_shapes=[pltpu.VMEM((rows * 4, LANES), F32)],
         compiler_params=pltpu.CompilerParams(vmem_limit_bytes=32 * 2**20),
         cost_estimate=SMALL_COST,
         name="finished_tiles",
@@ -605,13 +605,13 @@
             [(tiles, 0)] + [(item, beam) for item in arrived], slots, owners * capacity
         )
         sent = lax.all_to_all(
-            tiles.reshape(owners, capacity * 2, 2 * LANES),
+            tiles.reshape(owners, capacity * 4, LANES),
             ("pulse", "gate"),
             split_axis=0,
             concat_axis=0,
             tiled=True,
         )
-        results.append(sent.reshape(owners * capacity * 2, 2 * LANES))
+        results.append(sent.reshape(owners * capacity * 4, LANES))
     return finished(results, owners * capacity)
 
 

time: 160 us -> 160 us (level)
  no operation moved by 1% of the time
where the time goes in v4:
time: 160 us; the launch traced here: 159 us
  Pallas kernels  78.3 us (49%)
  starting transfers between devices  39.5 us (25%)
  blocking collectives  21.8 us (14%)
  waiting for transfers between devices  14.6 us (9%)
  local copies, waits for them, and re-layouts  2.82 us (2%)
  other arithmetic  2.05 us (1%)
    pallas_call x2, Pallas kernels, partial_beams(): pl.pallas_call(functools.partial(partial_beams_body, ranks, beams, edges,...  35.4 us
    pallas_call x3, Pallas kernels, beam_tiles(): pl.pallas_call(functools.partial(tiles_body, tracks, len(pieces)), grid=(...  28.2 us
    all_to_all x1, blocking collectives, local(): lax.all_to_all(tiles.reshape(owners, capacity * 4, LANES), ('pulse', 'gat...  21.8 us
    ppermute x7, starting transfers between devices, passed_along(): lax.ppermute(value, axis, [(source, source + steps) for source in range(l...  16.3 us
    all_to_all x1, starting transfers between devices, local(): lax.all_to_all(tiles.reshape(owners, capacity * 4, LANES), ('pulse', 'gat...  10.1 us
    ppermute x6, starting transfers between devices, exchanged(): lax.ppermute(value, 'pulse', [(rank, rank ^ slot) for rank in range(ranks)])  9.58 us
    all_to_all x1, waiting for transfers between devices, local(): lax.all_to_all(tiles.reshape(owners, capacity * 4, LANES), ('pulse', 'gat...  9.12 us
    pallas_call x2, Pallas kernels, summed_block(): pl.pallas_call(functools.partial(summed_body, len(terms), edges), grid=(b...  5.84 us
  transfers between devices with their start and end apart: 17, of which 7 were waited for; matrix products, arithmetic and copies ran while one was open for 2% of the time, Pallas kernels for 33%

profile of v4, /device:TPU:0, one launch (start us, length us, event | category | flops | bytes accessed | tf_op | source)
XLA Modules:
  0.0 159.3 jit_solution(4687794031545955897)
XLA Ops:
  0.0 0.7 fusion.3
  0.8 4.0 %collective-permute-start.3 = (s32[3,256]{1,0:T(4,128)S(1)}, s32[3,256]{1,0:T(4,128)S(1)}, u32[]{:S(2)}, u32[]{:S(2)}) collective-permute-start(s32[3,256]{1,0:T(4,128)S(1)} %pad_add_fusion.1), channel_id=1, source_target_pairs={{0,24},{8,16},{16,8},{24,0},{1,25},{9,17},{17,9},{25,1},{2,26},{10... | collective-permute-start | bytes 9224 | tf_op jit(solution)/shard_map/ppermute | solution.py:550
  4.7 0.1 collective-permute-start.2
  4.8 1.9 %collective-permute-start.1 = (f32[32,512]{1,0:T(8,128)}, f32[32,512]{1,0:T(8,128)S(1)}, u32[]{:S(2)}, u32[]{:S(2)}) collective-permute-start(f32[32,512]{1,0:T(8,128)} %bitcast.31), channel_id=1, source_target_pairs={{0,16},{8,24},{16,0},{24,8},{1,17},{9,25},{17,1},{25,9},{2,18},{10... | collective-permute-start | bytes 196616 | tf_op jit(solution)/shard_map/ppermute | solution.py:127
  6.7 1.5 collective-permute-start
  8.2 1.8 %toeplitz_taps.1.rest_8_.taps_ref = bf16[768,256]{1,0:T(8,128)(2,1)} custom-call(bf16[2,256]{1,0:T(2,128)(2,1)} %replica_ref.1), custom_call_target="tpu_custom_call" | custom-call | flops 1048576 | bytes 65536 | tf_op jit(solution)/shard_map/toeplitz_taps/pallas_call | solution.py:360
  10.0 0.6 copy.20.rest_9_.place_ref
  10.6 0.6 collective-permute-done.rest_2_
  11.2 0.0 copy-done.2
  11.2 0.0 copy-done.3
  11.2 0.6 copy-done.4
  11.8 20.7 %partial_beams.2 = (bf16[2,2,528,256]{3,2,1,0:T(8,128)(2,1)}, bf16[2,2,528,256]{3,2,1,0:T(8,128)(2,1)}, bf16[2,2,528,256]{3,2,1,0:T(8,128)(2,1)}, bf16[2,2,528,2...) custom-call(bf16[2,8,512,512]{3,2,1,0:T(8,128)(2,1)} %echo_ref.3, ...), custom_call_target="tpu_custom_call" | custom-call | flops 1048576 | bytes 65536 | tf_op jit(solution)/shard_map/partial_beams/pallas_call | solution.py:280
  32.5 1.6 collective-permute-start.11
  34.1 0.5 collective-permute-start.12
  34.6 1.3 collective-permute-start.4
  35.8 1.3 collective-permute-start.8
  37.2 0.6 copy-done.5
  37.7 14.7 %partial_beams.3 = (bf16[2,2,528,256]{3,2,1,0:T(8,128)(2,1)}, bf16[2,2,528,256]{3,2,1,0:T(8,128)(2,1)}, bf16[2,2,528,256]{3,2,1,0:T(8,128)(2,1)}, bf16[2,2,528,2...) custom-call(bf16[2,8,512,512]{3,2,1,0:T(8,128)(2,1)} %echo_ref.3, ...), custom_call_target="tpu_custom_call" | custom-call | flops 1048576 | bytes 65536 | tf_op jit(solution)/shard_map/partial_beams/pallas_call | solution.py:280
  52.4 0.5 collective-permute-start.5
  52.9 1.6 %collective-permute-start.6 = (bf16[2,2,528,256]{3,2,1,0:T(8,128)(2,1)}, bf16[2,2,528,256]{3,2,1,0:T(8,128)(2,1)}, u32[]{:S(2)}, u32[]{:S(2)}) collective-permute-start(bf16[2,2,528,256]{3,2,1,0:T(8,128)(2,1)} %get-tuple-element.24), channel_id=1, source_target_pairs={{0,16},{8,24},{16,0},{24,8},{1,17},{9,25},{17,1},{25,9},{2,18},{10... | collective-permute-start | bytes 3244040 | tf_op jit(solution)/shard_map/ppermute | solution.py:550
  54.6 2.8 %collective-permute-done.11.refs_1_ = bf16[2,2,528,256]{3,2,1,0:T(8,128)(2,1)} collective-permute-done((bf16[2,2,528,256]{3,2,1,0:T(8,128)(2,1)}, bf16[2,2,528,256]{3,2,1,0:T(8,128)(2,1)}, u32[]{:S(2)}, u32[]{:S(2)}) %collective-permute-start.11) | collective-permute-done | bytes 1081376 | tf_op jit(solution)/shard_map/ppermute | solution.py:550
  57.4 1.5 collective-permute-start.7
  58.9 1.3 collective-permute-start.9
  60.2 2.9 %summed_block.3.rest_1_ = bf16[2,2,528,256]{3,2,1,0:T(8,128)(2,1)} custom-call(bf16[2,2,528,256]{3,2,1,0:T(8,128)(2,1)} %get-tuple-element.30.refs_0_, bf16[2,2,528,256]{3,2,1,0:T(8,128)(2,1)} %collective-permute-done.11.refs_1_, bf16[2,2,528,256]{3,2,1,0:T(8,128)(2,1)} %collective-permute-done.12.refs_2_), custom_call_target="tpu_custom_call" | custom-call | flops 1048576 | bytes 65536 | tf_op jit(solution)/shard_map/summed_block/pallas_call | solution.py:324
  63.1 1.3 collective-permute-start.13
  64.4 0.5 collective-permute-done.9.rest_4_
  64.8 13.2 %beam_tiles.3.refs_3_ = bf16[2,512,256]{2,1,0:T(8,128)(2,1)} custom-call(s32[3,2,256]{2,1,0:T(2,128)} %copy.20.rest_9_.place_ref, f32[8,128]{1,0:T(8,128)} %copy-done.5, bf16[768,256]{1,0:T(8,128)(2,1)} %toeplitz_taps.1.rest_8_.taps_ref, bf16[128,256]{1,0:T(8,128)(2,1)} %constant.93.clone.repeat_ref, bf16[32,256]{1,0:T(8,128)(2,1)} %constant.92.clone.rest_7_.gather_ref, ...), custom_call_target="tpu_custom_call" | custom-call | flops 1048576 | bytes 65536 | tf_op jit(solution)/shard_map/beam_tiles/pallas_call | solution.py:479
  78.0 1.4 collective-permute-start.15
  79.4 0.1 collective-permute-done.5.refs_1_
  79.6 0.9 collective-permute-done.6.refs_2_
  80.5 3.0 %summed_block.2 = (bf16[2,2,528,256]{3,2,1,0:T(8,128)(2,1)}, bf16[2,1,528,256]{3,2,1,0:T(8,128)(2,1)}, bf16[2,1,528,256]{3,2,1,0:T(8,128)(2,1)}) custom-call(bf16[2,2,528,256]{3,2,1,0:T(8,128)(2,1)} %get-tuple-element.22.refs_0_, bf16[2,2,528,256]{3,2,1,0:T(8,128)(2,1)} %collective-permute-done.5.refs_1_, ...), custom_call_target="tpu_custom_call" | custom-call | flops 1048576 | bytes 65536 | tf_op jit(solution)/shard_map/summed_block/pallas_call | solution.py:324
  83.4 8.2 %collective-permute-start.10 = (bf16[2,1,528,256]{3,2,1,0:T(8,128)(2,1)}, bf16[2,1,528,256]{3,2,1,0:T(8,128)(2,1)S(1)}, u32[]{:S(2)}, u32[]{:S(2)}) collective-permute-start(bf16[2,1,528,256]{3,2,1,0:T(8,128)(2,1)} %get-tuple-element.29), channel_id=1, source_target_pairs={{0,1},{1,2},{2,3},{3,4},{4,5},{5,6},{6,7},{8,9},{9,10},{10,11},{11... | collective-permute-start | bytes 1622024 | tf_op jit(solution)/shard_map/ppermute | solution.py:25
  91.7 1.5 collective-permute-start.14
  93.2 0.6 broadcast_in_dim.2.place_ref
  93.8 0.6 reduce-window.6
  94.4 0.2 slice_reduce_fusion
  94.6 0.1 fusion.1
  94.7 0.6 add_add_fusion.slot_ref
  95.3 0.6 collective-permute-done.14.rest_4_
  95.9 0.2 copy-done
  96.1 7.5 %beam_tiles.4.rest_0_ = bf16[1,512,256]{2,1,0:T(8,128)(2,1)} custom-call(s32[3,1,256]{2,1,0:T(1,128)} %broadcast_in_dim.2.place_ref, f32[8,128]{1,0:T(8,128)} %copy-done.5, bf16[768,256]{1,0:T(8,128)(2,1)} %toeplitz_taps.1.rest_8_.taps_ref, bf16[128,256]{1,0:T(8,128)(2,1)} %constant.93.clone.repeat_ref, bf16[32,256]{1,0:T(8,128)(2,1)} %constant.92.clone.rest_7_.gather_ref, ...), custom_call_target="tpu_custom_call" | custom-call | flops 1048576 | bytes 65536 | tf_op jit(solution)/shard_map/beam_tiles/pallas_call | solution.py:479
  103.7 2.5 %slotted_tiles.2 = bf16[2560,128]{1,0:T(8,128)(2,1)} custom-call(s32[256]{0:T(256)} %add_add_fusion.slot_ref, bf16[1,512,256]{2,1,0:T(8,128)(2,1)} %beam_tiles.4.rest_0_, bf16[2,512,256]{2,1,0:T(8,128)(2,1)} %collective-permute-done.15.rest_1_), custom_call_target="tpu_custom_call" | custom-call | flops 1048576 | bytes 65536 | tf_op jit(solution)/shard_map/slotted_tiles/pallas_call | solution.py:442
  106.2 10.1 %all-to-all-start = ((bf16[32,80,128]{2,1,0:T(8,128)(2,1)}), bf16[32,80,128]{2,1,0:T(8,128)(2,1)S(1)}, u32[]{:S(2)}, u32[]{:S(2)}) async-start(bf16[32,80,128]{2,1,0:T(8,128)(2,1)} %bitcast.28), calls=%async_computation | async-start | bytes 1310720 | tf_op jit(solution)/shard_map/all_to_all | solution.py:607
  116.3 7.5 %beam_tiles.5.rest_0_ = bf16[1,512,256]{2,1,0:T(8,128)(2,1)} custom-call(s32[3,1,256]{2,1,0:T(1,128)} %broadcast_in_dim.2.place_ref, f32[8,128]{1,0:T(8,128)} %copy-done.5, bf16[768,256]{1,0:T(8,128)(2,1)} %toeplitz_taps.1.rest_8_.taps_ref, bf16[128,256]{1,0:T(8,128)(2,1)} %constant.93.clone.repeat_ref, bf16[32,256]{1,0:T(8,128)(2,1)} %constant.92.clone.rest_7_.gather_ref, ...), custom_call_target="tpu_custom_call" | custom-call | flops 1048576 | bytes 65536 | tf_op jit(solution)/shard_map/beam_tiles/pallas_call | solution.py:479
  123.8 2.5 %slotted_tiles.3 = bf16[2560,128]{1,0:T(8,128)(2,1)} custom-call(s32[256]{0:T(256)} %add_add_fusion.slot_ref, bf16[1,512,256]{2,1,0:T(8,128)(2,1)} %beam_tiles.5.rest_0_, bf16[2,512,256]{2,1,0:T(8,128)(2,1)} %collective-permute-done.15.rest_1_), custom_call_target="tpu_custom_call" | custom-call | flops 1048576 | bytes 65536 | tf_op jit(solution)/shard_map/slotted_tiles/pallas_call | solution.py:442
  126.3 9.1 %all-to-all-done = bf16[32,80,128]{2,1,0:T(8,128)(2,1)S(1)} async-done(((bf16[32,80,128]{2,1,0:T(8,128)(2,1)}), bf16[32,80,128]{2,1,0:T(8,128)(2,1)S(1)}, u32[]{:S(2)}, u32[]{:S(2)}) %all-to-all-start) | async-done | bytes 655392 | tf_op jit(solution)/shard_map/all_to_all | solution.py:607
  135.5 21.8 %all_to_all.10 = bf16[32,80,128]{2,1,0:T(8,128)(2,1)S(1)} all-to-all(bf16[32,80,128]{2,1,0:T(8,128)(2,1)} %bitcast.29), channel_id=1, replica_groups=mesh['pulse'=4,'gate'=8] {'pulse','gate'}, dimensions={0} | all-to-all | bytes 1310720 | tf_op jit(solution)/shard_map/all_to_all | solution.py:607
  157.2 2.1 %finished_tiles.1 = f32[640,1024]{1,0:T(8,128)} custom-call(bf16[2560,128]{1,0:T(8,128)(2,1)S(1)} %bitcast.26, bf16[2560,128]{1,0:T(8,128)(2,1)S(1)} %bitcast.27), custom_call_target="tpu_custom_call" | custom-call | flops 1048576 | bytes 65536 | tf_op jit(solution)/shard_map/finished_tiles/pallas_call | solution.py:519
  (25 shorter events, 0.1 us)
Async XLA Ops:
  0.8 9.2 %collective-permute-start.3 = (s32[3,256]{1,0:T(4,128)S(1)}, s32[3,256]{1,0:T(4,128)S(1)}, u32[]{:S(2)}, u32[]{:S(2)}) collective-permute-start(s32[3,256]{1,0:T(4,128)S(1)} %pad_add_fusion.1), channel_id=1, source_target_pairs={{0,24},{8,16},{16,8},{24,0},{1,25},{9,17},{17,9},{25,1},{2,26},{10... | collective-permute-start | bytes 9224 | tf_op jit(solution)/shard_map/ppermute | solution.py:550
  4.7 5.9 %collective-permute-start.2 = (f32[32,512]{1,0:T(8,128)}, f32[32,512]{1,0:T(8,128)S(1)}, u32[]{:S(2)}, u32[]{:S(2)}) collective-permute-start(f32[32,512]{1,0:T(8,128)} %bitcast.30), channel_id=1, source_target_pairs={{0,24},{8,16},{16,8},{24,0},{1,25},{9,17},{17,9},{25,1},{2,26},{10... | collective-permute-start | bytes 196616 | tf_op jit(solution)/shard_map/ppermute | solution.py:127
  4.8 5.8 %collective-permute-start.1 = (f32[32,512]{1,0:T(8,128)}, f32[32,512]{1,0:T(8,128)S(1)}, u32[]{:S(2)}, u32[]{:S(2)}) collective-permute-start(f32[32,512]{1,0:T(8,128)} %bitcast.31), channel_id=1, source_target_pairs={{0,16},{8,24},{16,0},{24,8},{1,17},{9,25},{17,1},{25,9},{2,18},{10... | collective-permute-start | bytes 196616 | tf_op jit(solution)/shard_map/ppermute | solution.py:127
  6.7 4.5 %collective-permute-start = (f32[32,512]{1,0:T(8,128)}, f32[32,512]{1,0:T(8,128)S(1)}, u32[]{:S(2)}, u32[]{:S(2)}) collective-permute-start(f32[32,512]{1,0:T(8,128)} %bitcast.32), channel_id=1, source_target_pairs={{0,8},{8,0},{16,24},{24,16},{1,9},{9,1},{17,25},{25,17},{2,10},{10... | collective-permute-start | bytes 196616 | tf_op jit(solution)/shard_map/ppermute | solution.py:127
  10.6 0.6 copy-start.2
  10.6 0.6 copy-start.3
  11.2 0.6 copy-start.4
  32.5 24.9 %collective-permute-start.11 = (bf16[2,2,528,256]{3,2,1,0:T(8,128)(2,1)}, bf16[2,2,528,256]{3,2,1,0:T(8,128)(2,1)}, u32[]{:S(2)}, u32[]{:S(2)}) collective-permute-start(bf16[2,2,528,256]{3,2,1,0:T(8,128)(2,1)} %get-tuple-element.31), channel_id=1, source_target_pairs={{0,8},{8,0},{16,24},{24,16},{1,9},{9,1},{17,25},{25,17},{2,10},{10... | collective-permute-start | bytes 3244040 | tf_op jit(solution)/shard_map/ppermute | solution.py:550
  34.1 24.8 %collective-permute-start.12 = (bf16[2,2,528,256]{3,2,1,0:T(8,128)(2,1)}, bf16[2,2,528,256]{3,2,1,0:T(8,128)(2,1)}, u32[]{:S(2)}, u32[]{:S(2)}) collective-permute-start(bf16[2,2,528,256]{3,2,1,0:T(8,128)(2,1)} %get-tuple-element.32), channel_id=1, source_target_pairs={{0,16},{8,24},{16,0},{24,8},{1,17},{9,25},{17,1},{25,9},{2,18},{10... | collective-permute-start | bytes 3244040 | tf_op jit(solution)/shard_map/ppermute | solution.py:550
  34.6 2.6 %collective-permute-start.4 = (f32[8,128]{1,0:T(8,128)}, f32[8,128]{1,0:T(8,128)S(1)}, u32[]{:S(2)}, u32[]{:S(2)}) collective-permute-start(f32[8,128]{1,0:T(8,128)} %get-tuple-element.20), channel_id=1, source_target_pairs={{0,1},{1,2},{2,3},{3,4},{4,5},{5,6},{6,7},{8,9},{9,10},{10,11},{11... | collective-permute-start | bytes 12296 | tf_op jit(solution)/shard_map/ppermute | solution.py:25
  35.8 29.0 %collective-permute-start.8 = (bf16[2,2,528,256]{3,2,1,0:T(8,128)(2,1)}, bf16[2,2,528,256]{3,2,1,0:T(8,128)(2,1)}, u32[]{:S(2)}, u32[]{:S(2)}) collective-permute-start(bf16[2,2,528,256]{3,2,1,0:T(8,128)(2,1)} %get-tuple-element.26.rest_1_), channel_id=1, source_target_pairs={{1,0},{2,1},{3,2},{4,3},{5,4},{6,5},{7,6},{9,8},{10,9},{11,10},{12... | collective-permute-start | bytes 3244040 | tf_op jit(solution)/shard_map/ppermute | solution.py:25
  37.2 0.6 copy-start.5
  52.4 27.1 %collective-permute-start.5 = (bf16[2,2,528,256]{3,2,1,0:T(8,128)(2,1)}, bf16[2,2,528,256]{3,2,1,0:T(8,128)(2,1)}, u32[]{:S(2)}, u32[]{:S(2)}) collective-permute-start(bf16[2,2,528,256]{3,2,1,0:T(8,128)(2,1)} %get-tuple-element.23), channel_id=1, source_target_pairs={{0,8},{8,0},{16,24},{24,16},{1,9},{9,1},{17,25},{25,17},{2,10},{10... | collective-permute-start | bytes 3244040 | tf_op jit(solution)/shard_map/ppermute | solution.py:550
  52.9 27.5 %collective-permute-start.6 = (bf16[2,2,528,256]{3,2,1,0:T(8,128)(2,1)}, bf16[2,2,528,256]{3,2,1,0:T(8,128)(2,1)}, u32[]{:S(2)}, u32[]{:S(2)}) collective-permute-start(bf16[2,2,528,256]{3,2,1,0:T(8,128)(2,1)} %get-tuple-element.24), channel_id=1, source_target_pairs={{0,16},{8,24},{16,0},{24,8},{1,17},{9,25},{17,1},{25,9},{2,18},{10... | collective-permute-start | bytes 3244040 | tf_op jit(solution)/shard_map/ppermute | solution.py:550
  57.4 5.7 %collective-permute-start.7 = (bf16[2,1,528,256]{3,2,1,0:T(8,128)(2,1)}, bf16[2,1,528,256]{3,2,1,0:T(8,128)(2,1)S(1)}, u32[]{:S(2)}, u32[]{:S(2)}) collective-permute-start(bf16[2,1,528,256]{3,2,1,0:T(8,128)(2,1)} %get-tuple-element.25), channel_id=1, source_target_pairs={{0,1},{1,2},{2,3},{3,4},{4,5},{5,6},{6,7},{8,9},{9,10},{10,11},{11... | collective-permute-start | bytes 1622024 | tf_op jit(solution)/shard_map/ppermute | solution.py:25
  58.9 5.9 %collective-permute-start.9 = (bf16[2,1,528,256]{3,2,1,0:T(8,128)(2,1)}, bf16[2,1,528,256]{3,2,1,0:T(8,128)(2,1)}, u32[]{:S(2)}, u32[]{:S(2)}) collective-permute-start(bf16[2,1,528,256]{3,2,1,0:T(8,128)(2,1)} %get-tuple-element.28), channel_id=1, source_target_pairs={{1,0},{2,1},{3,2},{4,3},{5,4},{6,5},{7,6},{9,8},{10,9},{11,10},{12... | collective-permute-start | bytes 1622024 | tf_op jit(solution)/shard_map/ppermute | solution.py:25
  63.1 1.8 %copy-start.1 = (bf16[2,1,528,256]{3,2,1,0:T(8,128)(2,1)}, bf16[2,1,528,256]{3,2,1,0:T(8,128)(2,1)S(1)}, u32[]{:S(2)}) copy-start(bf16[2,1,528,256]{3,2,1,0:T(8,128)(2,1)S(1)} %collective-permute-done.7.rest_0_) | copy-start | bytes 1622020
  63.1 32.8 %collective-permute-start.13 = (bf16[2,2,528,256]{3,2,1,0:T(8,128)(2,1)}, bf16[2,2,528,256]{3,2,1,0:T(8,128)(2,1)}, u32[]{:S(2)}, u32[]{:S(2)}) collective-permute-start(bf16[2,2,528,256]{3,2,1,0:T(8,128)(2,1)} %summed_block.3.rest_1_), channel_id=1, source_target_pairs={{1,0},{2,1},{3,2},{4,3},{5,4},{6,5},{7,6},{9,8},{10,9},{11,10},{12... | collective-permute-start | bytes 3244040 | tf_op jit(solution)/shard_map/ppermute | solution.py:25
  78.0 25.6 %collective-permute-start.15 = (bf16[2,512,256]{2,1,0:T(8,128)(2,1)}, bf16[2,512,256]{2,1,0:T(8,128)(2,1)}, u32[]{:S(2)}, u32[]{:S(2)}) collective-permute-start(bf16[2,512,256]{2,1,0:T(8,128)(2,1)} %beam_tiles.3.refs_3_), channel_id=1, source_target_pairs={{0,24},{8,16},{16,8},{24,0},{1,25},{9,17},{17,9},{25,1},{2,26},{10... | collective-permute-start | bytes 1572872 | tf_op jit(solution)/shard_map/ppermute | solution.py:550
  80.5 12.7 %copy-start.6 = (s32[256]{0:T(256)S(1)}, s32[256]{0:T(256)}, u32[]{:S(2)}) copy-start(s32[256]{0:T(256)} %param.21) | copy-start | bytes 3076
  83.4 11.9 %collective-permute-start.10 = (bf16[2,1,528,256]{3,2,1,0:T(8,128)(2,1)}, bf16[2,1,528,256]{3,2,1,0:T(8,128)(2,1)S(1)}, u32[]{:S(2)}, u32[]{:S(2)}) collective-permute-start(bf16[2,1,528,256]{3,2,1,0:T(8,128)(2,1)} %get-tuple-element.29), channel_id=1, source_target_pairs={{0,1},{1,2},{2,3},{3,4},{4,5},{5,6},{6,7},{8,9},{9,10},{10,11},{11... | collective-permute-start | bytes 1622024 | tf_op jit(solution)/shard_map/ppermute | solution.py:25
  91.7 4.2 %collective-permute-start.14 = (bf16[2,1,528,256]{3,2,1,0:T(8,128)(2,1)}, bf16[2,1,528,256]{3,2,1,0:T(8,128)(2,1)}, u32[]{:S(2)}, u32[]{:S(2)}) collective-permute-start(bf16[2,1,528,256]{3,2,1,0:T(8,128)(2,1)} %get-tuple-element.34), channel_id=1, source_target_pairs={{1,0},{2,1},{3,2},{4,3},{5,4},{6,5},{7,6},{9,8},{10,9},{11,10},{12... | collective-permute-start | bytes 1622024 | tf_op jit(solution)/shard_map/ppermute | solution.py:25
  95.3 0.8 copy-start
  106.2 29.3 %all-to-all-start = ((bf16[32,80,128]{2,1,0:T(8,128)(2,1)}), bf16[32,80,128]{2,1,0:T(8,128)(2,1)S(1)}, u32[]{:S(2)}, u32[]{:S(2)}) async-start(bf16[32,80,128]{2,1,0:T(8,128)(2,1)} %bitcast.28), calls=%async_computation | async-start | bytes 1310720 | tf_op jit(solution)/shard_map/all_to_all | solution.py:607

commit v5 on v2

--- a/solution.py
+++ b/solution.py
@@ -177,7 +177,7 @@
         for part in range(2):
             wide = echo_ref[part, channel].astype(F32)
             for column in range(columns):
-                wide_ref[side, part, column] = wide[:, column * LANES : (column + 1) * LANES]
+                wide_ref[side, part, column, :pulses] = wide[:, column * LANES : (column + 1) * LANES]
         for phase in range(ranks):
             here = pl.ds(phase, depth, stride=ranks)
             for part in range(2):
@@ -289,7 +289,7 @@
         + [anywhere] * len(before),
         out_specs=[whole] * len(outs) + ([anywhere] if tables else []),
         scratch_shapes=[
-            pltpu.VMEM((2, 2, width // LANES, pulses, LANES), F32),
+            pltpu.VMEM((2, 2, width // LANES, pulses + 8, LANES), F32),
             pltpu.VMEM((2, ranks, 2 * pulses // ranks, width), BF16),
             pltpu.VMEM((groups, channels * ranks, 16, width), BF16),
             pltpu.VMEM(weights.shape, BF16),
@@ -508,7 +508,7 @@
     rows = out_ref.shape[0]
     for beam, part in enumerate(parts):
         for side in range(2):
-            wide_ref[...] = part[:, side * LANES : (side + 1) * LANES].astype(F32)
+            wide_ref[: rows * 2] = part[:, side * LANES : (side + 1) * LANES].astype(F32)
             for half in range(2):
                 column = ((side * len(parts) + beam) * 2 + half) * LANES
                 out_ref[:, column : column + LANES] = wide_ref[pl.ds(half, rows, stride=2), :]
@@ -521,7 +521,7 @@
         out_shape=jax.ShapeDtypeStruct((rows, len(parts) * 4 * LANES), F32),
         in_specs=[whole] * len(parts),
         out_specs=whole,
-        scratch_shapes=[pltpu.VMEM((rows * 2, LANES), F32)],
+        scratch_shapes=[pltpu.VMEM((rows * 2 + 8, LANES), F32)],
         compiler_params=pltpu.CompilerParams(vmem_limit_bytes=32 * 2**20),
         cost_estimate=SMALL_COST,
         name="finished_tiles",

time: 160 us -> 160 us (level)
  no operation moved by 1% of the time
where the time goes in v5:
time: 160 us; the launch traced here: 159 us
  Pallas kernels  78.5 us (49%)
  starting transfers between devices  39.5 us (25%)
  blocking collectives  21.8 us (14%)
  waiting for transfers between devices  14.6 us (9%)
  local copies, waits for them, and re-layouts  2.82 us (2%)
  other arithmetic  2.05 us (1%)
    pallas_call x2, Pallas kernels, partial_beams(): pl.pallas_call(functools.partial(partial_beams_body, ranks, beams, edges,...  35.4 us
    pallas_call x3, Pallas kernels, beam_tiles(): pl.pallas_call(functools.partial(tiles_body, tracks, len(pieces)), grid=(...  28.2 us
    all_to_all x1, blocking collectives, local(): lax.all_to_all(tiles.reshape(owners, capacity * 2, 2 * LANES), ('pulse',...  21.8 us
    ppermute x7, starting transfers between devices, passed_along(): lax.ppermute(value, axis, [(source, source + steps) for source in range(l...  16.4 us
    all_to_all x1, starting transfers between devices, local(): lax.all_to_all(tiles.reshape(owners, capacity * 2, 2 * LANES), ('pulse',...  10.1 us
    ppermute x6, starting transfers between devices, exchanged(): lax.ppermute(value, 'pulse', [(rank, rank ^ slot) for rank in range(ranks)])  9.58 us
    all_to_all x1, waiting for transfers between devices, local(): lax.all_to_all(tiles.reshape(owners, capacity * 2, 2 * LANES), ('pulse',...  9.06 us
    pallas_call x2, Pallas kernels, summed_block(): pl.pallas_call(functools.partial(summed_body, len(terms), edges), grid=(b...  5.84 us
  transfers between devices with their start and end apart: 17, of which 7 were waited for; matrix products, arithmetic and copies ran while one was open for 2% of the time, Pallas kernels for 33%

profile of v5, /device:TPU:0, one launch (start us, length us, event | category | flops | bytes accessed | tf_op | source)
XLA Modules:
  0.0 159.4 jit_solution(7326356051974378853)
XLA Ops:
  0.0 0.7 fusion.3
  0.8 4.0 %collective-permute-start.3 = (s32[3,256]{1,0:T(4,128)S(1)}, s32[3,256]{1,0:T(4,128)S(1)}, u32[]{:S(2)}, u32[]{:S(2)}) collective-permute-start(s32[3,256]{1,0:T(4,128)S(1)} %pad_add_fusion.1), channel_id=1, source_target_pairs={{0,24},{8,16},{16,8},{24,0},{1,25},{9,17},{17,9},{25,1},{2,26},{10... | collective-permute-start | bytes 9224 | tf_op jit(solution)/shard_map/ppermute | solution.py:550
  4.7 0.1 collective-permute-start.2
  4.8 1.9 %collective-permute-start.1 = (f32[32,512]{1,0:T(8,128)}, f32[32,512]{1,0:T(8,128)S(1)}, u32[]{:S(2)}, u32[]{:S(2)}) collective-permute-start(f32[32,512]{1,0:T(8,128)} %bitcast.31), channel_id=1, source_target_pairs={{0,16},{8,24},{16,0},{24,8},{1,17},{9,25},{17,1},{25,9},{2,18},{10... | collective-permute-start | bytes 196616 | tf_op jit(solution)/shard_map/ppermute | solution.py:127
  6.7 1.5 collective-permute-start
  8.2 1.8 %toeplitz_taps.1.rest_8_.taps_ref = bf16[768,256]{1,0:T(8,128)(2,1)} custom-call(bf16[2,256]{1,0:T(2,128)(2,1)} %replica_ref.1), custom_call_target="tpu_custom_call" | custom-call | flops 1048576 | bytes 65536 | tf_op jit(solution)/shard_map/toeplitz_taps/pallas_call | solution.py:360
  10.0 0.6 copy.20.rest_9_.place_ref
  10.6 0.6 collective-permute-done.rest_2_
  11.2 0.0 copy-done.2
  11.2 0.0 copy-done.3
  11.2 0.6 copy-done.4
  11.8 20.7 %partial_beams.2 = (bf16[2,2,528,256]{3,2,1,0:T(8,128)(2,1)}, bf16[2,2,528,256]{3,2,1,0:T(8,128)(2,1)}, bf16[2,2,528,256]{3,2,1,0:T(8,128)(2,1)}, bf16[2,2,528,2...) custom-call(bf16[2,8,512,512]{3,2,1,0:T(8,128)(2,1)} %echo_ref.3, ...), custom_call_target="tpu_custom_call" | custom-call | flops 1048576 | bytes 65536 | tf_op jit(solution)/shard_map/partial_beams/pallas_call | solution.py:280
  32.5 1.6 collective-permute-start.11
  34.1 0.5 collective-permute-start.12
  34.6 1.3 collective-permute-start.4
  35.9 1.3 collective-permute-start.8
  37.2 0.6 copy-done.5
  37.8 14.7 %partial_beams.3 = (bf16[2,2,528,256]{3,2,1,0:T(8,128)(2,1)}, bf16[2,2,528,256]{3,2,1,0:T(8,128)(2,1)}, bf16[2,2,528,256]{3,2,1,0:T(8,128)(2,1)}, bf16[2,2,528,2...) custom-call(bf16[2,8,512,512]{3,2,1,0:T(8,128)(2,1)} %echo_ref.3, ...), custom_call_target="tpu_custom_call" | custom-call | flops 1048576 | bytes 65536 | tf_op jit(solution)/shard_map/partial_beams/pallas_call | solution.py:280
  52.5 0.5 collective-permute-start.5
  53.0 1.6 %collective-permute-start.6 = (bf16[2,2,528,256]{3,2,1,0:T(8,128)(2,1)}, bf16[2,2,528,256]{3,2,1,0:T(8,128)(2,1)}, u32[]{:S(2)}, u32[]{:S(2)}) collective-permute-start(bf16[2,2,528,256]{3,2,1,0:T(8,128)(2,1)} %get-tuple-element.24), channel_id=1, source_target_pairs={{0,16},{8,24},{16,0},{24,8},{1,17},{9,25},{17,1},{25,9},{2,18},{10... | collective-permute-start | bytes 3244040 | tf_op jit(solution)/shard_map/ppermute | solution.py:550
  54.6 2.8 %collective-permute-done.11.refs_1_ = bf16[2,2,528,256]{3,2,1,0:T(8,128)(2,1)} collective-permute-done((bf16[2,2,528,256]{3,2,1,0:T(8,128)(2,1)}, bf16[2,2,528,256]{3,2,1,0:T(8,128)(2,1)}, u32[]{:S(2)}, u32[]{:S(2)}) %collective-permute-start.11) | collective-permute-done | bytes 1081376 | tf_op jit(solution)/shard_map/ppermute | solution.py:550
  57.4 1.5 collective-permute-start.7
  59.0 1.3 collective-permute-start.9
  60.3 2.9 %summed_block.3.rest_1_ = bf16[2,2,528,256]{3,2,1,0:T(8,128)(2,1)} custom-call(bf16[2,2,528,256]{3,2,1,0:T(8,128)(2,1)} %get-tuple-element.30.refs_0_, bf16[2,2,528,256]{3,2,1,0:T(8,128)(2,1)} %collective-permute-done.11.refs_1_, bf16[2,2,528,256]{3,2,1,0:T(8,128)(2,1)} %collective-permute-done.12.refs_2_), custom_call_target="tpu_custom_call" | custom-call | flops 1048576 | bytes 65536 | tf_op jit(solution)/shard_map/summed_block/pallas_call | solution.py:324
  63.1 1.3 collective-permute-start.13
  64.4 0.5 collective-permute-done.9.rest_4_
  64.9 13.2 %beam_tiles.3.refs_3_ = bf16[2,512,256]{2,1,0:T(8,128)(2,1)} custom-call(s32[3,2,256]{2,1,0:T(2,128)} %copy.20.rest_9_.place_ref, f32[8,128]{1,0:T(8,128)} %copy-done.5, bf16[768,256]{1,0:T(8,128)(2,1)} %toeplitz_taps.1.rest_8_.taps_ref, bf16[128,256]{1,0:T(8,128)(2,1)} %constant.93.clone.repeat_ref, bf16[32,256]{1,0:T(8,128)(2,1)} %constant.92.clone.rest_7_.gather_ref, ...), custom_call_target="tpu_custom_call" | custom-call | flops 1048576 | bytes 65536 | tf_op jit(solution)/shard_map/beam_tiles/pallas_call | solution.py:480
  78.1 1.4 collective-permute-start.15
  79.5 0.1 collective-permute-done.5.refs_1_
  79.6 0.9 collective-permute-done.6.refs_2_
  80.5 3.0 %summed_block.2 = (bf16[2,2,528,256]{3,2,1,0:T(8,128)(2,1)}, bf16[2,1,528,256]{3,2,1,0:T(8,128)(2,1)}, bf16[2,1,528,256]{3,2,1,0:T(8,128)(2,1)}) custom-call(bf16[2,2,528,256]{3,2,1,0:T(8,128)(2,1)} %get-tuple-element.22.refs_0_, bf16[2,2,528,256]{3,2,1,0:T(8,128)(2,1)} %collective-permute-done.5.refs_1_, ...), custom_call_target="tpu_custom_call" | custom-call | flops 1048576 | bytes 65536 | tf_op jit(solution)/shard_map/summed_block/pallas_call | solution.py:324
  83.5 8.3 %collective-permute-start.10 = (bf16[2,1,528,256]{3,2,1,0:T(8,128)(2,1)}, bf16[2,1,528,256]{3,2,1,0:T(8,128)(2,1)S(1)}, u32[]{:S(2)}, u32[]{:S(2)}) collective-permute-start(bf16[2,1,528,256]{3,2,1,0:T(8,128)(2,1)} %get-tuple-element.29), channel_id=1, source_target_pairs={{0,1},{1,2},{2,3},{3,4},{4,5},{5,6},{6,7},{8,9},{9,10},{10,11},{11... | collective-permute-start | bytes 1622024 | tf_op jit(solution)/shard_map/ppermute | solution.py:25
  91.7 1.5 collective-permute-start.14
  93.2 0.6 broadcast_in_dim.2.place_ref
  93.8 0.6 reduce-window.6
  94.4 0.2 slice_reduce_fusion
  94.6 0.1 fusion.1
  94.7 0.6 add_add_fusion.slot_ref
  95.3 0.6 collective-permute-done.14.rest_4_
  95.9 0.2 copy-done
  96.2 7.5 %beam_tiles.4.rest_0_ = bf16[1,512,256]{2,1,0:T(8,128)(2,1)} custom-call(s32[3,1,256]{2,1,0:T(1,128)} %broadcast_in_dim.2.place_ref, f32[8,128]{1,0:T(8,128)} %copy-done.5, bf16[768,256]{1,0:T(8,128)(2,1)} %toeplitz_taps.1.rest_8_.taps_ref, bf16[128,256]{1,0:T(8,128)(2,1)} %constant.93.clone.repeat_ref, bf16[32,256]{1,0:T(8,128)(2,1)} %constant.92.clone.rest_7_.gather_ref, ...), custom_call_target="tpu_custom_call" | custom-call | flops 1048576 | bytes 65536 | tf_op jit(solution)/shard_map/beam_tiles/pallas_call | solution.py:480
  103.7 2.6 %slotted_tiles.2 = bf16[1280,256]{1,0:T(8,128)(2,1)} custom-call(s32[256]{0:T(256)} %add_add_fusion.slot_ref, bf16[1,512,256]{2,1,0:T(8,128)(2,1)} %beam_tiles.4.rest_0_, bf16[2,512,256]{2,1,0:T(8,128)(2,1)} %collective-permute-done.15.rest_1_), custom_call_target="tpu_custom_call" | custom-call | flops 1048576 | bytes 65536 | tf_op jit(solution)/shard_map/slotted_tiles/pallas_call | solution.py:443
  106.3 10.1 %all-to-all-start = ((bf16[32,40,256]{2,1,0:T(8,128)(2,1)}), bf16[32,40,256]{2,1,0:T(8,128)(2,1)S(1)}, u32[]{:S(2)}, u32[]{:S(2)}) async-start(bf16[32,40,256]{2,1,0:T(8,128)(2,1)} %bitcast.28), calls=%async_computation | async-start | bytes 1310720 | tf_op jit(solution)/shard_map/all_to_all | solution.py:607
  116.4 7.5 %beam_tiles.5.rest_0_ = bf16[1,512,256]{2,1,0:T(8,128)(2,1)} custom-call(s32[3,1,256]{2,1,0:T(1,128)} %broadcast_in_dim.2.place_ref, f32[8,128]{1,0:T(8,128)} %copy-done.5, bf16[768,256]{1,0:T(8,128)(2,1)} %toeplitz_taps.1.rest_8_.taps_ref, bf16[128,256]{1,0:T(8,128)(2,1)} %constant.93.clone.repeat_ref, bf16[32,256]{1,0:T(8,128)(2,1)} %constant.92.clone.rest_7_.gather_ref, ...), custom_call_target="tpu_custom_call" | custom-call | flops 1048576 | bytes 65536 | tf_op jit(solution)/shard_map/beam_tiles/pallas_call | solution.py:480
  123.9 2.6 %slotted_tiles.3 = bf16[1280,256]{1,0:T(8,128)(2,1)} custom-call(s32[256]{0:T(256)} %add_add_fusion.slot_ref, bf16[1,512,256]{2,1,0:T(8,128)(2,1)} %beam_tiles.5.rest_0_, bf16[2,512,256]{2,1,0:T(8,128)(2,1)} %collective-permute-done.15.rest_1_), custom_call_target="tpu_custom_call" | custom-call | flops 1048576 | bytes 65536 | tf_op jit(solution)/shard_map/slotted_tiles/pallas_call | solution.py:443
  126.5 9.1 %all-to-all-done = bf16[32,40,256]{2,1,0:T(8,128)(2,1)S(1)} async-done(((bf16[32,40,256]{2,1,0:T(8,128)(2,1)}), bf16[32,40,256]{2,1,0:T(8,128)(2,1)S(1)}, u32[]{:S(2)}, u32[]{:S(2)}) %all-to-all-start) | async-done | bytes 655392 | tf_op jit(solution)/shard_map/all_to_all | solution.py:607
  135.6 21.8 %all_to_all.10 = bf16[32,40,256]{2,1,0:T(8,128)(2,1)S(1)} all-to-all(bf16[32,40,256]{2,1,0:T(8,128)(2,1)} %bitcast.29), channel_id=1, replica_groups=mesh['pulse'=4,'gate'=8] {'pulse','gate'}, dimensions={0} | all-to-all | bytes 1310720 | tf_op jit(solution)/shard_map/all_to_all | solution.py:607
  157.3 2.0 %finished_tiles.1 = f32[640,1024]{1,0:T(8,128)} custom-call(bf16[1280,256]{1,0:T(8,128)(2,1)S(1)} %bitcast.26, bf16[1280,256]{1,0:T(8,128)(2,1)S(1)} %bitcast.27), custom_call_target="tpu_custom_call" | custom-call | flops 1048576 | bytes 65536 | tf_op jit(solution)/shard_map/finished_tiles/pallas_call | solution.py:519
  (25 shorter events, 0.1 us)
Async XLA Ops:
  0.8 9.2 %collective-permute-start.3 = (s32[3,256]{1,0:T(4,128)S(1)}, s32[3,256]{1,0:T(4,128)S(1)}, u32[]{:S(2)}, u32[]{:S(2)}) collective-permute-start(s32[3,256]{1,0:T(4,128)S(1)} %pad_add_fusion.1), channel_id=1, source_target_pairs={{0,24},{8,16},{16,8},{24,0},{1,25},{9,17},{17,9},{25,1},{2,26},{10... | collective-permute-start | bytes 9224 | tf_op jit(solution)/shard_map/ppermute | solution.py:550
  4.7 5.9 %collective-permute-start.2 = (f32[32,512]{1,0:T(8,128)}, f32[32,512]{1,0:T(8,128)S(1)}, u32[]{:S(2)}, u32[]{:S(2)}) collective-permute-start(f32[32,512]{1,0:T(8,128)} %bitcast.30), channel_id=1, source_target_pairs={{0,24},{8,16},{16,8},{24,0},{1,25},{9,17},{17,9},{25,1},{2,26},{10... | collective-permute-start | bytes 196616 | tf_op jit(solution)/shard_map/ppermute | solution.py:127
  4.8 5.8 %collective-permute-start.1 = (f32[32,512]{1,0:T(8,128)}, f32[32,512]{1,0:T(8,128)S(1)}, u32[]{:S(2)}, u32[]{:S(2)}) collective-permute-start(f32[32,512]{1,0:T(8,128)} %bitcast.31), channel_id=1, source_target_pairs={{0,16},{8,24},{16,0},{24,8},{1,17},{9,25},{17,1},{25,9},{2,18},{10... | collective-permute-start | bytes 196616 | tf_op jit(solution)/shard_map/ppermute | solution.py:127
  6.7 4.5 %collective-permute-start = (f32[32,512]{1,0:T(8,128)}, f32[32,512]{1,0:T(8,128)S(1)}, u32[]{:S(2)}, u32[]{:S(2)}) collective-permute-start(f32[32,512]{1,0:T(8,128)} %bitcast.32), channel_id=1, source_target_pairs={{0,8},{8,0},{16,24},{24,16},{1,9},{9,1},{17,25},{25,17},{2,10},{10... | collective-permute-start | bytes 196616 | tf_op jit(solution)/shard_map/ppermute | solution.py:127
  10.6 0.6 copy-start.2
  10.6 0.6 copy-start.3
  11.2 0.6 copy-start.4
  32.5 24.9 %collective-permute-start.11 = (bf16[2,2,528,256]{3,2,1,0:T(8,128)(2,1)}, bf16[2,2,528,256]{3,2,1,0:T(8,128)(2,1)}, u32[]{:S(2)}, u32[]{:S(2)}) collective-permute-start(bf16[2,2,528,256]{3,2,1,0:T(8,128)(2,1)} %get-tuple-element.31), channel_id=1, source_target_pairs={{0,8},{8,0},{16,24},{24,16},{1,9},{9,1},{17,25},{25,17},{2,10},{10... | collective-permute-start | bytes 3244040 | tf_op jit(solution)/shard_map/ppermute | solution.py:550
  34.1 24.9 %collective-permute-start.12 = (bf16[2,2,528,256]{3,2,1,0:T(8,128)(2,1)}, bf16[2,2,528,256]{3,2,1,0:T(8,128)(2,1)}, u32[]{:S(2)}, u32[]{:S(2)}) collective-permute-start(bf16[2,2,528,256]{3,2,1,0:T(8,128)(2,1)} %get-tuple-element.32), channel_id=1, source_target_pairs={{0,16},{8,24},{16,0},{24,8},{1,17},{9,25},{17,1},{25,9},{2,18},{10... | collective-permute-start | bytes 3244040 | tf_op jit(solution)/shard_map/ppermute | solution.py:550
  34.6 2.6 %collective-permute-start.4 = (f32[8,128]{1,0:T(8,128)}, f32[8,128]{1,0:T(8,128)S(1)}, u32[]{:S(2)}, u32[]{:S(2)}) collective-permute-start(f32[8,128]{1,0:T(8,128)} %get-tuple-element.20), channel_id=1, source_target_pairs={{0,1},{1,2},{2,3},{3,4},{4,5},{5,6},{6,7},{8,9},{9,10},{10,11},{11... | collective-permute-start | bytes 12296 | tf_op jit(solution)/shard_map/ppermute | solution.py:25
  35.9 29.0 %collective-permute-start.8 = (bf16[2,2,528,256]{3,2,1,0:T(8,128)(2,1)}, bf16[2,2,528,256]{3,2,1,0:T(8,128)(2,1)}, u32[]{:S(2)}, u32[]{:S(2)}) collective-permute-start(bf16[2,2,528,256]{3,2,1,0:T(8,128)(2,1)} %get-tuple-element.26.rest_1_), channel_id=1, source_target_pairs={{1,0},{2,1},{3,2},{4,3},{5,4},{6,5},{7,6},{9,8},{10,9},{11,10},{12... | collective-permute-start | bytes 3244040 | tf_op jit(solution)/shard_map/ppermute | solution.py:25
  37.2 0.6 copy-start.5
  52.5 27.1 %collective-permute-start.5 = (bf16[2,2,528,256]{3,2,1,0:T(8,128)(2,1)}, bf16[2,2,528,256]{3,2,1,0:T(8,128)(2,1)}, u32[]{:S(2)}, u32[]{:S(2)}) collective-permute-start(bf16[2,2,528,256]{3,2,1,0:T(8,128)(2,1)} %get-tuple-element.23), channel_id=1, source_target_pairs={{0,8},{8,0},{16,24},{24,16},{1,9},{9,1},{17,25},{25,17},{2,10},{10... | collective-permute-start | bytes 3244040 | tf_op jit(solution)/shard_map/ppermute | solution.py:550
  53.0 27.5 %collective-permute-start.6 = (bf16[2,2,528,256]{3,2,1,0:T(8,128)(2,1)}, bf16[2,2,528,256]{3,2,1,0:T(8,128)(2,1)}, u32[]{:S(2)}, u32[]{:S(2)}) collective-permute-start(bf16[2,2,528,256]{3,2,1,0:T(8,128)(2,1)} %get-tuple-element.24), channel_id=1, source_target_pairs={{0,16},{8,24},{16,0},{24,8},{1,17},{9,25},{17,1},{25,9},{2,18},{10... | collective-permute-start | bytes 3244040 | tf_op jit(solution)/shard_map/ppermute | solution.py:550
  57.4 5.7 %collective-permute-start.7 = (bf16[2,1,528,256]{3,2,1,0:T(8,128)(2,1)}, bf16[2,1,528,256]{3,2,1,0:T(8,128)(2,1)S(1)}, u32[]{:S(2)}, u32[]{:S(2)}) collective-permute-start(bf16[2,1,528,256]{3,2,1,0:T(8,128)(2,1)} %get-tuple-element.25), channel_id=1, source_target_pairs={{0,1},{1,2},{2,3},{3,4},{4,5},{5,6},{6,7},{8,9},{9,10},{10,11},{11... | collective-permute-start | bytes 1622024 | tf_op jit(solution)/shard_map/ppermute | solution.py:25
  59.0 5.9 %collective-permute-start.9 = (bf16[2,1,528,256]{3,2,1,0:T(8,128)(2,1)}, bf16[2,1,528,256]{3,2,1,0:T(8,128)(2,1)}, u32[]{:S(2)}, u32[]{:S(2)}) collective-permute-start(bf16[2,1,528,256]{3,2,1,0:T(8,128)(2,1)} %get-tuple-element.28), channel_id=1, source_target_pairs={{1,0},{2,1},{3,2},{4,3},{5,4},{6,5},{7,6},{9,8},{10,9},{11,10},{12... | collective-permute-start | bytes 1622024 | tf_op jit(solution)/shard_map/ppermute | solution.py:25
  63.1 1.8 %copy-start.1 = (bf16[2,1,528,256]{3,2,1,0:T(8,128)(2,1)}, bf16[2,1,528,256]{3,2,1,0:T(8,128)(2,1)S(1)}, u32[]{:S(2)}) copy-start(bf16[2,1,528,256]{3,2,1,0:T(8,128)(2,1)S(1)} %collective-permute-done.7.rest_0_) | copy-start | bytes 1622020
  63.1 32.8 %collective-permute-start.13 = (bf16[2,2,528,256]{3,2,1,0:T(8,128)(2,1)}, bf16[2,2,528,256]{3,2,1,0:T(8,128)(2,1)}, u32[]{:S(2)}, u32[]{:S(2)}) collective-permute-start(bf16[2,2,528,256]{3,2,1,0:T(8,128)(2,1)} %summed_block.3.rest_1_), channel_id=1, source_target_pairs={{1,0},{2,1},{3,2},{4,3},{5,4},{6,5},{7,6},{9,8},{10,9},{11,10},{12... | collective-permute-start | bytes 3244040 | tf_op jit(solution)/shard_map/ppermute | solution.py:25
  78.1 25.7 %collective-permute-start.15 = (bf16[2,512,256]{2,1,0:T(8,128)(2,1)}, bf16[2,512,256]{2,1,0:T(8,128)(2,1)}, u32[]{:S(2)}, u32[]{:S(2)}) collective-permute-start(bf16[2,512,256]{2,1,0:T(8,128)(2,1)} %beam_tiles.3.refs_3_), channel_id=1, source_target_pairs={{0,24},{8,16},{16,8},{24,0},{1,25},{9,17},{17,9},{25,1},{2,26},{10... | collective-permute-start | bytes 1572872 | tf_op jit(solution)/shard_map/ppermute | solution.py:550
  80.5 12.7 %copy-start.6 = (s32[256]{0:T(256)S(1)}, s32[256]{0:T(256)}, u32[]{:S(2)}) copy-start(s32[256]{0:T(256)} %param.21) | copy-start | bytes 3076
  83.5 11.9 %collective-permute-start.10 = (bf16[2,1,528,256]{3,2,1,0:T(8,128)(2,1)}, bf16[2,1,528,256]{3,2,1,0:T(8,128)(2,1)S(1)}, u32[]{:S(2)}, u32[]{:S(2)}) collective-permute-start(bf16[2,1,528,256]{3,2,1,0:T(8,128)(2,1)} %get-tuple-element.29), channel_id=1, source_target_pairs={{0,1},{1,2},{2,3},{3,4},{4,5},{5,6},{6,7},{8,9},{9,10},{10,11},{11... | collective-permute-start | bytes 1622024 | tf_op jit(solution)/shard_map/ppermute | solution.py:25
  91.7 4.2 %collective-permute-start.14 = (bf16[2,1,528,256]{3,2,1,0:T(8,128)(2,1)}, bf16[2,1,528,256]{3,2,1,0:T(8,128)(2,1)}, u32[]{:S(2)}, u32[]{:S(2)}) collective-permute-start(bf16[2,1,528,256]{3,2,1,0:T(8,128)(2,1)} %get-tuple-element.34), channel_id=1, source_target_pairs={{1,0},{2,1},{3,2},{4,3},{5,4},{6,5},{7,6},{9,8},{10,9},{11,10},{12... | collective-permute-start | bytes 1622024 | tf_op jit(solution)/shard_map/ppermute | solution.py:25
  95.3 0.8 copy-start
  106.3 29.3 %all-to-all-start = ((bf16[32,40,256]{2,1,0:T(8,128)(2,1)}), bf16[32,40,256]{2,1,0:T(8,128)(2,1)S(1)}, u32[]{:S(2)}, u32[]{:S(2)}) async-start(bf16[32,40,256]{2,1,0:T(8,128)(2,1)} %bitcast.28), calls=%async_computation | async-start | bytes 1310720 | tf_op jit(solution)/shard_map/all_to_all | solution.py:607
